TPU v7x, 32 devices: a whole 2x2x4 slice. The times are simulated.
32 devices in a mesh: section: 2 (over x), expert: 4 (over z), dp: 4 (over y, core).
Axes of the slice: x: 2, y: 2, z: 4, core: 2. Of those that a mesh axis runs over, the one named last changes fastest.
Arguments:
- frames: bfloat16 [4, 32, 48, 1280], P(None, ('expert', 'dp')), may hold values from -6 to 6
- norm_gain: float32 [2, 1280], P('section'), may hold values from 0.1 to 1.9
- router: bfloat16 [2, 1280, 4], P('section'), may hold values from -0.15625 to 0.15625
- w_in: bfloat16 [2, 4, 1280, 256], P('section', 'expert'), may hold values from -0.15625 to 0.15625
- w_out: bfloat16 [2, 4, 256, 1280], P('section', 'expert'), may hold values from -0.375 to 0.375
- routing: int32 [2, 4, 32, 48, 1], P('section', None, ('expert', 'dp')), may hold values from 0 to 3; in each aligned block of 96 rows (0 to 95, 96 to 191, ..., all dimensions but the last counted through in order) at most 27 rows name the same one
- head_gain: float32 [1280], replicated, may hold values from 0.1 to 1.9
- head_weight: bfloat16 [1280, 8000], P(None, 'expert'), may hold values from -6 to 6
- frame_lengths: int32 [4, 32], P(None, ('expert', 'dp')), may hold values from 24 to 48
- labels: int32 [4, 32, 12], P(None, ('expert', 'dp')), may hold values from 1 to 7999
- label_lengths: int32 [4, 32], P(None, ('expert', 'dp')), may hold values from 1 to 12
Outputs:
- losses: float32 [8, 16], P('section', ('expert', 'dp'))
- head_grad: bfloat16 [1280, 8000], P(None, 'expert')
Inputs may be any that keep to these rules, and one draw needn't show every extreme that they name: `routing`: in each layer and micro-batch, within the frames of one device (aligned blocks of 96 frames), no expert is named by more than 27 frames.
All inputs are finite; a program needn't handle non-finite values.
Results may differ from a plain program's by a relative error of at most 0.015.
Values may be sent and summed in bfloat16 or wider, within the bound.
No kernel may reach another device: no remote copies, remote signals or barrier semaphores. Data moves between devices by JAX's collectives and lax.ppermute only.
A program may use at most 64 MiB of HBM per device.

v0:
```python
import jax
import jax.numpy as jnp
import numpy as np
from jax import lax
from jax.experimental import pallas as pl
from jax.experimental.pallas import tpu as pltpu
from jax.sharding import Mesh, PartitionSpec as P

EPSILON = 1e-06
LOG_ZERO = -1e30
VMEM_LIMIT = 12 * 1024 * 1024
LARGE_LIMIT = 24 * 1024 * 1024
LANES = 128
COLS = 16
PEAK, TOTAL, WHOLE = COLS - 3, COLS - 2, COLS - 3
BLOCK_ROWS = 256
NT = (((1,), (1,)), ((), ()))
NN = (((1,), (0,)), ((), ()))


def round_up(value, unit):
    return -(-value // unit) * unit


def vmem_spec():
    return pl.BlockSpec(memory_space=pltpu.VMEM)


def smem_spec():
    return pl.BlockSpec(memory_space=pltpu.SMEM)


def call(kernel, out_shape, flops=0, limit=VMEM_LIMIT, **options):
    return pl.pallas_call(
        kernel,
        out_shape=out_shape,
        compiler_params=pltpu.CompilerParams(vmem_limit_bytes=limit),
        cost_estimate=pl.CostEstimate(flops=flops, bytes_accessed=0, transcendentals=0),
        **options,
    )


def bf16_rows(count, width):
    return jax.ShapeDtypeStruct((count, width), jnp.bfloat16)


def as_mask(values):
    return values.astype(jnp.float32).astype(jnp.bfloat16)


def split_rows(values, out_refs, spare=None, note=None):
    size, width = out_refs[0].shape
    for turn, out_ref in enumerate(out_refs):
        part = values[turn * size : (turn + 1) * size]
        if note is not None:
            row = lax.broadcasted_iota(jnp.int32, (size, width), 0)
            part = jnp.where(row == spare, note, part)
        out_ref[...] = part.astype(jnp.bfloat16)


def join_rows(refs):
    return jnp.concatenate([ref[...].astype(jnp.float32) for ref in refs], axis=0)


def rms_scale(values, gain):
    values = values.astype(jnp.float32)
    scale = lax.rsqrt(jnp.mean(values * values, axis=-1, keepdims=True) + EPSILON)
    return (values * scale * gain).astype(jnp.bfloat16)


def expert_column(ids, frame_count):
    pairs = ids.shape[0]
    square = jnp.concatenate(
        [ids.astype(jnp.float32), jnp.full((LANES - pairs, LANES), -1.0, jnp.float32)], axis=0
    )
    turned = jnp.transpose(square, (1, 0)).astype(jnp.int32)
    return jnp.concatenate([turned[:frame_count, p : p + 1] for p in range(pairs)], axis=0)


def placement(column, member, experts, capacity):
    count = column.shape[0]
    shifted = column - member
    relative = jnp.where(shifted < 0, shifted + experts, shifted)
    lane = lax.broadcasted_iota(jnp.int32, (count, LANES), 1)
    one_hot = (lane == relative).astype(jnp.float32)
    before = lax.broadcasted_iota(jnp.int32, (count, count), 1) <= lax.broadcasted_iota(
        jnp.int32, (count, count), 0
    )
    rank = lax.dot_general(
        as_mask(before), one_hot.astype(jnp.bfloat16), NN, preferred_element_type=jnp.float32
    )
    start = (lane * capacity - 1).astype(jnp.float32)
    slots = jnp.sum(one_hot * (rank + start), axis=1, keepdims=True).astype(jnp.int32)
    places = lax.broadcasted_iota(jnp.int32, (count, experts * capacity), 1)
    return (places == slots).astype(jnp.float32)


def scatter_rows(rows, ids, member, experts, capacity, frame_count, out_refs):
    count = rows.shape[0]
    chosen = placement(expert_column(ids, frame_count), member, experts, capacity)
    tall = round_up(count, LANES)
    if tall > count:
        chosen = jnp.concatenate(
            [chosen, jnp.zeros((tall - count, chosen.shape[1]), jnp.float32)], axis=0
        )
    pick = jnp.transpose(chosen, (1, 0))[:, :count].astype(jnp.bfloat16)
    placed = lax.dot_general(pick, rows, NN, preferred_element_type=jnp.float32)
    split_rows(placed, out_refs)


def combine_rows(rows, returned, ids, table, member, experts, capacity, frame_count):
    column = expert_column(ids, frame_count)
    pick = placement(column, member, experts, capacity).astype(jnp.bfloat16)
    normed = rms_scale(rows, table[:1])
    router = jnp.concatenate(
        [table[8:], jnp.zeros((LANES + 8 - table.shape[0], rows.shape[1]), jnp.float32)], axis=0
    ).astype(jnp.bfloat16)
    logits = lax.dot_general(normed, router, NT, preferred_element_type=jnp.float32)
    lane = lax.broadcasted_iota(jnp.int32, logits.shape, 1)
    gate = jax.nn.sigmoid(jnp.sum(jnp.where(lane == column, logits, 0.0), axis=1, keepdims=True))
    stacked = join_rows(returned).astype(jnp.bfloat16)
    mixed = lax.dot_general(pick, stacked, NN, preferred_element_type=jnp.float32)
    return (rows.astype(jnp.float32) + gate * mixed).astype(jnp.bfloat16)


def dispatch(rows, ids, member, experts, capacity, frame_count):
    width = rows.shape[1]

    def kernel(member_ref, rows_ref, ids_ref, *out_refs):
        scatter_rows(
            rows_ref[...], ids_ref[...], member_ref[0], experts, capacity, frame_count, out_refs
        )

    return call(
        kernel,
        tuple(bf16_rows(capacity, width) for _ in range(experts)),
        1 << 27,
        in_specs=[smem_spec()] + [vmem_spec()] * 2,
        out_specs=tuple(vmem_spec() for _ in range(experts)),
    )(member, rows, ids)


def pick_table(pick_ref, tables):
    if len(tables) == 1:
        return tables[0][...]
    return jnp.where(pick_ref[0] == 1, tables[0][...], tables[1][...])


def run_expert(received, tables, own, other, pick_own, spare, note):
    count = len(received)
    capacity, width = received[0].shape
    others, choices = len(other), len(tables)
    noted = [] if note is None else [note]

    def kernel(pick_ref, in_ref, out_weight_ref, *refs):
        table_refs, refs = refs[:choices], refs[choices:]
        other_refs, refs = refs[: 2 * others], refs[2 * others :]
        received_refs, refs = refs[:count], refs[count:]
        out_refs = refs[len(noted) :]

        def work(pieces):
            gain = pick_table(pick_ref, table_refs)[:1]
            normed = rms_scale(join_rows(received_refs), gain)
            total = None
            for weight_in, weight_out in pieces:
                hidden = lax.dot_general(
                    normed, weight_in[...], NN, preferred_element_type=jnp.float32
                )
                active = (hidden / (1.0 + jnp.exp(-hidden))).astype(jnp.bfloat16)
                part = lax.dot_general(
                    active, weight_out[...], NN, preferred_element_type=jnp.float32
                )
                total = part if total is None else total + part
            split_rows(total, out_refs, spare, refs[0][...] if noted else None)

        if others == 0:
            work([(in_ref, out_weight_ref)])
            return

        @pl.when(pick_ref[0] == 1)
        def _():
            work([(in_ref, out_weight_ref)])

        @pl.when(pick_ref[0] != 1)
        def _():
            work([(other_refs[2 * i], other_refs[2 * i + 1]) for i in range(others)])

    flat = [weight for pair in other for weight in pair]
    return call(
        kernel,
        tuple(bf16_rows(capacity, width) for _ in range(count)),
        4 * count * capacity * width * own[0].shape[1],
        in_specs=[smem_spec()] + [vmem_spec()] * (2 + choices + 2 * others + count + len(noted)),
        out_specs=tuple(vmem_spec() for _ in range(count)),
    )(pick_own, *own, *tables, *flat, *received, *noted)


def combine_and_dispatch(
    rows, returned, ids, tables, pick_own, next_ids, member, experts, capacity, frame_count
):
    width = rows.shape[1]
    choices = len(tables)

    def kernel(member_ref, pick_ref, rows_ref, ids_ref, next_ref, *refs):
        table_refs, refs = refs[:choices], refs[choices:]
        returned_refs, x_ref, out_refs = refs[:experts], refs[experts], refs[experts + 1 :]
        mixed = combine_rows(
            rows_ref[...],
            returned_refs,
            ids_ref[...],
            pick_table(pick_ref, table_refs),
            member_ref[0],
            experts,
            capacity,
            frame_count,
        )
        x_ref[...] = mixed
        scatter_rows(
            mixed, next_ref[...], member_ref[0], experts, capacity, frame_count, out_refs
        )

    shapes = (bf16_rows(*rows.shape),) + tuple(
        bf16_rows(capacity, width) for _ in range(experts)
    )
    result = call(
        kernel,
        shapes,
        1 << 28,
        in_specs=[smem_spec()] * 2 + [vmem_spec()] * (3 + choices + experts),
        out_specs=tuple(vmem_spec() for _ in shapes),
    )(member, pick_own, rows, ids, next_ids, *tables, *returned)
    return result[0], result[1:]


def combine_and_norm(
    rows, returned, ids, tables, pick_own, head_gain, member, experts, capacity, frame_count
):
    choices = len(tables)

    def kernel(member_ref, pick_ref, rows_ref, ids_ref, head_ref, *refs):
        table_refs, refs = refs[:choices], refs[choices:]
        final = combine_rows(
            rows_ref[...],
            refs[:experts],
            ids_ref[...],
            pick_table(pick_ref, table_refs),
            member_ref[0],
            experts,
            capacity,
            frame_count,
        )
        refs[experts][...] = rms_scale(final, head_ref[...])

    return call(
        kernel,
        bf16_rows(*rows.shape),
        1 << 28,
        in_specs=[smem_spec()] * 2 + [vmem_spec()] * (3 + choices + experts),
        out_specs=vmem_spec(),
    )(member, pick_own, rows, ids, head_gain, *tables, *returned)


def half_weights(core, weight_in, weight_out):
    width, hidden = weight_in.shape
    half = hidden // 2

    def kernel(core_ref, in_ref, out_ref, half_in, half_out, sems):
        start = pl.multiple_of(core_ref[0] * half, half)
        copies = (
            pltpu.make_async_copy(in_ref.at[:, pl.ds(start, half)], half_in, sems.at[0]),
            pltpu.make_async_copy(out_ref.at[pl.ds(start, half)], half_out, sems.at[1]),
        )
        for copy in copies:
            copy.start()
        for copy in copies:
            copy.wait()

    return call(
        kernel,
        (bf16_rows(width, half), bf16_rows(half, width)),
        1 << 20,
        in_specs=[smem_spec()] + [pl.BlockSpec(memory_space=pl.ANY)] * 2,
        out_specs=(vmem_spec(), vmem_spec()),
        scratch_shapes=[pltpu.SemaphoreType.DMA((2,))],
    )(core, weight_in, weight_out)


def block_list(shard):
    return [(i, min(BLOCK_ROWS, shard - i)) for i in range(0, shard, BLOCK_ROWS)]


def label_rows(weight, notes, member, pairs, spare, label_max, line):
    shard, width = weight.shape
    sources = len(notes)
    utterances = sources * pairs
    entries = utterances * COLS

    def kernel(member_ref, weight_ref, *refs):
        note_refs = refs[:sources]
        out_ref, places_ref, names_ref, turned_ref = refs[sources:]
        place = member_ref[0]
        found = []
        for ref in note_refs:
            row = ref[...].astype(jnp.float32)[spare : spare + 1]
            found.append((row[:, :LANES] * LANES + row[:, LANES : 2 * LANES]).astype(jnp.int32))
        if line:
            low = place < 2
            found = [
                found[0],
                jnp.where(low, found[1], found[3]),
                found[2],
                jnp.where(low, found[3], found[1]),
            ]
        names_ref[...] = jnp.zeros(names_ref.shape, jnp.int32)
        for slot in range(sources):
            for pair in range(pairs):
                row = slot * pairs + pair
                names_ref[row : row + 1, :COLS] = found[slot][:, pair * COLS : (pair + 1) * COLS]
        lane = lax.broadcasted_iota(jnp.int32, (utterances, LANES), 1)
        named = jnp.where(lane < label_max, names_ref[...], jnp.where(lane == label_max, 0, -1))
        local = named - place * shard
        local = jnp.where((named >= 0) & (local >= 0) & (local < shard), local, -1)
        square = jnp.concatenate(
            [
                local.astype(jnp.float32),
                jnp.full((LANES - utterances, LANES), -1.0, jnp.float32),
            ],
            axis=0,
        )
        turned = jnp.transpose(square, (1, 0))
        for utterance in range(utterances):
            turned_ref[utterance * COLS : (utterance + 1) * COLS] = jnp.broadcast_to(
                turned[:COLS, utterance : utterance + 1], (COLS, LANES)
            )
        places = turned_ref[:, :1].astype(jnp.int32)
        places_ref[...] = jnp.transpose(turned_ref[...], (1, 0))[:1].astype(jnp.int32)
        total = jnp.zeros((entries, width), jnp.float32)
        for first, size in block_list(shard):
            entry = first + lax.broadcasted_iota(jnp.int32, (entries, size), 1)
            total = total + lax.dot_general(
                as_mask(entry == places),
                weight_ref[first : first + size],
                NN,
                preferred_element_type=jnp.float32,
            )
        out_ref[...] = total.astype(jnp.bfloat16)

    return call(
        kernel,
        (
            bf16_rows(entries, width),
            jax.ShapeDtypeStruct((1, entries), jnp.int32),
            jax.ShapeDtypeStruct((utterances, LANES), jnp.int32),
        ),
        2 * shard * entries * width,
        LARGE_LIMIT,
        in_specs=[smem_spec()] + [vmem_spec()] * (1 + sources),
        out_specs=tuple(vmem_spec() for _ in range(3)),
        scratch_shapes=[pltpu.VMEM((entries, LANES), jnp.float32)],
    )(member, weight, *notes)


def head_logits(
    fill, first_slot, count, pieces, member, weight, label_weight, frame_count, earlier
):
    given = len(pieces)
    ahead = 0 if earlier is None else earlier.shape[0]
    span, width = pieces[0].shape
    row_count = count * span
    shard = weight.shape[0]
    height = round_up(shard, BLOCK_ROWS)
    entries = row_count // frame_count * COLS
    first_entry = first_slot * entries // count
    others = [] if earlier is None else [earlier]

    def kernel(member_ref, weight_ref, label_ref, *refs):
        piece_refs = refs[:given]
        logits_ref, rows_ref, stats_ref = refs[given + len(others) :]

        def put(slot, piece_ref):
            rows_ref[slot * span : (slot + 1) * span] = piece_ref[...]

        def put_if(condition, slot, piece_ref):
            @pl.when(condition)
            def _():
                put(slot, piece_ref)

        fill(member_ref[0], piece_refs, put, put_if)
        peak = jnp.full((1, row_count), LOG_ZERO, jnp.float32)
        total = jnp.zeros((1, row_count), jnp.float32)
        for first, size in block_list(shard):
            logits = lax.dot_general(
                weight_ref[first : first + size],
                rows_ref[...],
                NT,
                preferred_element_type=jnp.float32,
            )
            logits_ref[first : first + size] = logits
            before = peak
            peak = jnp.maximum(before, jnp.max(logits, axis=0, keepdims=True))
            total = total * jnp.exp(before - peak) + jnp.sum(
                jnp.exp(logits - peak), axis=0, keepdims=True
            )
        if height > shard:
            logits_ref[shard:] = jnp.full((height - shard, row_count), LOG_ZERO, jnp.float32)
        crossed = lax.dot_general(
            label_ref[first_entry : first_entry + entries],
            rows_ref[...],
            NT,
            preferred_element_type=jnp.float32,
        )
        owner = lax.broadcasted_iota(jnp.int32, (COLS, row_count), 1) // frame_count
        picked = jnp.zeros((COLS, row_count), jnp.float32)
        for utterance in range(entries // COLS):
            part = crossed[utterance * COLS : (utterance + 1) * COLS]
            picked = picked + jnp.where(owner == utterance, part, 0.0)
        place = lax.broadcasted_iota(jnp.int32, (COLS, row_count), 0)
        stats = jnp.where(place == PEAK, peak, picked)
        stats = jnp.where(place == TOTAL, total, stats)
        for slot in range(ahead):
            stats_ref[slot] = refs[given][slot]
        for slot in range(count):
            stats_ref[ahead + slot] = stats[:, slot * span : (slot + 1) * span]

    return call(
        kernel,
        (
            jax.ShapeDtypeStruct((height, row_count), jnp.float32),
            bf16_rows(row_count, width),
            jax.ShapeDtypeStruct((ahead + count, COLS, span), jnp.float32),
        ),
        2 * height * row_count * width,
        LARGE_LIMIT,
        in_specs=[smem_spec()] + [vmem_spec()] * (2 + given + len(others)),
        out_specs=tuple(vmem_spec() for _ in range(3)),
    )(member, weight, label_weight, *pieces, *others)


def fill_near(place, piece_refs, put, put_if):
    value_ref, left_ref, right_ref = piece_refs
    put(0, value_ref)
    put_if(place < 2, 1, left_ref)
    put_if(place >= 2, 1, right_ref)


def fill_far(place, piece_refs, put, put_if):
    left_far, right_far, left_end, right_end, left_ref, right_ref = piece_refs
    put_if(place < 2, 0, left_far)
    put_if(place >= 2, 0, right_far)
    put_if(place == 0, 1, left_end)
    put_if(place == 3, 1, right_end)
    put_if(place == 1, 1, right_ref)
    put_if(place == 2, 1, left_ref)


def fill_all(place, piece_refs, put, put_if):
    for slot, piece_ref in enumerate(piece_refs):
        put(slot, piece_ref)


def log_add(first, second):
    peak = jnp.maximum(first, second)
    return peak + jnp.log(jnp.exp(first - peak) + jnp.exp(second - peak))


def log_add3(first, second, third):
    peak = jnp.maximum(jnp.maximum(first, second), third)
    return peak + jnp.log(
        jnp.exp(first - peak) + jnp.exp(second - peak) + jnp.exp(third - peak)
    )


def ctc_pass(stats, slots, notes, frame_count, label_max, kept):
    sources = len(stats)
    count, _, span = stats[0].shape
    row_count = count * span
    utterances = notes.shape[0]
    entries = utterances * COLS
    tall = round_up(span, LANES)

    def kernel(slots_ref, notes_ref, *refs):
        (
            out_ref,
            high_ref,
            low_ref,
            loss_ref,
            turn_ref,
            emission_ref,
            emit_blank,
            emit_label,
            blank_fwd,
            label_fwd,
            blank_bwd,
            label_bwd,
            occupancy_ref,
        ) = refs[sources:]
        place = lax.broadcasted_iota(jnp.int32, (COLS, span), 0)
        turn_ref[...] = jnp.zeros(turn_ref.shape, jnp.float32)
        for slot in range(count):
            found = [refs[k][slots_ref[k * count + slot]] for k in range(sources)]
            joined = found[0]
            peak = found[0][PEAK : PEAK + 1]
            for other in found[1:]:
                joined = joined + other
                peak = jnp.maximum(peak, other[PEAK : PEAK + 1])
            total = jnp.zeros((1, span), jnp.float32)
            for other in found:
                total = total + other[TOTAL : TOTAL + 1] * jnp.exp(other[PEAK : PEAK + 1] - peak)
            log_total = peak + jnp.log(total)
            turn_ref[:COLS, :span] = jnp.where(place == TOTAL, log_total, joined - log_total)
            emission_ref[slot * span : (slot + 1) * span] = jnp.transpose(turn_ref[...], (1, 0))[
                :span
            ]

        lane = lax.broadcasted_iota(jnp.int32, (utterances, LANES), 1)
        is_label = lane < label_max
        is_blank = lane <= label_max
        names = jnp.where(is_label, notes_ref[...], 0)
        earlier = pltpu.roll(names, 1, 1)
        skip = is_label & (lane >= 1) & (names != 0) & (names != earlier)
        later = pltpu.roll(names, LANES - 1, 1)
        skip_next = (lane < label_max - 1) & (later != 0) & (later != names)
        frames = notes_ref[:, label_max : label_max + 1]
        counts = notes_ref[:, label_max + 1 : label_max + 2]
        ends_blank = jnp.where(lane == counts, 0.0, LOG_ZERO)
        ends_label = jnp.where(lane == counts - 1, 0.0, LOG_ZERO)

        def spread(step, carry):
            row = emission_ref[pl.ds(step, utterances, stride=frame_count), :]
            blank = jnp.sum(jnp.where(lane == label_max, row, 0.0), axis=1, keepdims=True)
            emit_blank[step] = jnp.where(is_blank, blank, LOG_ZERO)
            emit_label[step] = jnp.where(is_label, row, LOG_ZERO)
            return carry

        lax.fori_loop(0, frame_count, spread, 0, unroll=16)

        def advance(step, carry):
            fwd_blank, fwd_label, bwd_blank, bwd_label = carry
            moved = jnp.where(lane == 0, LOG_ZERO, pltpu.roll(fwd_label, 1, 1))
            new_blank = log_add(fwd_blank, moved) + emit_blank[step]
            new_label = (
                log_add3(fwd_label, fwd_blank, jnp.where(skip, moved, LOG_ZERO))
                + emit_label[step]
            )
            alive = step < frames
            fwd_blank = jnp.where(alive, new_blank, fwd_blank)
            fwd_label = jnp.where(alive, new_label, fwd_label)
            blank_fwd[step] = fwd_blank
            label_fwd[step] = fwd_label

            back = frame_count - 1 - step
            out_blank = bwd_blank + emit_blank[back + 1]
            out_label = bwd_label + emit_label[back + 1]
            next_blank = pltpu.roll(out_blank, LANES - 1, 1)
            next_label = jnp.where(skip_next, pltpu.roll(out_label, LANES - 1, 1), LOG_ZERO)
            ended = back >= frames - 1
            bwd_blank = jnp.where(ended, ends_blank, log_add(out_blank, out_label))
            bwd_label = jnp.where(
                ended, ends_label, log_add3(out_label, next_blank, next_label)
            )
            blank_bwd[back] = bwd_blank
            label_bwd[back] = bwd_label
            return (fwd_blank, fwd_label, bwd_blank, bwd_label)

        first_blank = jnp.where(lane == 0, emit_blank[0], LOG_ZERO)
        first_label = jnp.where(lane == 0, emit_label[0], LOG_ZERO)
        blank_fwd[0] = first_blank
        label_fwd[0] = first_label
        blank_bwd[frame_count - 1] = ends_blank
        label_bwd[frame_count - 1] = ends_label
        fwd_blank, fwd_label, _, _ = lax.fori_loop(
            1, frame_count, advance, (first_blank, first_label, ends_blank, ends_label), unroll=4
        )
        end_state = jnp.sum(jnp.where(lane == counts, fwd_blank, 0.0), axis=1, keepdims=True)
        near_state = jnp.sum(jnp.where(lane == counts - 1, fwd_label, 0.0), axis=1, keepdims=True)
        log_like = log_add(end_state, near_state)
        loss_ref[...] = -log_like[:kept]

        def occupy(step, carry):
            blank = jnp.exp(blank_fwd[step] + blank_bwd[step] - log_like)
            label = jnp.exp(label_fwd[step] + label_bwd[step] - log_like)
            blank = jnp.sum(jnp.where(is_blank, blank, 0.0), axis=1, keepdims=True)
            label = jnp.where(is_label, label, 0.0)
            whole = blank + jnp.sum(label, axis=1, keepdims=True)
            filled = jnp.where(lane == label_max, blank, label)
            filled = jnp.where(lane == WHOLE, whole, filled)
            filled = jnp.where(step < frames, -filled, 0.0)
            row = emission_ref[pl.ds(step, utterances, stride=frame_count), :]
            occupancy_ref[pl.ds(step, utterances, stride=frame_count), :] = jnp.where(
                lane == TOTAL, row, filled
            )
            return carry

        lax.fori_loop(0, frame_count, occupy, 0, unroll=16)
        turned = jnp.transpose(occupancy_ref[...], (1, 0))[:COLS]
        out_ref[...] = turned
        row_place = lax.broadcasted_iota(jnp.int32, (COLS, row_count), 0)
        owner = lax.broadcasted_iota(jnp.int32, (COLS, row_count), 1) // frame_count
        source = jnp.where(row_place < WHOLE, turned, 0.0)
        for utterance in range(utterances):
            part = jnp.where(owner == utterance, source, 0.0)
            high = part.astype(jnp.bfloat16)
            high_ref[utterance * COLS : (utterance + 1) * COLS] = high
            low_ref[utterance * COLS : (utterance + 1) * COLS] = (
                part - high.astype(jnp.float32)
            ).astype(jnp.bfloat16)

    held = pltpu.VMEM((frame_count, utterances, LANES), jnp.float32)
    table = pltpu.VMEM((row_count, LANES), jnp.float32)
    return call(
        kernel,
        (
            jax.ShapeDtypeStruct((COLS, row_count), jnp.float32),
            bf16_rows(entries, row_count),
            bf16_rows(entries, row_count),
            jax.ShapeDtypeStruct((kept, 1), jnp.float32),
        ),
        1 << 26,
        in_specs=[smem_spec()] + [vmem_spec()] * (1 + sources),
        out_specs=tuple(vmem_spec() for _ in range(4)),
        scratch_shapes=[pltpu.VMEM((LANES, tall), jnp.float32), table]
        + [held] * 6
        + [table],
    )(slots, notes, *stats)


def head_gradient(logits, rows, occupancy, high, low, places, order, outputs, each):
    count = len(logits)
    row_count, width = rows[0].shape
    entries = places.shape[1]
    blocks = outputs * each

    def kernel(order_ref, *refs):
        logits_refs, rows_refs = refs[:count], refs[count : 2 * count]
        occupancy_ref, high_ref, low_ref, places_ref = refs[2 * count : 2 * count + 4]
        out_refs = refs[2 * count + 4 :]
        for block in range(blocks):
            start = pl.multiple_of(order_ref[block] * BLOCK_ROWS, BLOCK_ROWS)
            entry = start + lax.broadcasted_iota(jnp.int32, (BLOCK_ROWS, entries), 0)
            select = as_mask(entry == places_ref[...])
            total = None
            for g in range(count):
                lanes = slice(g * row_count, (g + 1) * row_count)
                scattered = lax.dot_general(
                    select, high_ref[:, lanes], NN, preferred_element_type=jnp.float32
                ) + lax.dot_general(
                    select, low_ref[:, lanes], NN, preferred_element_type=jnp.float32
                )
                whole = occupancy_ref[WHOLE : WHOLE + 1, lanes]
                log_total = occupancy_ref[TOTAL : TOTAL + 1, lanes]
                values = logits_refs[g][pl.ds(start, BLOCK_ROWS), :]
                grad = (scattered - jnp.exp(values - log_total) * whole).astype(jnp.bfloat16)
                part = lax.dot_general(
                    grad, rows_refs[g][...], NN, preferred_element_type=jnp.float32
                )
                total = part if total is None else total + part
            out_refs[block // each][
                block % each * BLOCK_ROWS : (block % each + 1) * BLOCK_ROWS
            ] = total.astype(jnp.bfloat16)

    return call(
        kernel,
        tuple(bf16_rows(each * BLOCK_ROWS, width) for _ in range(outputs)),
        2 * blocks * BLOCK_ROWS * count * row_count * (width + 2 * entries),
        LARGE_LIMIT,
        in_specs=[smem_spec()] + [vmem_spec()] * (2 * count + 4),
        out_specs=tuple(vmem_spec() for _ in range(outputs)),
    )(order, *logits, *rows, occupancy, high, low, places)


def assemble(pieces, offsets, height, whole=None):
    count = len(pieces)
    part, width = pieces[0].shape
    short = height % part
    started = [] if whole is None else [whole]

    def kernel(offsets_ref, *refs):
        out_ref, sems = refs[count + len(started) :]

        def each(act):
            for index in range(count):
                offset = pl.multiple_of(offsets_ref[index], part)

                @pl.when(offset + part <= height)
                def _():
                    act(
                        pltpu.make_async_copy(
                            refs[index], out_ref.at[pl.ds(offset, part)], sems.at[index]
                        )
                    )

                if short:

                    @pl.when(offset + part > height)
                    def _():
                        act(
                            pltpu.make_async_copy(
                                refs[index].at[pl.ds(0, short)],
                                out_ref.at[pl.ds(height - short, short)],
                                sems.at[index],
                            )
                        )

        each(lambda copy: copy.start())
        each(lambda copy: copy.wait())

    anywhere = pl.BlockSpec(memory_space=pl.ANY)
    return call(
        kernel,
        bf16_rows(height, width),
        in_specs=[smem_spec()] + [vmem_spec()] * count + [anywhere] * len(started),
        out_specs=anywhere,
        scratch_shapes=[pltpu.SemaphoreType.DMA((count,))],
        input_output_aliases={} if whole is None else {1 + count: 0},
    )(offsets, *pieces, *started)


def swap(value, axis):
    return lax.ppermute(value, axis, [(0, 1), (1, 0)])


def rotate(value, axis, by):
    count = lax.axis_size(axis)
    return lax.ppermute(value, axis, [(i, (i + by) % count) for i in range(count)])


def after(value, *others):
    return lax.optimization_barrier((value,) + others)[0]


def line_near(value):
    left = lax.ppermute(value, "expert", [(1, 0), (2, 1), (3, 2)])
    right = lax.ppermute(value, "expert", [(0, 1), (1, 2), (2, 3)])
    return left, right


def line_far(left, right):
    return (
        lax.ppermute(left, "expert", [(1, 0), (2, 1)]),
        lax.ppermute(right, "expert", [(1, 2), (2, 3)]),
    )


def line_end(left_far, right_far):
    return (
        lax.ppermute(left_far, "expert", [(1, 0)]),
        lax.ppermute(right_far, "expert", [(2, 3)]),
    )


LINE_ORDER = np.array([[0, 1, 2, 3], [1, 2, 3, 0], [2, 1, 0, 3], [3, 2, 1, 0]])


def slot_orders(count):
    return LINE_ORDER if count == 4 else np.tile(np.arange(count), (count, 1))


def slot_tables(count):
    orders = slot_orders(count)
    tables = np.zeros((count, count, count), np.int32)
    for member in range(count):
        for k in range(count):
            source = (member + k) % count
            for slot in range(count):
                tables[member, k, slot] = list(orders[source]).index(orders[member][slot])
    return tables.reshape(count, count * count)


def wide(ref, start, size):
    return ref[pl.ds(start, size), :].astype(jnp.float32)


def sum_sent(own, came, places):
    height, width = own.shape
    part = height // 4

    def kernel(places_ref, own_ref, came_ref, *out_refs):
        section, outer = places_ref[0], places_ref[1]
        starts = (
            (1 - outer) * part,
            outer * part,
            (2 + 1 - section) * part,
            (2 + section) * part,
        )
        for start, out_ref in zip(starts, out_refs):
            start = pl.multiple_of(start, part)
            out_ref[...] = (wide(own_ref, start, part) + wide(came_ref, start, part)).astype(
                jnp.bfloat16
            )

    return call(
        kernel,
        tuple(bf16_rows(part, width) for _ in range(4)),
        1 << 20,
        in_specs=[smem_spec()] + [vmem_spec()] * 2,
        out_specs=tuple(vmem_spec() for _ in range(4)),
    )(places, own, came)


def sum_kept(own, came, arrived, places, keep):
    height, width = own.shape
    part = height // 4
    count = len(arrived) // 2

    def kernel(places_ref, own_ref, came_ref, *refs):
        section, outer = places_ref[0], places_ref[1]
        if not keep:
            section, outer = 1 - section, 1 - outer
        for side, start in enumerate((outer * part, (2 + section) * part)):
            start = pl.multiple_of(start, part)
            total = wide(own_ref, start, part) + wide(came_ref, start, part)
            for ref in refs[side * count : (side + 1) * count]:
                total = total + ref[...].astype(jnp.float32)
            refs[2 * count + side][...] = total.astype(jnp.bfloat16)

    return call(
        kernel,
        (bf16_rows(part, width), bf16_rows(part, width)),
        1 << 20,
        in_specs=[smem_spec()] + [vmem_spec()] * (2 + 2 * count),
        out_specs=(vmem_spec(), vmem_spec()),
    )(places, own, came, *arrived)


def per_device(
    frames,
    norm_gain,
    router,
    w_in,
    w_out,
    routing,
    head_gain,
    head_weight,
    frame_lengths,
    labels,
    label_lengths,
):
    sections = lax.axis_size("section")
    section_id = lax.axis_index("section")
    group_size = lax.axis_size("expert")
    member = lax.axis_index("expert")
    outer_size = lax.axis_size("dpo")
    inner_size = lax.axis_size("dpi")
    core = lax.axis_index("dpi")
    micro, utt_dev, frame_count, width = frames.shape
    label_max = labels.shape[2]
    experts = w_in.shape[1] * group_size
    pair_count = micro * utt_dev
    per_section = pair_count // sections
    first_pair = section_id * per_section
    share = (utt_dev * frame_count * 9 + 8 * experts - 1) // (8 * experts)
    filled = share * -(-per_section // utt_dev)
    capacity = round_up(filled + 1, 8)
    span = per_section * frame_count
    member_ref = member.astype(jnp.int32).reshape(1)

    def mine_of(value):
        return lax.dynamic_slice_in_dim(value, first_pair, per_section, 0)

    def exchange(blocks, sign):
        return [blocks[0]] + [
            rotate(blocks[k], "expert", sign * k) for k in range(1, group_size)
        ]

    def lanes_of(ids):
        return jnp.pad(mine_of(ids), ((0, 0), (0, LANES - frame_count)), constant_values=-1)

    current = lax.dynamic_slice_in_dim(
        frames.reshape(pair_count * frame_count, width), first_pair * frame_count, span, 0
    )
    own_ids = routing.reshape(pair_count, frame_count)
    paired = sections == 2 and inner_size == 2
    if paired:
        other_ids = swap(own_ids, "section")
        all_ids = [
            jnp.where(section_id == layer, own_ids, other_ids) for layer in range(sections)
        ]
    else:
        all_ids = lax.all_gather(own_ids, "section")
    layer_ids = [lanes_of(all_ids[layer]) for layer in range(sections)]
    own_table = jnp.concatenate(
        [
            norm_gain,
            jnp.zeros((7, width), jnp.float32),
            jnp.transpose(router[0]).astype(jnp.float32),
            jnp.zeros((round_up(experts, 8) - experts, width), jnp.float32),
        ],
        axis=0,
    )
    own = (w_in[0, 0], w_out[0, 0])
    layers = []
    if paired:
        other_table = swap(own_table, "section")
        sent_in, sent_out = half_weights(core.astype(jnp.int32).reshape(1), *own)
        came_in = swap(sent_in, "section")
        came_out = swap(sent_out, "section")
    else:
        all_tables = lax.all_gather(own_table, "section")
        all_in = lax.all_gather(own[0], "section")
        all_out = lax.all_gather(own[1], "section")
        for layer in range(sections):
            chosen = (all_in[layer], all_out[layer])
            layers.append(((all_tables[layer],), chosen, [], jnp.ones((1,), jnp.int32)))

    outgoing = dispatch(current, layer_ids[0], member_ref, experts, capacity, frame_count)
    received = exchange(outgoing, 1)
    if paired:
        (came_in, came_out), received = lax.optimization_barrier(((came_in, came_out), received))
        other = [(came_in, came_out), (swap(came_in, "dpi"), swap(came_out, "dpi"))]
        for layer in range(sections):
            mine = (section_id == layer).astype(jnp.int32).reshape(1)
            layers.append(((own_table, other_table), own, other, mine))

    labels, frame_lengths, label_lengths = lax.optimization_barrier(
        (labels, frame_lengths, label_lengths, outgoing[0])
    )[:3]
    notes = jnp.concatenate(
        [
            mine_of(labels.reshape(pair_count, label_max)),
            mine_of(frame_lengths.reshape(pair_count, 1)),
            mine_of(label_lengths.reshape(pair_count, 1)),
        ],
        axis=1,
    )
    notes = jnp.pad(notes, ((0, 0), (0, COLS - label_max - 2))).reshape(1, per_section * COLS)
    notes = jnp.pad(notes, ((0, 0), (0, LANES - per_section * COLS)))
    notes = jnp.concatenate([notes // LANES, notes % LANES], axis=1).astype(jnp.float32)
    notes = jnp.pad(notes, ((0, 0), (0, width - 2 * LANES)))
    shard = head_weight.shape[1]
    weight_rows = jnp.transpose(head_weight)
    line = group_size == 4
    tables = jnp.asarray(slot_tables(group_size))
    slots = lax.dynamic_index_in_dim(tables, member, 0, keepdims=False)
    outer = lax.axis_index("dpo")
    blocks = -(-shard // BLOCK_ROWS)
    tree = paired and outer_size == 2 and blocks == 8

    def pair_of(side, first, second):
        return [side * 4 + first, side * 4 + 2 + second]

    def offset_of(side, s, y):
        base = side * 4 * BLOCK_ROWS
        part = BLOCK_ROWS // 2
        return [
            base + s * BLOCK_ROWS + y * part,
            base + 2 * BLOCK_ROWS + y * BLOCK_ROWS + s * part,
        ]

    def whole_numbers(values):
        return jnp.stack([jnp.asarray(value, jnp.int32) for value in values])

    here, there = (section_id, outer), (1 - section_id, 1 - outer)
    sibling_order = whole_numbers(pair_of(1 - core, *there) + pair_of(1 - core, *here))
    sent_order = whole_numbers(pair_of(core, *there))
    kept_order = whole_numbers(pair_of(core, *here))
    chip_place = whole_numbers(here)
    first_offsets, last_offsets = [], offset_of(core, *there) + offset_of(1 - core, *there)
    for side in (core, 1 - core):
        for s, y in (here, (section_id, 1 - outer), (1 - section_id, outer)):
            first_offsets += offset_of(side, s, y)
    first_offsets, last_offsets = whole_numbers(first_offsets), whole_numbers(last_offsets)
    early = (
        notes,
        slots,
        head_gain.reshape(1, width),
        layer_ids[1:],
        sibling_order,
        sent_order,
        kept_order,
        chip_place,
        first_offsets,
        last_offsets,
    )
    early, received = lax.optimization_barrier((early, received))
    notes, slots, head_row, later_ids, sibling_order, sent_order = early[:6]
    kept_order, chip_place, first_offsets, last_offsets = early[6:]
    layer_ids = [layer_ids[0]] + list(later_ids)

    for layer in range(sections):
        choices, weights, others, pick_own = layers[layer]
        note = notes if layer == 0 else None
        done = run_expert(received, choices, weights, others, pick_own, filled, note)
        returned = exchange(done, -1)
        if layer == 0:
            found = returned
            if not line:
                stacked = jnp.stack(returned)
                found = [
                    lax.dynamic_index_in_dim(stacked, (k - member) % group_size, 0, keepdims=False)
                    for k in range(group_size)
                ]
        if layer < sections - 1:
            current, outgoing = combine_and_dispatch(
                current,
                returned,
                layer_ids[layer],
                choices,
                pick_own,
                layer_ids[layer + 1],
                member_ref,
                experts,
                capacity,
                frame_count,
            )
            received = exchange(outgoing, 1)
            if layer == 0:
                found = [after(found[0], current)] + list(found[1:])
                label_weight, places, names = label_rows(
                    weight_rows, found, member_ref, per_section, filled, label_max, line
                )
                received, label_weight = lax.optimization_barrier((received, label_weight))
        else:
            normed = combine_and_norm(
                current,
                returned,
                layer_ids[layer],
                choices,
                pick_own,
                head_row,
                member_ref,
                experts,
                capacity,
                frame_count,
            )

    def logits_of(fill, first, count, pieces, earlier):
        return head_logits(
            fill, first, count, pieces, member_ref, weight_rows, label_weight, frame_count, earlier
        )

    if line:
        left, right = line_near(normed)
        far = line_far(left, right)
        heads = [logits_of(fill_near, 0, 2, [normed, left, right], None)]
        far, heads[0] = lax.optimization_barrier((far, heads[0]))
        end = line_end(*far)
        heads.append(logits_of(fill_far, 2, 2, [*far, *end, left, right], heads[0][2]))
        stats = heads[1][2]
        found = [stats] + [rotate(stats, "expert", -k) for k in range(1, group_size)]
    else:
        gathered = lax.all_gather(normed, "expert")
        pieces = [gathered[k] for k in range(group_size)]
        heads = [logits_of(fill_all, 0, group_size, pieces, None)]
        gathered = lax.all_gather(heads[0][2], "expert")
        found = [
            lax.dynamic_index_in_dim(gathered, (member + k) % group_size, 0, keepdims=False)
            for k in range(group_size)
        ]
    kept_losses = per_section if line else group_size * per_section
    occupancy, high, low, losses = ctc_pass(
        found, slots, names, frame_count, label_max, kept_losses
    )
    if not line:
        losses = lax.dynamic_slice(losses, (member * per_section, 0), (per_section, 1))

    def gradient(order, outputs, each):
        return head_gradient(
            [head[0] for head in heads],
            [head[1] for head in heads],
            occupancy,
            high,
            low,
            places,
            order,
            outputs,
            each,
        )

    if tree:
        sibling_sent, sibling_kept = gradient(sibling_order, 2, 2)
        came_sent, came_kept = swap(sibling_sent, "dpi"), swap(sibling_kept, "dpi")
        own_sent = gradient(after(sent_order, sibling_sent), 1, 2)[0]
        a_far, a_near, b_far, b_near = sum_sent(own_sent, came_sent, chip_place)
        kept_order = after(kept_order, a_far)
        a_far, b_far = swap(a_far, "section"), swap(b_far, "dpo")
        a_near, b_near = swap(a_near, "section"), swap(b_near, "dpo")
        own_kept = gradient(kept_order, 1, 2)[0]
        a_on, b_on = sum_kept(own_kept, came_kept, [a_far, b_far], chip_place, False)
        a_in, b_in = swap(a_on, "dpo"), swap(b_on, "section")
        a, b = sum_kept(own_kept, came_kept, [a_near, a_in, b_near, b_in], chip_place, True)
        a_y, b_x = swap(a, "dpo"), swap(b, "section")
        b_y, a_x = swap(b, "dpo"), swap(a, "section")
        a_xy, b_xy = swap(a_y, "section"), swap(b_x, "dpo")
        a_y, b_y, a_x, b_x = lax.optimization_barrier((a_y, b_y, a_x, b_x))
        mine = [a, b, a_y, b_y, a_x, b_x]
        theirs = [swap(value, "dpi") for value in mine]
        whole = assemble(mine + theirs, first_offsets, shard)
        last = [a_xy, b_xy, swap(a_xy, "dpi"), swap(b_xy, "dpi")]
        whole = assemble(last, last_offsets, shard, whole)
    else:
        partial = gradient(jnp.arange(blocks, dtype=jnp.int32), 1, blocks)[0][:shard]
        whole = lax.psum(partial.astype(jnp.float32), ("section", "dpo", "dpi")).astype(
            jnp.bfloat16
        )
    return (losses, jnp.transpose(whole))


def solution(mesh):
    sections, group_size, spread = (mesh.shape[name] for name in ("section", "expert", "dp"))
    inner = 2 if spread % 2 == 0 else 1
    split = Mesh(
        mesh.devices.reshape(sections, group_size, spread // inner, inner),
        ("section", "expert", "dpo", "dpi"),
    )
    block = ("expert", "dpo", "dpi")
    placed = (
        P(None, block, None, None),
        P("section", None),
        P("section", None, None),
        P("section", "expert", None, None),
        P("section", "expert", None, None),
        P("section", None, block, None, None),
        P(),
        P(None, "expert"),
        P(None, block),
        P(None, block, None),
        P(None, block),
    )
    return jax.shard_map(
        per_device,
        mesh=split,
        in_specs=placed,
        out_specs=(P("section", block), P(None, "expert")),
        check_vma=False,
    )
```

profile of v0, /device:TPU:0, one launch (start us, length us, event | category | flops | bytes accessed | tf_op | source)
XLA Modules:
  0.0 219.1 jit_solution(8964889599100946687)
XLA Ops:
  0.7 3.0 %collective-permute-start = (s32[8,48]{1,0:T(8,128)}, s32[8,48]{1,0:T(8,128)S(1)}, u32[]{:S(2)}, u32[]{:S(2)}) collective-permute-start(s32[8,48]{1,0:T(8,128)} %bitcast.55), channel_id=1, source_target_pairs={{0,16},{16,0},{1,17},{17,1},{2,18},{18,2},{3,19},{19,3},{4,20},{20... | collective-permute-start | bytes 4616 | tf_op jit(solution)/shard_map/ppermute | solution.py:719
  14.3 2.6 %collective-permute-start.4 = (bf16[56,1280]{1,0:T(8,128)(2,1)}, bf16[56,1280]{1,0:T(8,128)(2,1)}, u32[]{:S(2)}, u32[]{:S(2)}) collective-permute-start(bf16[56,1280]{1,0:T(8,128)(2,1)} %get-tuple-element.91), channel_id=1, source_target_pairs={{0,8},{4,12},{8,0},{12,4},{1,9},{5,13},{9,1},{13,5},{2,10},{6,14},... | collective-permute-start | bytes 430088 | tf_op jit(solution)/shard_map/ppermute | solution.py:724
  18.8 2.8 %collective-permute-done.3.refs_7_ = bf16[56,1280]{1,0:T(8,128)(2,1)S(1)} collective-permute-done((bf16[56,1280]{1,0:T(8,128)(2,1)}, bf16[56,1280]{1,0:T(8,128)(2,1)S(1)}, u32[]{:S(2)}, u32[]{:S(2)}) %collective-permute-start.3) | collective-permute-done | bytes 143392 | tf_op jit(solution)/shard_map/ppermute | solution.py:724
  22.5 3.3 %collective-permute-done.4.refs_8_ = bf16[56,1280]{1,0:T(8,128)(2,1)} collective-permute-done((bf16[56,1280]{1,0:T(8,128)(2,1)}, bf16[56,1280]{1,0:T(8,128)(2,1)}, u32[]{:S(2)}, u32[]{:S(2)}) %collective-permute-start.4) | collective-permute-done | bytes 143392 | tf_op jit(solution)/shard_map/ppermute | solution.py:724
  32.2 4.9 %collective-permute-start.10 = (bf16[56,1280]{1,0:T(8,128)(2,1)S(1)}, bf16[56,1280]{1,0:T(8,128)(2,1)S(1)}, u32[]{:S(2)}, u32[]{:S(2)}) collective-permute-start(bf16[56,1280]{1,0:T(8,128)(2,1)S(1)} %get-tuple-element.108), channel_id=1, source_target_pairs={{0,8},{4,12},{8,0},{12,4},{1,9},{5,13},{9,1},{13,5},{2,10},{6,14},... | collective-permute-start | bytes 430088 | tf_op jit(solution)/shard_map/ppermute | solution.py:724
  37.4 3.5 %collective-permute-start.9 = (bf16[56,1280]{1,0:T(8,128)(2,1)S(1)}, bf16[56,1280]{1,0:T(8,128)(2,1)S(1)}, u32[]{:S(2)}, u32[]{:S(2)}) collective-permute-start(bf16[56,1280]{1,0:T(8,128)(2,1)S(1)} %get-tuple-element.107), channel_id=1, source_target_pairs={{0,12},{4,0},{8,4},{12,8},{1,13},{5,1},{9,5},{13,9},{2,14},{6,2},{... | collective-permute-start | bytes 430088 | tf_op jit(solution)/shard_map/ppermute | solution.py:724
  40.9 6.7 %collective-permute-done.10.refs_4_.refs_2_ = bf16[56,1280]{1,0:T(8,128)(2,1)S(1)} collective-permute-done((bf16[56,1280]{1,0:T(8,128)(2,1)S(1)}, bf16[56,1280]{1,0:T(8,128)(2,1)S(1)}, u32[]{:S(2)}, u32[]{:S(2)}) %collective-permute-start.10) | collective-permute-done | bytes 143392 | tf_op jit(solution)/shard_map/ppermute | solution.py:724
  55.0 2.9 %collective-permute-start.14 = (bf16[56,1280]{1,0:T(8,128)(2,1)}, bf16[56,1280]{1,0:T(8,128)(2,1)}, u32[]{:S(2)}, u32[]{:S(2)}) collective-permute-start(bf16[56,1280]{1,0:T(8,128)(2,1)} %get-tuple-element.116), channel_id=1, source_target_pairs={{0,12},{4,0},{8,4},{12,8},{1,13},{5,1},{9,5},{13,9},{2,14},{6,2},{... | collective-permute-start | bytes 430088 | tf_op jit(solution)/shard_map/ppermute | solution.py:724
  57.9 2.4 %copy-done.1 = bf16[1280,2000]{0,1:T(8,128)(2,1)S(1)} copy-done((bf16[1280,2000]{0,1:T(8,128)(2,1)S(1)}, bf16[1280,2000]{0,1:T(8,128)(2,1)}, u32[]{:S(2)}) %copy-start.1) | copy-done | bytes 5120024
  67.4 6.1 %collective-permute-start.15 = (bf16[56,1280]{1,0:T(8,128)(2,1)S(1)}, bf16[56,1280]{1,0:T(8,128)(2,1)S(1)}, u32[]{:S(2)}, u32[]{:S(2)}) collective-permute-start(bf16[56,1280]{1,0:T(8,128)(2,1)S(1)} %get-tuple-element.125), channel_id=1, source_target_pairs={{0,12},{4,0},{8,4},{12,8},{1,13},{5,1},{9,5},{13,9},{2,14},{6,2},{... | collective-permute-start | bytes 430088 | tf_op jit(solution)/shard_map/ppermute | solution.py:724
  74.1 3.6 %collective-permute-done.15.refs_3_ = bf16[56,1280]{1,0:T(8,128)(2,1)S(1)} collective-permute-done((bf16[56,1280]{1,0:T(8,128)(2,1)S(1)}, bf16[56,1280]{1,0:T(8,128)(2,1)S(1)}, u32[]{:S(2)}, u32[]{:S(2)}) %collective-permute-start.15) | collective-permute-done | bytes 143392 | tf_op jit(solution)/shard_map/ppermute | solution.py:724
  77.7 7.0 %collective-permute-done.16.refs_4_ = bf16[56,1280]{1,0:T(8,128)(2,1)S(1)} collective-permute-done((bf16[56,1280]{1,0:T(8,128)(2,1)S(1)}, bf16[56,1280]{1,0:T(8,128)(2,1)S(1)}, u32[]{:S(2)}, u32[]{:S(2)}) %collective-permute-start.16) | collective-permute-done | bytes 143392 | tf_op jit(solution)/shard_map/ppermute | solution.py:724
  87.0 4.6 %collective-permute-start.20 = (bf16[192,1280]{1,0:T(8,128)(2,1)S(1)}, bf16[192,1280]{1,0:T(8,128)(2,1)S(1)}, u32[]{:S(2)}, u32[]{:S(2)}) collective-permute-start(bf16[192,1280]{1,0:T(8,128)(2,1)S(1)} %shard_map.137.refs_0_), channel_id=1, source_target_pairs={{0,4},{4,8},{8,12},{1,5},{5,9},{9,13},{2,6},{6,10},{10,14},{3,7},{... | collective-permute-start | bytes 1474568 | tf_op jit(solution)/shard_map/ppermute | solution.py:733
  91.6 8.2 %collective-permute-done.18.refs_1_.refs_4_ = bf16[192,1280]{1,0:T(8,128)(2,1)S(1)} collective-permute-done((bf16[192,1280]{1,0:T(8,128)(2,1)S(1)}, bf16[192,1280]{1,0:T(8,128)(2,1)S(1)}, u32[]{:S(2)}, u32[]{:S(2)}) %collective-permute-start.18) | collective-permute-done | bytes 491552 | tf_op jit(solution)/shard_map/ppermute | solution.py:732
  101.8 2.4 %copy-done.2 = bf16[1280,2000]{0,1:T(8,128)(2,1)S(1)} copy-done((bf16[1280,2000]{0,1:T(8,128)(2,1)S(1)}, bf16[1280,2000]{0,1:T(8,128)(2,1)}, u32[]{:S(2)}) %copy-start.2) | copy-done | bytes 5120024
  104.2 3.4 %shard_map.138 = (f32[2048,384]{1,0:T(8,128)S(1)}, bf16[384,1280]{1,0:T(8,128)(2,1)S(1)}, f32[2,16,192]{2,1,0:T(8,128)S(1)}) custom-call(s32[1]{0:T(128)} %bitcast.member_ref, bf16[2000,1280]{1,0:T(8,128)(2,1)S(1)} %bitcast.46, bf16[256,1280]{1,0:T(8,128)(2,1)S(1)} %get-tuple-element.118.label_ref, bf16[192,1280]{1,0:T(8,128)(2,1)S(1)} %shard_map.137.refs_0_, ...), custom_call_target="tpu_custom_call" | custom-call | flops 2013265920 | tf_op jit(solution)/shard_map/pallas_call | solution.py:425
  107.6 5.8 %collective-permute-done.19.refs_0_ = bf16[192,1280]{1,0:T(8,128)(2,1)S(1)} collective-permute-done((bf16[192,1280]{1,0:T(8,128)(2,1)S(1)}, bf16[192,1280]{1,0:T(8,128)(2,1)S(1)}, u32[]{:S(2)}, u32[]{:S(2)}) %collective-permute-start.19) | collective-permute-done | bytes 491552 | tf_op jit(solution)/shard_map/ppermute | solution.py:739
  115.4 10.9 %collective-permute-done.22.refs_2_ = bf16[192,1280]{1,0:T(8,128)(2,1)S(1)} collective-permute-done((bf16[192,1280]{1,0:T(8,128)(2,1)S(1)}, bf16[192,1280]{1,0:T(8,128)(2,1)S(1)}, u32[]{:S(2)}, u32[]{:S(2)}) %collective-permute-start.22) | collective-permute-done | bytes 491552 | tf_op jit(solution)/shard_map/ppermute | solution.py:746
  126.3 3.3 %shard_map.139 = (f32[2048,384]{1,0:T(8,128)S(1)}, bf16[384,1280]{1,0:T(8,128)(2,1)S(1)}, f32[4,16,192]{2,1,0:T(8,128)S(1)}) custom-call(s32[1]{0:T(128)} %bitcast.member_ref, bf16[2000,1280]{1,0:T(8,128)(2,1)S(1)} %bitcast.47, bf16[256,1280]{1,0:T(8,128)(2,1)S(1)} %get-tuple-element.118.label_ref, bf16[192,1280]{1,0:T(8,128)(2,1)S(1)} %collective-permute-done.19.refs_0_, ...), custom_call_target="tpu_custom_call" | custom-call | flops 2013265920 | tf_op jit(solution)/shard_map/pallas_call | solution.py:425
  129.6 5.3 %collective-permute-start.24 = (f32[4,16,192]{2,1,0:T(8,128)S(1)}, f32[4,16,192]{2,1,0:T(8,128)S(1)}, u32[]{:S(2)}, u32[]{:S(2)}) collective-permute-start(f32[4,16,192]{2,1,0:T(8,128)S(1)} %get-tuple-element.134.refs_0_), channel_id=1, source_target_pairs={{0,12},{4,0},{8,4},{12,8},{1,13},{5,1},{9,5},{13,9},{2,14},{6,2},{... | collective-permute-start | bytes 147464 | tf_op jit(solution)/shard_map/ppermute | solution.py:724
  136.8 3.3 %collective-permute-done.25.refs_2_ = f32[4,16,192]{2,1,0:T(8,128)S(1)} collective-permute-done((f32[4,16,192]{2,1,0:T(8,128)S(1)}, f32[4,16,192]{2,1,0:T(8,128)S(1)}, u32[]{:S(2)}, u32[]{:S(2)}) %collective-permute-start.25) | collective-permute-done | bytes 49184 | tf_op jit(solution)/shard_map/ppermute | solution.py:724
  141.0 6.6 %shard_map.140 = (f32[16,768]{1,0:T(8,128)S(1)}, bf16[256,768]{1,0:T(8,128)(2,1)S(1)}, bf16[256,768]{1,0:T(8,128)(2,1)S(1)}, f32[4,1]{1,0:T(4,128)S(1)}) custom-call(s32[16]{0:T(128)S(1)} %fusion.slots_ref, s32[16,128]{1,0:T(8,128)S(1)} %get-tuple-element.112.notes_ref, f32[4,16,192]{2,1,0:T(8,128)S(1)} %get-tuple-element.134.refs_0_, ...), custom_call_target="tpu_custom_call" | custom-call | flops 67108864 | tf_op jit(solution)/shard_map/pallas_call | solution.py:610
  147.6 5.0 %shard_map.141 = (bf16[512,1280]{1,0:T(8,128)(2,1)S(1)}, bf16[512,1280]{1,0:T(8,128)(2,1)S(1)}) custom-call(s32[4]{0:T(128)S(1)} %get-tuple-element.140.order_ref, f32[2048,384]{1,0:T(8,128)S(1)} %get-tuple-element.141.refs_0_, f32[2048,384]{1,0:T(8,128)S(1)} %get-tuple-element.142.refs_1_, bf16[384,1280]{1,0:T(8,128)(2,1)S(1)} %get-tuple-element.143.refs_2_, ...), custom_call_target="tpu_custom_call" | custom-call | flops 2818572288 | tf_op jit(solution)/shard_map/pallas_call | solution.py:661
  153.1 2.9 %shard_map.142.own_ref = bf16[512,1280]{1,0:T(8,128)(2,1)S(1)} custom-call(s32[2]{0:T(128)S(1)} %get-tuple-element.150.order_ref, f32[2048,384]{1,0:T(8,128)S(1)} %get-tuple-element.141.refs_0_, f32[2048,384]{1,0:T(8,128)S(1)} %get-tuple-element.142.refs_1_, bf16[384,1280]{1,0:T(8,128)(2,1)S(1)} %get-tuple-element.143.refs_2_, ...), custom_call_target="tpu_custom_call" | custom-call | flops 1409286144 | tf_op jit(solution)/shard_map/pallas_call | solution.py:661
  161.0 2.8 %shard_map.144.own_ref = bf16[512,1280]{1,0:T(8,128)(2,1)S(1)} custom-call(s32[2]{0:T(128)S(1)} %get-tuple-element.152.order_ref, f32[2048,384]{1,0:T(8,128)S(1)} %get-tuple-element.141.refs_0_, f32[2048,384]{1,0:T(8,128)S(1)} %get-tuple-element.142.refs_1_, bf16[384,1280]{1,0:T(8,128)(2,1)S(1)} %get-tuple-element.143.refs_2_, ...), custom_call_target="tpu_custom_call" | custom-call | flops 1409286144 | tf_op jit(solution)/shard_map/pallas_call | solution.py:661
  163.8 3.6 %collective-permute-done.30.refs_0_ = bf16[128,1280]{1,0:T(8,128)(2,1)S(1)} collective-permute-done((bf16[128,1280]{1,0:T(8,128)(2,1)S(1)}, bf16[128,1280]{1,0:T(8,128)(2,1)S(1)}, u32[]{:S(2)}, u32[]{:S(2)}) %collective-permute-start.30) | collective-permute-done | bytes 327712 | tf_op jit(solution)/shard_map/ppermute | solution.py:719
  171.9 2.6 %collective-permute-done.29.refs_0_ = bf16[128,1280]{1,0:T(8,128)(2,1)S(1)} collective-permute-done((bf16[128,1280]{1,0:T(8,128)(2,1)S(1)}, bf16[128,1280]{1,0:T(8,128)(2,1)S(1)}, u32[]{:S(2)}, u32[]{:S(2)}) %collective-permute-start.29) | collective-permute-done | bytes 327712 | tf_op jit(solution)/shard_map/ppermute | solution.py:719
  174.6 6.1 %collective-permute-done.32.refs_1_ = bf16[128,1280]{1,0:T(8,128)(2,1)S(1)} collective-permute-done((bf16[128,1280]{1,0:T(8,128)(2,1)S(1)}, bf16[128,1280]{1,0:T(8,128)(2,1)S(1)}, u32[]{:S(2)}, u32[]{:S(2)}) %collective-permute-start.32) | collective-permute-done | bytes 327712 | tf_op jit(solution)/shard_map/ppermute | solution.py:719
  185.7 6.6 %collective-permute-done.35.refs_2_ = bf16[128,1280]{1,0:T(8,128)(2,1)S(1)} collective-permute-done((bf16[128,1280]{1,0:T(8,128)(2,1)S(1)}, bf16[128,1280]{1,0:T(8,128)(2,1)S(1)}, u32[]{:S(2)}, u32[]{:S(2)}) %collective-permute-start.35) | collective-permute-done | bytes 327712 | tf_op jit(solution)/shard_map/ppermute | solution.py:719
  193.9 3.7 %collective-permute-done.41.refs_3_ = bf16[128,1280]{1,0:T(8,128)(2,1)} collective-permute-done((bf16[128,1280]{1,0:T(8,128)(2,1)S(1)}, bf16[128,1280]{1,0:T(8,128)(2,1)}, u32[]{:S(2)}, u32[]{:S(2)}) %collective-permute-start.41) | collective-permute-done | bytes 327712 | tf_op jit(solution)/shard_map/ppermute | solution.py:719
  203.4 5.5 %collective-permute-done.36.refs_0_ = bf16[128,1280]{1,0:T(8,128)(2,1)S(1)} collective-permute-done((bf16[128,1280]{1,0:T(8,128)(2,1)S(1)}, bf16[128,1280]{1,0:T(8,128)(2,1)S(1)}, u32[]{:S(2)}, u32[]{:S(2)}) %collective-permute-start.36) | collective-permute-done | bytes 327712 | tf_op jit(solution)/shard_map/ppermute | solution.py:719
  213.8 3.5 %shard_map.147.refs_4_ = bf16[2000,1280]{1,0:T(8,128)(2,1)} custom-call(s32[12]{0:T(128)S(1)} %stack.122.offsets_ref, bf16[128,1280]{1,0:T(8,128)(2,1)S(1)} %get-tuple-element.159.refs_0_, bf16[128,1280]{1,0:T(8,128)(2,1)S(1)} %get-tuple-element.160.refs_1_, bf16[128,1280]{1,0:T(8,128)(2,1)S(1)} %collective-permute-done.35.refs_2_, ...), custom_call_target="tpu_custom_call" | custom-call | tf_op jit(solution)/shard_map/pallas_call | solution.py:708
  (192 shorter events, 73.0 us)
Async XLA Ops:
  7.0 18.9 %collective-permute-start.1 = (bf16[1280,128]{1,0:T(8,128)(2,1)}, bf16[1280,128]{1,0:T(8,128)(2,1)S(1)}, u32[]{:S(2)}, u32[]{:S(2)}) collective-permute-start(bf16[1280,128]{1,0:T(8,128)(2,1)} %get-tuple-element.88), channel_id=1, source_target_pairs={{0,16},{16,0},{1,17},{17,1},{2,18},{18,2},{3,19},{19,3},{4,20},{20... | collective-permute-start | bytes 983048 | tf_op jit(solution)/shard_map/ppermute | solution.py:719
  7.1 18.7 %collective-permute-start.2 = (bf16[128,1280]{1,0:T(8,128)(2,1)}, bf16[128,1280]{1,0:T(8,128)(2,1)}, u32[]{:S(2)}, u32[]{:S(2)}) collective-permute-start(bf16[128,1280]{1,0:T(8,128)(2,1)} %get-tuple-element.89), channel_id=1, source_target_pairs={{0,16},{16,0},{1,17},{17,1},{2,18},{18,2},{3,19},{19,3},{4,20},{20... | collective-permute-start | bytes 983048 | tf_op jit(solution)/shard_map/ppermute | solution.py:719
  14.3 11.5 %collective-permute-start.4 = (bf16[56,1280]{1,0:T(8,128)(2,1)}, bf16[56,1280]{1,0:T(8,128)(2,1)}, u32[]{:S(2)}, u32[]{:S(2)}) collective-permute-start(bf16[56,1280]{1,0:T(8,128)(2,1)} %get-tuple-element.91), channel_id=1, source_target_pairs={{0,8},{4,12},{8,0},{12,4},{1,9},{5,13},{9,1},{13,5},{2,10},{6,14},... | collective-permute-start | bytes 430088 | tf_op jit(solution)/shard_map/ppermute | solution.py:724
  32.2 15.5 %collective-permute-start.10 = (bf16[56,1280]{1,0:T(8,128)(2,1)S(1)}, bf16[56,1280]{1,0:T(8,128)(2,1)S(1)}, u32[]{:S(2)}, u32[]{:S(2)}) collective-permute-start(bf16[56,1280]{1,0:T(8,128)(2,1)S(1)} %get-tuple-element.108), channel_id=1, source_target_pairs={{0,8},{4,12},{8,0},{12,4},{1,9},{5,13},{9,1},{13,5},{2,10},{6,14},... | collective-permute-start | bytes 430088 | tf_op jit(solution)/shard_map/ppermute | solution.py:724
  37.1 10.6 %collective-permute-start.11 = (bf16[56,1280]{1,0:T(8,128)(2,1)S(1)}, bf16[56,1280]{1,0:T(8,128)(2,1)S(1)}, u32[]{:S(2)}, u32[]{:S(2)}) collective-permute-start(bf16[56,1280]{1,0:T(8,128)(2,1)S(1)} %get-tuple-element.109), channel_id=1, source_target_pairs={{0,4},{4,8},{8,12},{12,0},{1,5},{5,9},{9,13},{13,1},{2,6},{6,10},{... | collective-permute-start | bytes 430088 | tf_op jit(solution)/shard_map/ppermute | solution.py:724
  37.4 10.3 %collective-permute-start.9 = (bf16[56,1280]{1,0:T(8,128)(2,1)S(1)}, bf16[56,1280]{1,0:T(8,128)(2,1)S(1)}, u32[]{:S(2)}, u32[]{:S(2)}) collective-permute-start(bf16[56,1280]{1,0:T(8,128)(2,1)S(1)} %get-tuple-element.107), channel_id=1, source_target_pairs={{0,12},{4,0},{8,4},{12,8},{1,13},{5,1},{9,5},{13,9},{2,14},{6,2},{... | collective-permute-start | bytes 430088 | tf_op jit(solution)/shard_map/ppermute | solution.py:724
  51.2 13.7 %collective-permute-start.12 = (bf16[56,1280]{1,0:T(8,128)(2,1)}, bf16[56,1280]{1,0:T(8,128)(2,1)}, u32[]{:S(2)}, u32[]{:S(2)}) collective-permute-start(bf16[56,1280]{1,0:T(8,128)(2,1)} %get-tuple-element.114), channel_id=1, source_target_pairs={{0,4},{4,8},{8,12},{12,0},{1,5},{5,9},{9,13},{13,1},{2,6},{6,10},{... | collective-permute-start | bytes 430088 | tf_op jit(solution)/shard_map/ppermute | solution.py:724
  53.5 11.4 %collective-permute-start.13 = (bf16[56,1280]{1,0:T(8,128)(2,1)}, bf16[56,1280]{1,0:T(8,128)(2,1)}, u32[]{:S(2)}, u32[]{:S(2)}) collective-permute-start(bf16[56,1280]{1,0:T(8,128)(2,1)} %get-tuple-element.115), channel_id=1, source_target_pairs={{0,8},{4,12},{8,0},{12,4},{1,9},{5,13},{9,1},{13,5},{2,10},{6,14},... | collective-permute-start | bytes 430088 | tf_op jit(solution)/shard_map/ppermute | solution.py:724
  55.0 10.0 %collective-permute-start.14 = (bf16[56,1280]{1,0:T(8,128)(2,1)}, bf16[56,1280]{1,0:T(8,128)(2,1)}, u32[]{:S(2)}, u32[]{:S(2)}) collective-permute-start(bf16[56,1280]{1,0:T(8,128)(2,1)} %get-tuple-element.116), channel_id=1, source_target_pairs={{0,12},{4,0},{8,4},{12,8},{1,13},{5,1},{9,5},{13,9},{2,14},{6,2},{... | collective-permute-start | bytes 430088 | tf_op jit(solution)/shard_map/ppermute | solution.py:724
  67.4 10.4 %collective-permute-start.15 = (bf16[56,1280]{1,0:T(8,128)(2,1)S(1)}, bf16[56,1280]{1,0:T(8,128)(2,1)S(1)}, u32[]{:S(2)}, u32[]{:S(2)}) collective-permute-start(bf16[56,1280]{1,0:T(8,128)(2,1)S(1)} %get-tuple-element.125), channel_id=1, source_target_pairs={{0,12},{4,0},{8,4},{12,8},{1,13},{5,1},{9,5},{13,9},{2,14},{6,2},{... | collective-permute-start | bytes 430088 | tf_op jit(solution)/shard_map/ppermute | solution.py:724
  73.5 11.2 %collective-permute-start.16 = (bf16[56,1280]{1,0:T(8,128)(2,1)S(1)}, bf16[56,1280]{1,0:T(8,128)(2,1)S(1)}, u32[]{:S(2)}, u32[]{:S(2)}) collective-permute-start(bf16[56,1280]{1,0:T(8,128)(2,1)S(1)} %get-tuple-element.126), channel_id=1, source_target_pairs={{0,8},{4,12},{8,0},{12,4},{1,9},{5,13},{9,1},{13,5},{2,10},{6,14},... | collective-permute-start | bytes 430088 | tf_op jit(solution)/shard_map/ppermute | solution.py:724
  73.5 11.2 %collective-permute-start.17 = (bf16[56,1280]{1,0:T(8,128)(2,1)S(1)}, bf16[56,1280]{1,0:T(8,128)(2,1)S(1)}, u32[]{:S(2)}, u32[]{:S(2)}) collective-permute-start(bf16[56,1280]{1,0:T(8,128)(2,1)S(1)} %get-tuple-element.127), channel_id=1, source_target_pairs={{0,4},{4,8},{8,12},{12,0},{1,5},{5,9},{9,13},{13,1},{2,6},{6,10},{... | collective-permute-start | bytes 430088 | tf_op jit(solution)/shard_map/ppermute | solution.py:724
  85.7 14.0 %collective-permute-start.18 = (bf16[192,1280]{1,0:T(8,128)(2,1)S(1)}, bf16[192,1280]{1,0:T(8,128)(2,1)S(1)}, u32[]{:S(2)}, u32[]{:S(2)}) collective-permute-start(bf16[192,1280]{1,0:T(8,128)(2,1)S(1)} %shard_map.137.refs_0_), channel_id=1, source_target_pairs={{4,0},{8,4},{12,8},{5,1},{9,5},{13,9},{6,2},{10,6},{14,10},{7,3},{... | collective-permute-start | bytes 1474568 | tf_op jit(solution)/shard_map/ppermute | solution.py:732
  87.0 14.0 %collective-permute-start.20 = (bf16[192,1280]{1,0:T(8,128)(2,1)S(1)}, bf16[192,1280]{1,0:T(8,128)(2,1)S(1)}, u32[]{:S(2)}, u32[]{:S(2)}) collective-permute-start(bf16[192,1280]{1,0:T(8,128)(2,1)S(1)} %shard_map.137.refs_0_), channel_id=1, source_target_pairs={{0,4},{4,8},{8,12},{1,5},{5,9},{9,13},{2,6},{6,10},{10,14},{3,7},{... | collective-permute-start | bytes 1474568 | tf_op jit(solution)/shard_map/ppermute | solution.py:733
  99.7 13.7 %collective-permute-start.19 = (bf16[192,1280]{1,0:T(8,128)(2,1)S(1)}, bf16[192,1280]{1,0:T(8,128)(2,1)S(1)}, u32[]{:S(2)}, u32[]{:S(2)}) collective-permute-start(bf16[192,1280]{1,0:T(8,128)(2,1)S(1)} %collective-permute-done.18.refs_1_.refs_4_), channel_id=1, source_target_pairs={{4,0},{8,4},{5,1},{9,5},{6,2},{10,6},{7,3},{11,7},{20,16},{24,20},... | collective-permute-start | bytes 1474568 | tf_op jit(solution)/shard_map/ppermute | solution.py:739
  101.0 12.4 %collective-permute-start.21 = (bf16[192,1280]{1,0:T(8,128)(2,1)S(1)}, bf16[192,1280]{1,0:T(8,128)(2,1)S(1)}, u32[]{:S(2)}, u32[]{:S(2)}) collective-permute-start(bf16[192,1280]{1,0:T(8,128)(2,1)S(1)} %collective-permute-done.20.refs_2_.refs_5_), channel_id=1, source_target_pairs={{4,8},{8,12},{5,9},{9,13},{6,10},{10,14},{7,11},{11,15},{20,24},{2... | collective-permute-start | bytes 1474568 | tf_op jit(solution)/shard_map/ppermute | solution.py:740
  113.4 12.9 %collective-permute-start.22 = (bf16[192,1280]{1,0:T(8,128)(2,1)S(1)}, bf16[192,1280]{1,0:T(8,128)(2,1)S(1)}, u32[]{:S(2)}, u32[]{:S(2)}) collective-permute-start(bf16[192,1280]{1,0:T(8,128)(2,1)S(1)} %collective-permute-done.19.refs_0_), channel_id=1, source_target_pairs={{4,0},{5,1},{6,2},{7,3},{20,16},{21,17},{22,18},{23,19}} | collective-permute-start | bytes 1474568 | tf_op jit(solution)/shard_map/ppermute | solution.py:746
  114.7 11.6 %collective-permute-start.23 = (bf16[192,1280]{1,0:T(8,128)(2,1)S(1)}, bf16[192,1280]{1,0:T(8,128)(2,1)S(1)}, u32[]{:S(2)}, u32[]{:S(2)}) collective-permute-start(bf16[192,1280]{1,0:T(8,128)(2,1)S(1)} %collective-permute-done.21.refs_1_), channel_id=1, source_target_pairs={{8,12},{9,13},{10,14},{11,15},{24,28},{25,29},{26,30},{27,31}} | collective-permute-start | bytes 1474568 | tf_op jit(solution)/shard_map/ppermute | solution.py:747
  152.6 11.2 %collective-permute-start.28 = (bf16[512,1280]{1,0:T(8,128)(2,1)S(1)}, bf16[512,1280]{1,0:T(8,128)(2,1)S(1)}, u32[]{:S(2)}, u32[]{:S(2)}) collective-permute-start(bf16[512,1280]{1,0:T(8,128)(2,1)S(1)} %get-tuple-element.153), channel_id=1, source_target_pairs={{0,1},{1,0},{2,3},{3,2},{4,5},{5,4},{6,7},{7,6},{8,9},{9,8},{10,11... | collective-permute-start | bytes 3932168 | tf_op jit(solution)/shard_map/ppermute | solution.py:719
  156.8 10.6 %collective-permute-start.30 = (bf16[128,1280]{1,0:T(8,128)(2,1)S(1)}, bf16[128,1280]{1,0:T(8,128)(2,1)S(1)}, u32[]{:S(2)}, u32[]{:S(2)}) collective-permute-start(bf16[128,1280]{1,0:T(8,128)(2,1)S(1)} %get-tuple-element.151), channel_id=1, source_target_pairs={{0,16},{16,0},{1,17},{17,1},{2,18},{18,2},{3,19},{19,3},{4,20},{20... | collective-permute-start | bytes 983048 | tf_op jit(solution)/shard_map/ppermute | solution.py:719
  157.0 10.6 %collective-permute-start.31 = (bf16[128,1280]{1,0:T(8,128)(2,1)S(1)}, bf16[128,1280]{1,0:T(8,128)(2,1)S(1)}, u32[]{:S(2)}, u32[]{:S(2)}) collective-permute-start(bf16[128,1280]{1,0:T(8,128)(2,1)S(1)} %get-tuple-element.155), channel_id=1, source_target_pairs={{0,2},{2,0},{1,3},{3,1},{4,6},{6,4},{5,7},{7,5},{8,10},{10,8},{9,1... | collective-permute-start | bytes 983048 | tf_op jit(solution)/shard_map/ppermute | solution.py:719
  158.6 15.9 %collective-permute-start.29 = (bf16[128,1280]{1,0:T(8,128)(2,1)S(1)}, bf16[128,1280]{1,0:T(8,128)(2,1)S(1)}, u32[]{:S(2)}, u32[]{:S(2)}) collective-permute-start(bf16[128,1280]{1,0:T(8,128)(2,1)S(1)} %get-tuple-element.154), channel_id=1, source_target_pairs={{0,16},{16,0},{1,17},{17,1},{2,18},{18,2},{3,19},{19,3},{4,20},{20... | collective-permute-start | bytes 983048 | tf_op jit(solution)/shard_map/ppermute | solution.py:719
  160.4 14.2 %collective-permute-start.33 = (bf16[128,1280]{1,0:T(8,128)(2,1)S(1)}, bf16[128,1280]{1,0:T(8,128)(2,1)S(1)}, u32[]{:S(2)}, u32[]{:S(2)}) collective-permute-start(bf16[128,1280]{1,0:T(8,128)(2,1)S(1)} %get-tuple-element.157), channel_id=1, source_target_pairs={{0,2},{2,0},{1,3},{3,1},{4,6},{6,4},{5,7},{7,5},{8,10},{10,8},{9,1... | collective-permute-start | bytes 983048 | tf_op jit(solution)/shard_map/ppermute | solution.py:719
  168.4 12.3 %collective-permute-start.32 = (bf16[128,1280]{1,0:T(8,128)(2,1)S(1)}, bf16[128,1280]{1,0:T(8,128)(2,1)S(1)}, u32[]{:S(2)}, u32[]{:S(2)}) collective-permute-start(bf16[128,1280]{1,0:T(8,128)(2,1)S(1)} %get-tuple-element.156), channel_id=1, source_target_pairs={{0,2},{2,0},{1,3},{3,1},{4,6},{6,4},{5,7},{7,5},{8,10},{10,8},{9,1... | collective-permute-start | bytes 983048 | tf_op jit(solution)/shard_map/ppermute | solution.py:719
  170.0 10.7 %collective-permute-start.34 = (bf16[128,1280]{1,0:T(8,128)(2,1)S(1)}, bf16[128,1280]{1,0:T(8,128)(2,1)S(1)}, u32[]{:S(2)}, u32[]{:S(2)}) collective-permute-start(bf16[128,1280]{1,0:T(8,128)(2,1)S(1)} %get-tuple-element.158), channel_id=1, source_target_pairs={{0,16},{16,0},{1,17},{17,1},{2,18},{18,2},{3,19},{19,3},{4,20},{20... | collective-permute-start | bytes 983048 | tf_op jit(solution)/shard_map/ppermute | solution.py:719
  181.6 10.7 %collective-permute-start.35 = (bf16[128,1280]{1,0:T(8,128)(2,1)S(1)}, bf16[128,1280]{1,0:T(8,128)(2,1)S(1)}, u32[]{:S(2)}, u32[]{:S(2)}) collective-permute-start(bf16[128,1280]{1,0:T(8,128)(2,1)S(1)} %get-tuple-element.159.refs_0_), channel_id=1, source_target_pairs={{0,2},{2,0},{1,3},{3,1},{4,6},{6,4},{5,7},{7,5},{8,10},{10,8},{9,1... | collective-permute-start | bytes 983048 | tf_op jit(solution)/shard_map/ppermute | solution.py:719
  183.1 10.8 %collective-permute-start.37 = (bf16[128,1280]{1,0:T(8,128)(2,1)S(1)}, bf16[128,1280]{1,0:T(8,128)(2,1)}, u32[]{:S(2)}, u32[]{:S(2)}) collective-permute-start(bf16[128,1280]{1,0:T(8,128)(2,1)S(1)} %get-tuple-element.160.refs_1_), channel_id=1, source_target_pairs={{0,16},{16,0},{1,17},{17,1},{2,18},{18,2},{3,19},{19,3},{4,20},{20... | collective-permute-start | bytes 983048 | tf_op jit(solution)/shard_map/ppermute | solution.py:719
  184.8 12.8 %collective-permute-start.41 = (bf16[128,1280]{1,0:T(8,128)(2,1)S(1)}, bf16[128,1280]{1,0:T(8,128)(2,1)}, u32[]{:S(2)}, u32[]{:S(2)}) collective-permute-start(bf16[128,1280]{1,0:T(8,128)(2,1)S(1)} %get-tuple-element.160.refs_1_), channel_id=1, source_target_pairs={{0,2},{2,0},{1,3},{3,1},{4,6},{6,4},{5,7},{7,5},{8,10},{10,8},{9,1... | collective-permute-start | bytes 983048 | tf_op jit(solution)/shard_map/ppermute | solution.py:719
  185.4 13.4 %collective-permute-start.42 = (bf16[128,1280]{1,0:T(8,128)(2,1)S(1)}, bf16[128,1280]{1,0:T(8,128)(2,1)}, u32[]{:S(2)}, u32[]{:S(2)}) collective-permute-start(bf16[128,1280]{1,0:T(8,128)(2,1)S(1)} %get-tuple-element.159.refs_0_), channel_id=1, source_target_pairs={{0,16},{16,0},{1,17},{17,1},{2,18},{18,2},{3,19},{19,3},{4,20},{20... | collective-permute-start | bytes 983048 | tf_op jit(solution)/shard_map/ppermute | solution.py:719
  185.7 15.0 %collective-permute-start.43 = (bf16[128,1280]{1,0:T(8,128)(2,1)S(1)}, bf16[128,1280]{1,0:T(8,128)(2,1)S(1)}, u32[]{:S(2)}, u32[]{:S(2)}) collective-permute-start(bf16[128,1280]{1,0:T(8,128)(2,1)S(1)} %get-tuple-element.159.refs_0_), channel_id=1, source_target_pairs={{0,1},{1,0},{2,3},{3,2},{4,5},{5,4},{6,7},{7,6},{8,9},{9,8},{10,11... | collective-permute-start | bytes 983048 | tf_op jit(solution)/shard_map/ppermute | solution.py:719
  198.8 10.1 %collective-permute-start.36 = (bf16[128,1280]{1,0:T(8,128)(2,1)S(1)}, bf16[128,1280]{1,0:T(8,128)(2,1)S(1)}, u32[]{:S(2)}, u32[]{:S(2)}) collective-permute-start(bf16[128,1280]{1,0:T(8,128)(2,1)S(1)} %collective-permute-done.35.refs_2_), channel_id=1, source_target_pairs={{0,16},{16,0},{1,17},{17,1},{2,18},{18,2},{3,19},{19,3},{4,20},{20... | collective-permute-start | bytes 983048 | tf_op jit(solution)/shard_map/ppermute | solution.py:719
  200.2 10.1 %collective-permute-start.38 = (bf16[128,1280]{1,0:T(8,128)(2,1)}, bf16[128,1280]{1,0:T(8,128)(2,1)S(1)}, u32[]{:S(2)}, u32[]{:S(2)}) collective-permute-start(bf16[128,1280]{1,0:T(8,128)(2,1)} %collective-permute-done.37.refs_5_), channel_id=1, source_target_pairs={{0,2},{2,0},{1,3},{3,1},{4,6},{6,4},{5,7},{7,5},{8,10},{10,8},{9,1... | collective-permute-start | bytes 983048 | tf_op jit(solution)/shard_map/ppermute | solution.py:719
  (55 other events, 287.5 us)
where the time goes:
time: 220 us; the launch traced here: 219 us
  waiting for transfers between devices  87.9 us (40%)
  starting transfers between devices  64.2 us (29%)
  Pallas kernels  43.6 us (20%)
  local copies, waits for them, and re-layouts  21.7 us (10%)
    ppermute x28, waiting for transfers between devices, swap(): return lax.ppermute(value, axis, [(0, 1), (1, 0)])  34.3 us
    ppermute x15, starting transfers between devices, rotate(): lax.ppermute(value, axis, [(i, (i + by) % count) for i in range(count)])  33.6 us
    ppermute x15, waiting for transfers between devices, rotate(): lax.ppermute(value, axis, [(i, (i + by) % count) for i in range(count)])  28.8 us
    ppermute x28, starting transfers between devices, swap(): return lax.ppermute(value, axis, [(0, 1), (1, 0)])  20.8 us
    unnamed x77, local copies, waits for them, and re-layouts  20.2 us
    ppermute x1, waiting for transfers between devices, line_end(): lax.ppermute(left_far, 'expert', [(1, 0)])  10.9 us
    pallas_call x3, Pallas kernels, head_gradient(): call(kernel, tuple((bf16_rows(each * BLOCK_ROWS, width) for _ in range(ou...  10.7 us
    ppermute x1, waiting for transfers between devices, line_near(): left = lax.ppermute(value, 'expert', [(1, 0), (2, 1), (3, 2)])  8.15 us
  transfers between devices with their start and end apart: 49, of which 25 were waited for; matrix products, arithmetic and copies ran while one was open for 1% of the time, Pallas kernels for 9%

commit v1 on v0

--- a/solution.py
+++ b/solution.py
@@ -361,21 +361,19 @@
 
 
 def head_logits(
-    fill, first_slot, count, pieces, member, weight, label_weight, frame_count, earlier
+    fill, first_slot, count, pieces, member, weight, label_weight, frame_count
 ):
     given = len(pieces)
-    ahead = 0 if earlier is None else earlier.shape[0]
     span, width = pieces[0].shape
     row_count = count * span
     shard = weight.shape[0]
     height = round_up(shard, BLOCK_ROWS)
     entries = row_count // frame_count * COLS
     first_entry = first_slot * entries // count
-    others = [] if earlier is None else [earlier]
 
     def kernel(member_ref, weight_ref, label_ref, *refs):
         piece_refs = refs[:given]
-        logits_ref, rows_ref, stats_ref = refs[given + len(others) :]
+        logits_ref, rows_ref, stats_ref = refs[given:]
 
         def put(slot, piece_ref):
             rows_ref[slot * span : (slot + 1) * span] = piece_ref[...]
@@ -417,23 +415,21 @@
         place = lax.broadcasted_iota(jnp.int32, (COLS, row_count), 0)
         stats = jnp.where(place == PEAK, peak, picked)
         stats = jnp.where(place == TOTAL, total, stats)
-        for slot in range(ahead):
-            stats_ref[slot] = refs[given][slot]
         for slot in range(count):
-            stats_ref[ahead + slot] = stats[:, slot * span : (slot + 1) * span]
+            stats_ref[slot] = stats[:, slot * span : (slot + 1) * span]
 
     return call(
         kernel,
         (
             jax.ShapeDtypeStruct((height, row_count), jnp.float32),
             bf16_rows(row_count, width),
-            jax.ShapeDtypeStruct((ahead + count, COLS, span), jnp.float32),
+            jax.ShapeDtypeStruct((count, COLS, span), jnp.float32),
         ),
         2 * height * row_count * width,
         LARGE_LIMIT,
-        in_specs=[smem_spec()] + [vmem_spec()] * (2 + given + len(others)),
+        in_specs=[smem_spec()] + [vmem_spec()] * (2 + given),
         out_specs=tuple(vmem_spec() for _ in range(3)),
-    )(member, weight, label_weight, *pieces, *others)
+    )(member, weight, label_weight, *pieces)
 
 
 def fill_near(place, piece_refs, put, put_if):
@@ -471,8 +467,9 @@
 
 
 def ctc_pass(stats, slots, notes, frame_count, label_max, kept):
-    sources = len(stats)
-    count, _, span = stats[0].shape
+    calls, sources = len(stats), len(stats[0])
+    each, _, span = stats[0][0].shape
+    count = calls * each
     row_count = count * span
     utterances = notes.shape[0]
     entries = utterances * COLS
@@ -493,11 +490,18 @@
             blank_bwd,
             label_bwd,
             occupancy_ref,
-        ) = refs[sources:]
+        ) = refs[calls * sources :]
         place = lax.broadcasted_iota(jnp.int32, (COLS, span), 0)
         turn_ref[...] = jnp.zeros(turn_ref.shape, jnp.float32)
         for slot in range(count):
-            found = [refs[k][slots_ref[k * count + slot]] for k in range(sources)]
+            found = []
+            for k in range(sources):
+                where = slots_ref[k * count + slot]
+                part = refs[k][where % each]
+                for other in range(1, calls):
+                    later = refs[other * sources + k][where % each]
+                    part = jnp.where(where >= other * each, later, part)
+                found.append(part)
             joined = found[0]
             peak = found[0][PEAK : PEAK + 1]
             for other in found[1:]:
@@ -574,7 +578,8 @@
         end_state = jnp.sum(jnp.where(lane == counts, fwd_blank, 0.0), axis=1, keepdims=True)
         near_state = jnp.sum(jnp.where(lane == counts - 1, fwd_label, 0.0), axis=1, keepdims=True)
         log_like = log_add(end_state, near_state)
-        loss_ref[...] = -log_like[:kept]
+        turned_losses = jnp.transpose(jnp.broadcast_to(-log_like, (utterances, LANES)), (1, 0))
+        loss_ref[...] = turned_losses[:1, :kept]
 
         def occupy(step, carry):
             blank = jnp.exp(blank_fwd[step] + blank_bwd[step] - log_like)
@@ -613,15 +618,15 @@
             jax.ShapeDtypeStruct((COLS, row_count), jnp.float32),
             bf16_rows(entries, row_count),
             bf16_rows(entries, row_count),
-            jax.ShapeDtypeStruct((kept, 1), jnp.float32),
+            jax.ShapeDtypeStruct((1, kept), jnp.float32),
         ),
         1 << 26,
-        in_specs=[smem_spec()] + [vmem_spec()] * (1 + sources),
+        in_specs=[smem_spec()] + [vmem_spec()] * (1 + calls * sources),
         out_specs=tuple(vmem_spec() for _ in range(4)),
         scratch_shapes=[pltpu.VMEM((LANES, tall), jnp.float32), table]
         + [held] * 6
         + [table],
-    )(slots, notes, *stats)
+    )(slots, notes, *[value for group in stats for value in group])
 
 
 def head_gradient(logits, rows, occupancy, high, low, places, order, outputs, each):
@@ -1023,35 +1028,40 @@
                 frame_count,
             )
 
-    def logits_of(fill, first, count, pieces, earlier):
+    def logits_of(fill, first, count, pieces):
         return head_logits(
-            fill, first, count, pieces, member_ref, weight_rows, label_weight, frame_count, earlier
+            fill, first, count, pieces, member_ref, weight_rows, label_weight, frame_count
         )
 
     if line:
         left, right = line_near(normed)
         far = line_far(left, right)
-        heads = [logits_of(fill_near, 0, 2, [normed, left, right], None)]
+        heads = [logits_of(fill_near, 0, 2, [normed, left, right])]
         far, heads[0] = lax.optimization_barrier((far, heads[0]))
         end = line_end(*far)
-        heads.append(logits_of(fill_far, 2, 2, [*far, *end, left, right], heads[0][2]))
-        stats = heads[1][2]
-        found = [stats] + [rotate(stats, "expert", -k) for k in range(1, group_size)]
+        heads.append(logits_of(fill_far, 2, 2, [*far, *end, left, right]))
+        found = [
+            [head[2]] + [rotate(head[2], "expert", -k) for k in range(1, group_size)]
+            for head in heads
+        ]
     else:
         gathered = lax.all_gather(normed, "expert")
         pieces = [gathered[k] for k in range(group_size)]
-        heads = [logits_of(fill_all, 0, group_size, pieces, None)]
+        heads = [logits_of(fill_all, 0, group_size, pieces)]
         gathered = lax.all_gather(heads[0][2], "expert")
         found = [
-            lax.dynamic_index_in_dim(gathered, (member + k) % group_size, 0, keepdims=False)
-            for k in range(group_size)
+            [
+                lax.dynamic_index_in_dim(gathered, (member + k) % group_size, 0, keepdims=False)
+                for k in range(group_size)
+            ]
         ]
     kept_losses = per_section if line else group_size * per_section
     occupancy, high, low, losses = ctc_pass(
         found, slots, names, frame_count, label_max, kept_losses
     )
     if not line:
-        losses = lax.dynamic_slice(losses, (member * per_section, 0), (per_section, 1))
+        losses = lax.dynamic_slice(losses, (0, member * per_section), (1, per_section))
+    losses = jnp.transpose(losses)
 
     def gradient(order, outputs, each):
         return head_gradient(
@@ -1081,7 +1091,7 @@
         a_y, b_x = swap(a, "dpo"), swap(b, "section")
         b_y, a_x = swap(b, "dpo"), swap(a, "section")
         a_xy, b_xy = swap(a_y, "section"), swap(b_x, "dpo")
-        a_y, b_y, a_x, b_x = lax.optimization_barrier((a_y, b_y, a_x, b_x))
+        b_y, a_x = lax.optimization_barrier((b_y, a_x, a_xy, b_xy))[:2]
         mine = [a, b, a_y, b_y, a_x, b_x]
         theirs = [swap(value, "dpi") for value in mine]
         whole = assemble(mine + theirs, first_offsets, shard)

time: 220 us -> 215 us (0.977)
  starting transfers between devices: 64.2 us -> 74.8 us
  waiting for transfers between devices: 87.9 us -> 78.9 us
  local copies, waits for them, and re-layouts: 21.7 us -> 16 us
    ppermute x15 -> x18, starting transfers between devices: 33.6 us -> 42.4 us  [rotate(): lax.ppermute(value, axis, [(i, (i + by) % count) for i in range(count)])]
    ppermute x1, waiting for transfers between devices: 10.9 us -> 3.89 us  [line_end(): lax.ppermute(left_far, 'expert', [(1, 0)])]
    unnamed x77 -> x64, local copies, waits for them, and re-layouts: 20.2 us -> 14.6 us
    ppermute x15 -> x18, waiting for transfers between devices: 28.8 us -> 28.4 us  [rotate(): lax.ppermute(value, axis, [(i, (i + by) % count) for i in range(count)])]
  transfers between devices with their start and end apart: 49 -> 52, of which waited for: 25 -> 26; matrix products, arithmetic and copies ran while one was open for 1% -> 1% of each run, Pallas kernels for 9% -> 10%
where the time goes in v1:
time: 215 us; the launch traced here: 214 us
  waiting for transfers between devices  78.9 us (37%)
  starting transfers between devices  74.8 us (35%)
  Pallas kernels  42.9 us (20%)
  local copies, waits for them, and re-layouts  16 us (7%)
    ppermute x18, starting transfers between devices, rotate(): lax.ppermute(value, axis, [(i, (i + by) % count) for i in range(count)])  42.4 us
    ppermute x28, waiting for transfers between devices, swap(): return lax.ppermute(value, axis, [(0, 1), (1, 0)])  32.6 us
    ppermute x18, waiting for transfers between devices, rotate(): lax.ppermute(value, axis, [(i, (i + by) % count) for i in range(count)])  28.4 us
    ppermute x28, starting transfers between devices, swap(): return lax.ppermute(value, axis, [(0, 1), (1, 0)])  22.6 us
    unnamed x64, local copies, waits for them, and re-layouts  14.6 us
    pallas_call x3, Pallas kernels, head_gradient(): call(kernel, tuple((bf16_rows(each * BLOCK_ROWS, width) for _ in range(ou...  10.6 us
    ppermute x1, waiting for transfers between devices, line_near(): left = lax.ppermute(value, 'expert', [(1, 0), (2, 1), (3, 2)])  8.16 us
    pallas_call x1, Pallas kernels, ctc_pass(): call(kernel, (jax.ShapeDtypeStruct((COLS, row_count), jnp.float32), bf16_...  6.84 us
  transfers between devices with their start and end apart: 52, of which 26 were waited for; matrix products, arithmetic and copies ran while one was open for 1% of the time, Pallas kernels for 10%

profile of v1, /device:TPU:0, one launch (start us, length us, event | category | flops | bytes accessed | tf_op | source)
XLA Modules:
  0.0 214.2 jit_solution(7485567786934338653)
XLA Ops:
  0.7 3.0 %collective-permute-start = (s32[8,48]{1,0:T(8,128)}, s32[8,48]{1,0:T(8,128)S(1)}, u32[]{:S(2)}, u32[]{:S(2)}) collective-permute-start(s32[8,48]{1,0:T(8,128)} %bitcast.56), channel_id=1, source_target_pairs={{0,16},{16,0},{1,17},{17,1},{2,18},{18,2},{3,19},{19,3},{4,20},{20... | collective-permute-start | bytes 4616 | tf_op jit(solution)/shard_map/ppermute | solution.py:724
  14.2 2.6 %collective-permute-start.4 = (bf16[56,1280]{1,0:T(8,128)(2,1)}, bf16[56,1280]{1,0:T(8,128)(2,1)}, u32[]{:S(2)}, u32[]{:S(2)}) collective-permute-start(bf16[56,1280]{1,0:T(8,128)(2,1)} %get-tuple-element.89), channel_id=1, source_target_pairs={{0,8},{4,12},{8,0},{12,4},{1,9},{5,13},{9,1},{13,5},{2,10},{6,14},... | collective-permute-start | bytes 430088 | tf_op jit(solution)/shard_map/ppermute | solution.py:729
  18.7 2.8 %collective-permute-done.3.refs_7_ = bf16[56,1280]{1,0:T(8,128)(2,1)S(1)} collective-permute-done((bf16[56,1280]{1,0:T(8,128)(2,1)}, bf16[56,1280]{1,0:T(8,128)(2,1)S(1)}, u32[]{:S(2)}, u32[]{:S(2)}) %collective-permute-start.3) | collective-permute-done | bytes 143392 | tf_op jit(solution)/shard_map/ppermute | solution.py:729
  22.5 3.3 %collective-permute-done.4.refs_8_ = bf16[56,1280]{1,0:T(8,128)(2,1)} collective-permute-done((bf16[56,1280]{1,0:T(8,128)(2,1)}, bf16[56,1280]{1,0:T(8,128)(2,1)}, u32[]{:S(2)}, u32[]{:S(2)}) %collective-permute-start.4) | collective-permute-done | bytes 143392 | tf_op jit(solution)/shard_map/ppermute | solution.py:729
  32.2 4.9 %collective-permute-start.10 = (bf16[56,1280]{1,0:T(8,128)(2,1)S(1)}, bf16[56,1280]{1,0:T(8,128)(2,1)S(1)}, u32[]{:S(2)}, u32[]{:S(2)}) collective-permute-start(bf16[56,1280]{1,0:T(8,128)(2,1)S(1)} %get-tuple-element.106), channel_id=1, source_target_pairs={{0,8},{4,12},{8,0},{12,4},{1,9},{5,13},{9,1},{13,5},{2,10},{6,14},... | collective-permute-start | bytes 430088 | tf_op jit(solution)/shard_map/ppermute | solution.py:729
  37.4 3.5 %collective-permute-start.9 = (bf16[56,1280]{1,0:T(8,128)(2,1)S(1)}, bf16[56,1280]{1,0:T(8,128)(2,1)S(1)}, u32[]{:S(2)}, u32[]{:S(2)}) collective-permute-start(bf16[56,1280]{1,0:T(8,128)(2,1)S(1)} %get-tuple-element.105), channel_id=1, source_target_pairs={{0,12},{4,0},{8,4},{12,8},{1,13},{5,1},{9,5},{13,9},{2,14},{6,2},{... | collective-permute-start | bytes 430088 | tf_op jit(solution)/shard_map/ppermute | solution.py:729
  40.9 6.7 %collective-permute-done.10.refs_4_.refs_2_ = bf16[56,1280]{1,0:T(8,128)(2,1)S(1)} collective-permute-done((bf16[56,1280]{1,0:T(8,128)(2,1)S(1)}, bf16[56,1280]{1,0:T(8,128)(2,1)S(1)}, u32[]{:S(2)}, u32[]{:S(2)}) %collective-permute-start.10) | collective-permute-done | bytes 143392 | tf_op jit(solution)/shard_map/ppermute | solution.py:729
  55.0 2.9 %collective-permute-start.14 = (bf16[56,1280]{1,0:T(8,128)(2,1)}, bf16[56,1280]{1,0:T(8,128)(2,1)}, u32[]{:S(2)}, u32[]{:S(2)}) collective-permute-start(bf16[56,1280]{1,0:T(8,128)(2,1)} %get-tuple-element.115), channel_id=1, source_target_pairs={{0,12},{4,0},{8,4},{12,8},{1,13},{5,1},{9,5},{13,9},{2,14},{6,2},{... | collective-permute-start | bytes 430088 | tf_op jit(solution)/shard_map/ppermute | solution.py:729
  57.8 2.4 %copy-done.1 = bf16[1280,2000]{0,1:T(8,128)(2,1)S(1)} copy-done((bf16[1280,2000]{0,1:T(8,128)(2,1)S(1)}, bf16[1280,2000]{0,1:T(8,128)(2,1)}, u32[]{:S(2)}) %copy-start.1) | copy-done | bytes 5120024
  67.3 6.1 %collective-permute-start.15 = (bf16[56,1280]{1,0:T(8,128)(2,1)S(1)}, bf16[56,1280]{1,0:T(8,128)(2,1)S(1)}, u32[]{:S(2)}, u32[]{:S(2)}) collective-permute-start(bf16[56,1280]{1,0:T(8,128)(2,1)S(1)} %get-tuple-element.122), channel_id=1, source_target_pairs={{0,12},{4,0},{8,4},{12,8},{1,13},{5,1},{9,5},{13,9},{2,14},{6,2},{... | collective-permute-start | bytes 430088 | tf_op jit(solution)/shard_map/ppermute | solution.py:729
  74.1 3.6 %collective-permute-done.15.refs_3_ = bf16[56,1280]{1,0:T(8,128)(2,1)S(1)} collective-permute-done((bf16[56,1280]{1,0:T(8,128)(2,1)S(1)}, bf16[56,1280]{1,0:T(8,128)(2,1)S(1)}, u32[]{:S(2)}, u32[]{:S(2)}) %collective-permute-start.15) | collective-permute-done | bytes 143392 | tf_op jit(solution)/shard_map/ppermute | solution.py:729
  77.7 7.0 %collective-permute-done.16.refs_4_ = bf16[56,1280]{1,0:T(8,128)(2,1)S(1)} collective-permute-done((bf16[56,1280]{1,0:T(8,128)(2,1)S(1)}, bf16[56,1280]{1,0:T(8,128)(2,1)S(1)}, u32[]{:S(2)}, u32[]{:S(2)}) %collective-permute-start.16) | collective-permute-done | bytes 143392 | tf_op jit(solution)/shard_map/ppermute | solution.py:729
  87.0 4.6 %collective-permute-start.20 = (bf16[192,1280]{1,0:T(8,128)(2,1)S(1)}, bf16[192,1280]{1,0:T(8,128)(2,1)S(1)}, u32[]{:S(2)}, u32[]{:S(2)}) collective-permute-start(bf16[192,1280]{1,0:T(8,128)(2,1)S(1)} %shard_map.137.refs_0_), channel_id=1, source_target_pairs={{0,4},{4,8},{8,12},{1,5},{5,9},{9,13},{2,6},{6,10},{10,14},{3,7},{... | collective-permute-start | bytes 1474568 | tf_op jit(solution)/shard_map/ppermute | solution.py:738
  91.6 8.2 %collective-permute-done.18.refs_1_.refs_4_ = bf16[192,1280]{1,0:T(8,128)(2,1)S(1)} collective-permute-done((bf16[192,1280]{1,0:T(8,128)(2,1)S(1)}, bf16[192,1280]{1,0:T(8,128)(2,1)S(1)}, u32[]{:S(2)}, u32[]{:S(2)}) %collective-permute-start.18) | collective-permute-done | bytes 491552 | tf_op jit(solution)/shard_map/ppermute | solution.py:737
  104.2 3.4 %shard_map.138 = (f32[2048,384]{1,0:T(8,128)S(1)}, bf16[384,1280]{1,0:T(8,128)(2,1)S(1)}, f32[2,16,192]{2,1,0:T(8,128)S(1)}) custom-call(s32[1]{0:T(128)} %bitcast.member_ref, bf16[2000,1280]{1,0:T(8,128)(2,1)S(1)} %bitcast.47, bf16[256,1280]{1,0:T(8,128)(2,1)S(1)} %get-tuple-element.125.label_ref, bf16[192,1280]{1,0:T(8,128)(2,1)S(1)} %shard_map.137.refs_0_, ...), custom_call_target="tpu_custom_call" | custom-call | flops 2013265920 | tf_op jit(solution)/shard_map/pallas_call | solution.py:421
  107.6 5.7 %collective-permute-done.19.refs_0_ = bf16[192,1280]{1,0:T(8,128)(2,1)S(1)} collective-permute-done((bf16[192,1280]{1,0:T(8,128)(2,1)S(1)}, bf16[192,1280]{1,0:T(8,128)(2,1)S(1)}, u32[]{:S(2)}, u32[]{:S(2)}) %collective-permute-start.19) | collective-permute-done | bytes 491552 | tf_op jit(solution)/shard_map/ppermute | solution.py:744
  115.4 5.5 %collective-permute-start.22 = (f32[2,16,192]{2,1,0:T(8,128)S(1)}, f32[2,16,192]{2,1,0:T(8,128)S(1)}, u32[]{:S(2)}, u32[]{:S(2)}) collective-permute-start(f32[2,16,192]{2,1,0:T(8,128)S(1)} %get-tuple-element.129.refs_0_), channel_id=1, source_target_pairs={{0,12},{4,0},{8,4},{12,8},{1,13},{5,1},{9,5},{13,9},{2,14},{6,2},{... | collective-permute-start | bytes 73736 | tf_op jit(solution)/shard_map/ppermute | solution.py:729
  124.1 3.9 %collective-permute-done.25.refs_2_ = bf16[192,1280]{1,0:T(8,128)(2,1)S(1)} collective-permute-done((bf16[192,1280]{1,0:T(8,128)(2,1)S(1)}, bf16[192,1280]{1,0:T(8,128)(2,1)S(1)}, u32[]{:S(2)}, u32[]{:S(2)}) %collective-permute-start.25) | collective-permute-done | bytes 491552 | tf_op jit(solution)/shard_map/ppermute | solution.py:751
  128.0 3.3 %shard_map.139 = (f32[2048,384]{1,0:T(8,128)S(1)}, bf16[384,1280]{1,0:T(8,128)(2,1)S(1)}, f32[2,16,192]{2,1,0:T(8,128)S(1)}) custom-call(s32[1]{0:T(128)} %bitcast.member_ref, bf16[2000,1280]{1,0:T(8,128)(2,1)S(1)} %bitcast.48, bf16[256,1280]{1,0:T(8,128)(2,1)S(1)} %get-tuple-element.125.label_ref, bf16[192,1280]{1,0:T(8,128)(2,1)S(1)} %collective-permute-done.19.refs_0_, ...), custom_call_target="tpu_custom_call" | custom-call | flops 2013265920 | tf_op jit(solution)/shard_map/pallas_call | solution.py:421
  131.3 5.3 %collective-permute-start.27 = (f32[2,16,192]{2,1,0:T(8,128)S(1)}, f32[2,16,192]{2,1,0:T(8,128)S(1)}, u32[]{:S(2)}, u32[]{:S(2)}) collective-permute-start(f32[2,16,192]{2,1,0:T(8,128)S(1)} %get-tuple-element.132.refs_4_), channel_id=1, source_target_pairs={{0,12},{4,0},{8,4},{12,8},{1,13},{5,1},{9,5},{13,9},{2,14},{6,2},{... | collective-permute-start | bytes 73736 | tf_op jit(solution)/shard_map/ppermute | solution.py:729
  138.2 3.2 %collective-permute-done.28.refs_6_ = f32[2,16,192]{2,1,0:T(8,128)S(1)} collective-permute-done((f32[2,16,192]{2,1,0:T(8,128)S(1)}, f32[2,16,192]{2,1,0:T(8,128)S(1)}, u32[]{:S(2)}, u32[]{:S(2)}) %collective-permute-start.28) | collective-permute-done | bytes 24608 | tf_op jit(solution)/shard_map/ppermute | solution.py:729
  142.3 6.8 %shard_map.140 = (f32[16,768]{1,0:T(8,128)S(1)}, bf16[256,768]{1,0:T(8,128)(2,1)S(1)}, bf16[256,768]{1,0:T(8,128)(2,1)S(1)}, f32[1,4]{1,0:T(1,128)}) custom-call(s32[16]{0:T(128)S(1)} %fusion.slots_ref, s32[16,128]{1,0:T(8,128)S(1)} %get-tuple-element.110.notes_ref, f32[2,16,192]{2,1,0:T(8,128)S(1)} %get-tuple-element.129.refs_0_, ...), custom_call_target="tpu_custom_call" | custom-call | flops 67108864 | tf_op jit(solution)/shard_map/pallas_call | solution.py:615
  149.2 4.9 %shard_map.141 = (bf16[512,1280]{1,0:T(8,128)(2,1)S(1)}, bf16[512,1280]{1,0:T(8,128)(2,1)S(1)}) custom-call(s32[4]{0:T(128)S(1)} %get-tuple-element.138.order_ref, f32[2048,384]{1,0:T(8,128)S(1)} %get-tuple-element.139.refs_0_, f32[2048,384]{1,0:T(8,128)S(1)} %get-tuple-element.140.refs_1_, bf16[384,1280]{1,0:T(8,128)(2,1)S(1)} %get-tuple-element.141.refs_2_, ...), custom_call_target="tpu_custom_call" | custom-call | flops 2818572288 | tf_op jit(solution)/shard_map/pallas_call | solution.py:666
  154.7 2.8 %shard_map.142.own_ref = bf16[512,1280]{1,0:T(8,128)(2,1)S(1)} custom-call(s32[2]{0:T(128)S(1)} %get-tuple-element.148.order_ref, f32[2048,384]{1,0:T(8,128)S(1)} %get-tuple-element.139.refs_0_, f32[2048,384]{1,0:T(8,128)S(1)} %get-tuple-element.140.refs_1_, bf16[384,1280]{1,0:T(8,128)(2,1)S(1)} %get-tuple-element.141.refs_2_, ...), custom_call_target="tpu_custom_call" | custom-call | flops 1409286144 | tf_op jit(solution)/shard_map/pallas_call | solution.py:666
  162.5 2.9 %shard_map.144.own_ref = bf16[512,1280]{1,0:T(8,128)(2,1)S(1)} custom-call(s32[2]{0:T(128)S(1)} %get-tuple-element.150.order_ref, f32[2048,384]{1,0:T(8,128)S(1)} %get-tuple-element.139.refs_0_, f32[2048,384]{1,0:T(8,128)S(1)} %get-tuple-element.140.refs_1_, bf16[384,1280]{1,0:T(8,128)(2,1)S(1)} %get-tuple-element.141.refs_2_, ...), custom_call_target="tpu_custom_call" | custom-call | flops 1409286144 | tf_op jit(solution)/shard_map/pallas_call | solution.py:666
  165.4 3.6 %collective-permute-done.33.refs_0_ = bf16[128,1280]{1,0:T(8,128)(2,1)S(1)} collective-permute-done((bf16[128,1280]{1,0:T(8,128)(2,1)S(1)}, bf16[128,1280]{1,0:T(8,128)(2,1)S(1)}, u32[]{:S(2)}, u32[]{:S(2)}) %collective-permute-start.33) | collective-permute-done | bytes 327712 | tf_op jit(solution)/shard_map/ppermute | solution.py:724
  173.5 2.5 %collective-permute-done.32.refs_0_ = bf16[128,1280]{1,0:T(8,128)(2,1)S(1)} collective-permute-done((bf16[128,1280]{1,0:T(8,128)(2,1)S(1)}, bf16[128,1280]{1,0:T(8,128)(2,1)S(1)}, u32[]{:S(2)}, u32[]{:S(2)}) %collective-permute-start.32) | collective-permute-done | bytes 327712 | tf_op jit(solution)/shard_map/ppermute | solution.py:724
  176.2 6.1 %collective-permute-done.35.refs_1_ = bf16[128,1280]{1,0:T(8,128)(2,1)S(1)} collective-permute-done((bf16[128,1280]{1,0:T(8,128)(2,1)S(1)}, bf16[128,1280]{1,0:T(8,128)(2,1)S(1)}, u32[]{:S(2)}, u32[]{:S(2)}) %collective-permute-start.35) | collective-permute-done | bytes 327712 | tf_op jit(solution)/shard_map/ppermute | solution.py:724
  187.3 6.6 %collective-permute-done.38.refs_2_ = bf16[128,1280]{1,0:T(8,128)(2,1)S(1)} collective-permute-done((bf16[128,1280]{1,0:T(8,128)(2,1)S(1)}, bf16[128,1280]{1,0:T(8,128)(2,1)S(1)}, u32[]{:S(2)}, u32[]{:S(2)}) %collective-permute-start.38) | collective-permute-done | bytes 327712 | tf_op jit(solution)/shard_map/ppermute | solution.py:724
  197.1 3.8 %collective-permute-done.44.refs_3_ = bf16[128,1280]{1,0:T(8,128)(2,1)S(1)} collective-permute-done((bf16[128,1280]{1,0:T(8,128)(2,1)S(1)}, bf16[128,1280]{1,0:T(8,128)(2,1)S(1)}, u32[]{:S(2)}, u32[]{:S(2)}) %collective-permute-start.44) | collective-permute-done | bytes 327712 | tf_op jit(solution)/shard_map/ppermute | solution.py:724
  202.4 4.9 %collective-permute-done.39.refs_0_ = bf16[128,1280]{1,0:T(8,128)(2,1)S(1)} collective-permute-done((bf16[128,1280]{1,0:T(8,128)(2,1)S(1)}, bf16[128,1280]{1,0:T(8,128)(2,1)S(1)}, u32[]{:S(2)}, u32[]{:S(2)}) %collective-permute-start.39) | collective-permute-done | bytes 327712 | tf_op jit(solution)/shard_map/ppermute | solution.py:724
  209.9 2.6 %shard_map.147.refs_4_ = bf16[2000,1280]{1,0:T(8,128)(2,1)} custom-call(s32[12]{0:T(128)S(1)} %stack.122.offsets_ref, bf16[128,1280]{1,0:T(8,128)(2,1)S(1)} %get-tuple-element.157.refs_0_, bf16[128,1280]{1,0:T(8,128)(2,1)S(1)} %get-tuple-element.158.refs_1_, bf16[128,1280]{1,0:T(8,128)(2,1)S(1)} %collective-permute-done.38.refs_2_, ...), custom_call_target="tpu_custom_call" | custom-call | tf_op jit(solution)/shard_map/pallas_call | solution.py:713
  (185 shorter events, 73.5 us)
Async XLA Ops:
  6.9 18.9 %collective-permute-start.1 = (bf16[1280,128]{1,0:T(8,128)(2,1)}, bf16[1280,128]{1,0:T(8,128)(2,1)S(1)}, u32[]{:S(2)}, u32[]{:S(2)}) collective-permute-start(bf16[1280,128]{1,0:T(8,128)(2,1)} %get-tuple-element.86), channel_id=1, source_target_pairs={{0,16},{16,0},{1,17},{17,1},{2,18},{18,2},{3,19},{19,3},{4,20},{20... | collective-permute-start | bytes 983048 | tf_op jit(solution)/shard_map/ppermute | solution.py:724
  7.1 18.7 %collective-permute-start.2 = (bf16[128,1280]{1,0:T(8,128)(2,1)}, bf16[128,1280]{1,0:T(8,128)(2,1)}, u32[]{:S(2)}, u32[]{:S(2)}) collective-permute-start(bf16[128,1280]{1,0:T(8,128)(2,1)} %get-tuple-element.87), channel_id=1, source_target_pairs={{0,16},{16,0},{1,17},{17,1},{2,18},{18,2},{3,19},{19,3},{4,20},{20... | collective-permute-start | bytes 983048 | tf_op jit(solution)/shard_map/ppermute | solution.py:724
  14.2 11.5 %collective-permute-start.4 = (bf16[56,1280]{1,0:T(8,128)(2,1)}, bf16[56,1280]{1,0:T(8,128)(2,1)}, u32[]{:S(2)}, u32[]{:S(2)}) collective-permute-start(bf16[56,1280]{1,0:T(8,128)(2,1)} %get-tuple-element.89), channel_id=1, source_target_pairs={{0,8},{4,12},{8,0},{12,4},{1,9},{5,13},{9,1},{13,5},{2,10},{6,14},... | collective-permute-start | bytes 430088 | tf_op jit(solution)/shard_map/ppermute | solution.py:729
  32.2 15.4 %collective-permute-start.10 = (bf16[56,1280]{1,0:T(8,128)(2,1)S(1)}, bf16[56,1280]{1,0:T(8,128)(2,1)S(1)}, u32[]{:S(2)}, u32[]{:S(2)}) collective-permute-start(bf16[56,1280]{1,0:T(8,128)(2,1)S(1)} %get-tuple-element.106), channel_id=1, source_target_pairs={{0,8},{4,12},{8,0},{12,4},{1,9},{5,13},{9,1},{13,5},{2,10},{6,14},... | collective-permute-start | bytes 430088 | tf_op jit(solution)/shard_map/ppermute | solution.py:729
  37.1 10.5 %collective-permute-start.11 = (bf16[56,1280]{1,0:T(8,128)(2,1)S(1)}, bf16[56,1280]{1,0:T(8,128)(2,1)S(1)}, u32[]{:S(2)}, u32[]{:S(2)}) collective-permute-start(bf16[56,1280]{1,0:T(8,128)(2,1)S(1)} %get-tuple-element.107), channel_id=1, source_target_pairs={{0,4},{4,8},{8,12},{12,0},{1,5},{5,9},{9,13},{13,1},{2,6},{6,10},{... | collective-permute-start | bytes 430088 | tf_op jit(solution)/shard_map/ppermute | solution.py:729
  51.2 13.8 %collective-permute-start.12 = (bf16[56,1280]{1,0:T(8,128)(2,1)}, bf16[56,1280]{1,0:T(8,128)(2,1)}, u32[]{:S(2)}, u32[]{:S(2)}) collective-permute-start(bf16[56,1280]{1,0:T(8,128)(2,1)} %get-tuple-element.113), channel_id=1, source_target_pairs={{0,4},{4,8},{8,12},{12,0},{1,5},{5,9},{9,13},{13,1},{2,6},{6,10},{... | collective-permute-start | bytes 430088 | tf_op jit(solution)/shard_map/ppermute | solution.py:729
  53.5 11.4 %collective-permute-start.13 = (bf16[56,1280]{1,0:T(8,128)(2,1)}, bf16[56,1280]{1,0:T(8,128)(2,1)}, u32[]{:S(2)}, u32[]{:S(2)}) collective-permute-start(bf16[56,1280]{1,0:T(8,128)(2,1)} %get-tuple-element.114), channel_id=1, source_target_pairs={{0,8},{4,12},{8,0},{12,4},{1,9},{5,13},{9,1},{13,5},{2,10},{6,14},... | collective-permute-start | bytes 430088 | tf_op jit(solution)/shard_map/ppermute | solution.py:729
  73.5 11.2 %collective-permute-start.16 = (bf16[56,1280]{1,0:T(8,128)(2,1)S(1)}, bf16[56,1280]{1,0:T(8,128)(2,1)S(1)}, u32[]{:S(2)}, u32[]{:S(2)}) collective-permute-start(bf16[56,1280]{1,0:T(8,128)(2,1)S(1)} %get-tuple-element.123), channel_id=1, source_target_pairs={{0,8},{4,12},{8,0},{12,4},{1,9},{5,13},{9,1},{13,5},{2,10},{6,14},... | collective-permute-start | bytes 430088 | tf_op jit(solution)/shard_map/ppermute | solution.py:729
  73.5 11.2 %collective-permute-start.17 = (bf16[56,1280]{1,0:T(8,128)(2,1)S(1)}, bf16[56,1280]{1,0:T(8,128)(2,1)S(1)}, u32[]{:S(2)}, u32[]{:S(2)}) collective-permute-start(bf16[56,1280]{1,0:T(8,128)(2,1)S(1)} %get-tuple-element.124), channel_id=1, source_target_pairs={{0,4},{4,8},{8,12},{12,0},{1,5},{5,9},{9,13},{13,1},{2,6},{6,10},{... | collective-permute-start | bytes 430088 | tf_op jit(solution)/shard_map/ppermute | solution.py:729
  85.7 14.0 %collective-permute-start.18 = (bf16[192,1280]{1,0:T(8,128)(2,1)S(1)}, bf16[192,1280]{1,0:T(8,128)(2,1)S(1)}, u32[]{:S(2)}, u32[]{:S(2)}) collective-permute-start(bf16[192,1280]{1,0:T(8,128)(2,1)S(1)} %shard_map.137.refs_0_), channel_id=1, source_target_pairs={{4,0},{8,4},{12,8},{5,1},{9,5},{13,9},{6,2},{10,6},{14,10},{7,3},{... | collective-permute-start | bytes 1474568 | tf_op jit(solution)/shard_map/ppermute | solution.py:737
  87.0 14.0 %collective-permute-start.20 = (bf16[192,1280]{1,0:T(8,128)(2,1)S(1)}, bf16[192,1280]{1,0:T(8,128)(2,1)S(1)}, u32[]{:S(2)}, u32[]{:S(2)}) collective-permute-start(bf16[192,1280]{1,0:T(8,128)(2,1)S(1)} %shard_map.137.refs_0_), channel_id=1, source_target_pairs={{0,4},{4,8},{8,12},{1,5},{5,9},{9,13},{2,6},{6,10},{10,14},{3,7},{... | collective-permute-start | bytes 1474568 | tf_op jit(solution)/shard_map/ppermute | solution.py:738
  99.7 13.6 %collective-permute-start.19 = (bf16[192,1280]{1,0:T(8,128)(2,1)S(1)}, bf16[192,1280]{1,0:T(8,128)(2,1)S(1)}, u32[]{:S(2)}, u32[]{:S(2)}) collective-permute-start(bf16[192,1280]{1,0:T(8,128)(2,1)S(1)} %collective-permute-done.18.refs_1_.refs_4_), channel_id=1, source_target_pairs={{4,0},{8,4},{5,1},{9,5},{6,2},{10,6},{7,3},{11,7},{20,16},{24,20},... | collective-permute-start | bytes 1474568 | tf_op jit(solution)/shard_map/ppermute | solution.py:744
  101.0 12.3 %collective-permute-start.21 = (bf16[192,1280]{1,0:T(8,128)(2,1)S(1)}, bf16[192,1280]{1,0:T(8,128)(2,1)S(1)}, u32[]{:S(2)}, u32[]{:S(2)}) collective-permute-start(bf16[192,1280]{1,0:T(8,128)(2,1)S(1)} %collective-permute-done.20.refs_2_.refs_5_), channel_id=1, source_target_pairs={{4,8},{8,12},{5,9},{9,13},{6,10},{10,14},{7,11},{11,15},{20,24},{2... | collective-permute-start | bytes 1474568 | tf_op jit(solution)/shard_map/ppermute | solution.py:745
  113.4 14.6 %collective-permute-start.25 = (bf16[192,1280]{1,0:T(8,128)(2,1)S(1)}, bf16[192,1280]{1,0:T(8,128)(2,1)S(1)}, u32[]{:S(2)}, u32[]{:S(2)}) collective-permute-start(bf16[192,1280]{1,0:T(8,128)(2,1)S(1)} %collective-permute-done.19.refs_0_), channel_id=1, source_target_pairs={{4,0},{5,1},{6,2},{7,3},{20,16},{21,17},{22,18},{23,19}} | collective-permute-start | bytes 1474568 | tf_op jit(solution)/shard_map/ppermute | solution.py:751
  114.7 13.3 %collective-permute-start.26 = (bf16[192,1280]{1,0:T(8,128)(2,1)S(1)}, bf16[192,1280]{1,0:T(8,128)(2,1)S(1)}, u32[]{:S(2)}, u32[]{:S(2)}) collective-permute-start(bf16[192,1280]{1,0:T(8,128)(2,1)S(1)} %collective-permute-done.21.refs_1_), channel_id=1, source_target_pairs={{8,12},{9,13},{10,14},{11,15},{24,28},{25,29},{26,30},{27,31}} | collective-permute-start | bytes 1474568 | tf_op jit(solution)/shard_map/ppermute | solution.py:752
  115.4 21.3 %collective-permute-start.22 = (f32[2,16,192]{2,1,0:T(8,128)S(1)}, f32[2,16,192]{2,1,0:T(8,128)S(1)}, u32[]{:S(2)}, u32[]{:S(2)}) collective-permute-start(f32[2,16,192]{2,1,0:T(8,128)S(1)} %get-tuple-element.129.refs_0_), channel_id=1, source_target_pairs={{0,12},{4,0},{8,4},{12,8},{1,13},{5,1},{9,5},{13,9},{2,14},{6,2},{... | collective-permute-start | bytes 73736 | tf_op jit(solution)/shard_map/ppermute | solution.py:729
  120.9 16.4 %collective-permute-start.23 = (f32[2,16,192]{2,1,0:T(8,128)S(1)}, f32[2,16,192]{2,1,0:T(8,128)S(1)}, u32[]{:S(2)}, u32[]{:S(2)}) collective-permute-start(f32[2,16,192]{2,1,0:T(8,128)S(1)} %get-tuple-element.129.refs_0_), channel_id=1, source_target_pairs={{0,8},{4,12},{8,0},{12,4},{1,9},{5,13},{9,1},{13,5},{2,10},{6,14},... | collective-permute-start | bytes 73736 | tf_op jit(solution)/shard_map/ppermute | solution.py:729
  122.2 15.1 %collective-permute-start.24 = (f32[2,16,192]{2,1,0:T(8,128)S(1)}, f32[2,16,192]{2,1,0:T(8,128)S(1)}, u32[]{:S(2)}, u32[]{:S(2)}) collective-permute-start(f32[2,16,192]{2,1,0:T(8,128)S(1)} %get-tuple-element.129.refs_0_), channel_id=1, source_target_pairs={{0,4},{4,8},{8,12},{12,0},{1,5},{5,9},{9,13},{13,1},{2,6},{6,10},{... | collective-permute-start | bytes 73736 | tf_op jit(solution)/shard_map/ppermute | solution.py:729
  154.2 11.2 %collective-permute-start.31 = (bf16[512,1280]{1,0:T(8,128)(2,1)S(1)}, bf16[512,1280]{1,0:T(8,128)(2,1)S(1)}, u32[]{:S(2)}, u32[]{:S(2)}) collective-permute-start(bf16[512,1280]{1,0:T(8,128)(2,1)S(1)} %get-tuple-element.151), channel_id=1, source_target_pairs={{0,1},{1,0},{2,3},{3,2},{4,5},{5,4},{6,7},{7,6},{8,9},{9,8},{10,11... | collective-permute-start | bytes 3932168 | tf_op jit(solution)/shard_map/ppermute | solution.py:724
  158.4 10.6 %collective-permute-start.33 = (bf16[128,1280]{1,0:T(8,128)(2,1)S(1)}, bf16[128,1280]{1,0:T(8,128)(2,1)S(1)}, u32[]{:S(2)}, u32[]{:S(2)}) collective-permute-start(bf16[128,1280]{1,0:T(8,128)(2,1)S(1)} %get-tuple-element.149), channel_id=1, source_target_pairs={{0,16},{16,0},{1,17},{17,1},{2,18},{18,2},{3,19},{19,3},{4,20},{20... | collective-permute-start | bytes 983048 | tf_op jit(solution)/shard_map/ppermute | solution.py:724
  158.6 10.6 %collective-permute-start.34 = (bf16[128,1280]{1,0:T(8,128)(2,1)S(1)}, bf16[128,1280]{1,0:T(8,128)(2,1)S(1)}, u32[]{:S(2)}, u32[]{:S(2)}) collective-permute-start(bf16[128,1280]{1,0:T(8,128)(2,1)S(1)} %get-tuple-element.153), channel_id=1, source_target_pairs={{0,2},{2,0},{1,3},{3,1},{4,6},{6,4},{5,7},{7,5},{8,10},{10,8},{9,1... | collective-permute-start | bytes 983048 | tf_op jit(solution)/shard_map/ppermute | solution.py:724
  160.2 15.9 %collective-permute-start.32 = (bf16[128,1280]{1,0:T(8,128)(2,1)S(1)}, bf16[128,1280]{1,0:T(8,128)(2,1)S(1)}, u32[]{:S(2)}, u32[]{:S(2)}) collective-permute-start(bf16[128,1280]{1,0:T(8,128)(2,1)S(1)} %get-tuple-element.152), channel_id=1, source_target_pairs={{0,16},{16,0},{1,17},{17,1},{2,18},{18,2},{3,19},{19,3},{4,20},{20... | collective-permute-start | bytes 983048 | tf_op jit(solution)/shard_map/ppermute | solution.py:724
  162.1 14.2 %collective-permute-start.36 = (bf16[128,1280]{1,0:T(8,128)(2,1)S(1)}, bf16[128,1280]{1,0:T(8,128)(2,1)S(1)}, u32[]{:S(2)}, u32[]{:S(2)}) collective-permute-start(bf16[128,1280]{1,0:T(8,128)(2,1)S(1)} %get-tuple-element.155), channel_id=1, source_target_pairs={{0,2},{2,0},{1,3},{3,1},{4,6},{6,4},{5,7},{7,5},{8,10},{10,8},{9,1... | collective-permute-start | bytes 983048 | tf_op jit(solution)/shard_map/ppermute | solution.py:724
  170.0 12.3 %collective-permute-start.35 = (bf16[128,1280]{1,0:T(8,128)(2,1)S(1)}, bf16[128,1280]{1,0:T(8,128)(2,1)S(1)}, u32[]{:S(2)}, u32[]{:S(2)}) collective-permute-start(bf16[128,1280]{1,0:T(8,128)(2,1)S(1)} %get-tuple-element.154), channel_id=1, source_target_pairs={{0,2},{2,0},{1,3},{3,1},{4,6},{6,4},{5,7},{7,5},{8,10},{10,8},{9,1... | collective-permute-start | bytes 983048 | tf_op jit(solution)/shard_map/ppermute | solution.py:724
  171.6 10.7 %collective-permute-start.37 = (bf16[128,1280]{1,0:T(8,128)(2,1)S(1)}, bf16[128,1280]{1,0:T(8,128)(2,1)S(1)}, u32[]{:S(2)}, u32[]{:S(2)}) collective-permute-start(bf16[128,1280]{1,0:T(8,128)(2,1)S(1)} %get-tuple-element.156), channel_id=1, source_target_pairs={{0,16},{16,0},{1,17},{17,1},{2,18},{18,2},{3,19},{19,3},{4,20},{20... | collective-permute-start | bytes 983048 | tf_op jit(solution)/shard_map/ppermute | solution.py:724
  183.2 10.7 %collective-permute-start.38 = (bf16[128,1280]{1,0:T(8,128)(2,1)S(1)}, bf16[128,1280]{1,0:T(8,128)(2,1)S(1)}, u32[]{:S(2)}, u32[]{:S(2)}) collective-permute-start(bf16[128,1280]{1,0:T(8,128)(2,1)S(1)} %get-tuple-element.157.refs_0_), channel_id=1, source_target_pairs={{0,2},{2,0},{1,3},{3,1},{4,6},{6,4},{5,7},{7,5},{8,10},{10,8},{9,1... | collective-permute-start | bytes 983048 | tf_op jit(solution)/shard_map/ppermute | solution.py:724
  184.8 10.8 %collective-permute-start.40 = (bf16[128,1280]{1,0:T(8,128)(2,1)S(1)}, bf16[128,1280]{1,0:T(8,128)(2,1)S(1)}, u32[]{:S(2)}, u32[]{:S(2)}) collective-permute-start(bf16[128,1280]{1,0:T(8,128)(2,1)S(1)} %get-tuple-element.158.refs_1_), channel_id=1, source_target_pairs={{0,16},{16,0},{1,17},{17,1},{2,18},{18,2},{3,19},{19,3},{4,20},{20... | collective-permute-start | bytes 983048 | tf_op jit(solution)/shard_map/ppermute | solution.py:724
  186.4 14.5 %collective-permute-start.44 = (bf16[128,1280]{1,0:T(8,128)(2,1)S(1)}, bf16[128,1280]{1,0:T(8,128)(2,1)S(1)}, u32[]{:S(2)}, u32[]{:S(2)}) collective-permute-start(bf16[128,1280]{1,0:T(8,128)(2,1)S(1)} %get-tuple-element.158.refs_1_), channel_id=1, source_target_pairs={{0,2},{2,0},{1,3},{3,1},{4,6},{6,4},{5,7},{7,5},{8,10},{10,8},{9,1... | collective-permute-start | bytes 983048 | tf_op jit(solution)/shard_map/ppermute | solution.py:724
  186.9 15.5 %collective-permute-start.45 = (bf16[128,1280]{1,0:T(8,128)(2,1)S(1)}, bf16[128,1280]{1,0:T(8,128)(2,1)S(1)}, u32[]{:S(2)}, u32[]{:S(2)}) collective-permute-start(bf16[128,1280]{1,0:T(8,128)(2,1)S(1)} %get-tuple-element.157.refs_0_), channel_id=1, source_target_pairs={{0,16},{16,0},{1,17},{17,1},{2,18},{18,2},{3,19},{19,3},{4,20},{20... | collective-permute-start | bytes 983048 | tf_op jit(solution)/shard_map/ppermute | solution.py:724
  193.9 13.4 %collective-permute-start.39 = (bf16[128,1280]{1,0:T(8,128)(2,1)S(1)}, bf16[128,1280]{1,0:T(8,128)(2,1)S(1)}, u32[]{:S(2)}, u32[]{:S(2)}) collective-permute-start(bf16[128,1280]{1,0:T(8,128)(2,1)S(1)} %collective-permute-done.38.refs_2_), channel_id=1, source_target_pairs={{0,16},{16,0},{1,17},{17,1},{2,18},{18,2},{3,19},{19,3},{4,20},{20... | collective-permute-start | bytes 983048 | tf_op jit(solution)/shard_map/ppermute | solution.py:724
  195.6 11.8 %collective-permute-start.41 = (bf16[128,1280]{1,0:T(8,128)(2,1)S(1)}, bf16[128,1280]{1,0:T(8,128)(2,1)S(1)}, u32[]{:S(2)}, u32[]{:S(2)}) collective-permute-start(bf16[128,1280]{1,0:T(8,128)(2,1)S(1)} %collective-permute-done.40.refs_5_), channel_id=1, source_target_pairs={{0,2},{2,0},{1,3},{3,1},{4,6},{6,4},{5,7},{7,5},{8,10},{10,8},{9,1... | collective-permute-start | bytes 983048 | tf_op jit(solution)/shard_map/ppermute | solution.py:724
  197.1 10.7 %collective-permute-start.46 = (bf16[128,1280]{1,0:T(8,128)(2,1)S(1)}, bf16[128,1280]{1,0:T(8,128)(2,1)S(1)}, u32[]{:S(2)}, u32[]{:S(2)}) collective-permute-start(bf16[128,1280]{1,0:T(8,128)(2,1)S(1)} %get-tuple-element.157.refs_0_), channel_id=1, source_target_pairs={{0,1},{1,0},{2,3},{3,2},{4,5},{5,4},{6,7},{7,6},{8,9},{9,8},{10,11... | collective-permute-start | bytes 983048 | tf_op jit(solution)/shard_map/ppermute | solution.py:724
  (52 other events, 285.1 us)

commit v2 on v1

--- a/solution.py
+++ b/solution.py
@@ -79,8 +79,7 @@
 
 def placement(column, member, experts, capacity):
     count = column.shape[0]
-    shifted = column - member
-    relative = jnp.where(shifted < 0, shifted + experts, shifted)
+    relative = column ^ member
     lane = lax.broadcasted_iota(jnp.int32, (count, LANES), 1)
     one_hot = (lane == relative).astype(jnp.float32)
     before = lax.broadcasted_iota(jnp.int32, (count, count), 1) <= lax.broadcasted_iota(
@@ -304,12 +303,12 @@
             row = ref[...].astype(jnp.float32)[spare : spare + 1]
             found.append((row[:, :LANES] * LANES + row[:, LANES : 2 * LANES]).astype(jnp.int32))
         if line:
-            low = place < 2
+            ends = (place == 0) | (place == 3)
             found = [
                 found[0],
-                jnp.where(low, found[1], found[3]),
-                found[2],
-                jnp.where(low, found[3], found[1]),
+                found[1],
+                jnp.where(ends, found[2], found[3]),
+                jnp.where(ends, found[3], found[2]),
             ]
         names_ref[...] = jnp.zeros(names_ref.shape, jnp.int32)
         for slot in range(sources):
@@ -432,21 +431,13 @@
     )(member, weight, label_weight, *pieces)
 
 
-def fill_near(place, piece_refs, put, put_if):
-    value_ref, left_ref, right_ref = piece_refs
-    put(0, value_ref)
-    put_if(place < 2, 1, left_ref)
-    put_if(place >= 2, 1, right_ref)
-
-
 def fill_far(place, piece_refs, put, put_if):
-    left_far, right_far, left_end, right_end, left_ref, right_ref = piece_refs
-    put_if(place < 2, 0, left_far)
-    put_if(place >= 2, 0, right_far)
-    put_if(place == 0, 1, left_end)
-    put_if(place == 3, 1, right_end)
-    put_if(place == 1, 1, right_ref)
-    put_if(place == 2, 1, left_ref)
+    middle, outward, far, last = piece_refs
+    ends = (place == 0) | (place == 3)
+    put_if(ends, 0, outward)
+    put_if(ends, 1, last)
+    put_if((place == 1) | (place == 2), 0, middle)
+    put_if((place == 1) | (place == 2), 1, far)
 
 
 def fill_all(place, piece_refs, put, put_if):
@@ -724,36 +715,18 @@
     return lax.ppermute(value, axis, [(0, 1), (1, 0)])
 
 
-def rotate(value, axis, by):
+def crossed(value, axis, by):
     count = lax.axis_size(axis)
-    return lax.ppermute(value, axis, [(i, (i + by) % count) for i in range(count)])
+    return lax.ppermute(value, axis, [(i, i ^ by) for i in range(count)])
 
 
 def after(value, *others):
     return lax.optimization_barrier((value,) + others)[0]
 
 
-def line_near(value):
-    left = lax.ppermute(value, "expert", [(1, 0), (2, 1), (3, 2)])
-    right = lax.ppermute(value, "expert", [(0, 1), (1, 2), (2, 3)])
-    return left, right
-
-
-def line_far(left, right):
-    return (
-        lax.ppermute(left, "expert", [(1, 0), (2, 1)]),
-        lax.ppermute(right, "expert", [(1, 2), (2, 3)]),
-    )
-
-
-def line_end(left_far, right_far):
-    return (
-        lax.ppermute(left_far, "expert", [(1, 0)]),
-        lax.ppermute(right_far, "expert", [(2, 3)]),
-    )
-
-
-LINE_ORDER = np.array([[0, 1, 2, 3], [1, 2, 3, 0], [2, 1, 0, 3], [3, 2, 1, 0]])
+LINE_ORDER = np.array([[0, 1, 2, 3], [1, 0, 2, 3], [2, 3, 1, 0], [3, 2, 1, 0]])
+MIDDLE = [(1, 2), (2, 1)]
+OUTWARD = [(1, 0), (2, 3)]
 
 
 def slot_orders(count):
@@ -765,7 +738,7 @@
     tables = np.zeros((count, count, count), np.int32)
     for member in range(count):
         for k in range(count):
-            source = (member + k) % count
+            source = member ^ k
             for slot in range(count):
                 tables[member, k, slot] = list(orders[source]).index(orders[member][slot])
     return tables.reshape(count, count * count)
@@ -862,10 +835,8 @@
     def mine_of(value):
         return lax.dynamic_slice_in_dim(value, first_pair, per_section, 0)
 
-    def exchange(blocks, sign):
-        return [blocks[0]] + [
-            rotate(blocks[k], "expert", sign * k) for k in range(1, group_size)
-        ]
+    def exchange(blocks):
+        return [blocks[0]] + [crossed(blocks[k], "expert", k) for k in range(1, group_size)]
 
     def lanes_of(ids):
         return jnp.pad(mine_of(ids), ((0, 0), (0, LANES - frame_count)), constant_values=-1)
@@ -908,7 +879,7 @@
             layers.append(((all_tables[layer],), chosen, [], jnp.ones((1,), jnp.int32)))
 
     outgoing = dispatch(current, layer_ids[0], member_ref, experts, capacity, frame_count)
-    received = exchange(outgoing, 1)
+    received = exchange(outgoing)
     if paired:
         (came_in, came_out), received = lax.optimization_barrier(((came_in, came_out), received))
         other = [(came_in, came_out), (swap(came_in, "dpi"), swap(came_out, "dpi"))]
@@ -985,13 +956,13 @@
         choices, weights, others, pick_own = layers[layer]
         note = notes if layer == 0 else None
         done = run_expert(received, choices, weights, others, pick_own, filled, note)
-        returned = exchange(done, -1)
+        returned = exchange(done)
         if layer == 0:
             found = returned
             if not line:
                 stacked = jnp.stack(returned)
                 found = [
-                    lax.dynamic_index_in_dim(stacked, (k - member) % group_size, 0, keepdims=False)
+                    lax.dynamic_index_in_dim(stacked, member ^ k, 0, keepdims=False)
                     for k in range(group_size)
                 ]
         if layer < sections - 1:
@@ -1007,7 +978,7 @@
                 capacity,
                 frame_count,
             )
-            received = exchange(outgoing, 1)
+            received = exchange(outgoing)
             if layer == 0:
                 found = [after(found[0], current)] + list(found[1:])
                 label_weight, places, names = label_rows(
@@ -1033,17 +1004,22 @@
             fill, first, count, pieces, member_ref, weight_rows, label_weight, frame_count
         )
 
+    def stats_of(stats):
+        first = crossed(stats, "expert", 1)
+        return [stats, first, crossed(stats, "expert", 2), crossed(first, "expert", 2)]
+
     if line:
-        left, right = line_near(normed)
-        far = line_far(left, right)
-        heads = [logits_of(fill_near, 0, 2, [normed, left, right])]
-        far, heads[0] = lax.optimization_barrier((far, heads[0]))
-        end = line_end(*far)
-        heads.append(logits_of(fill_far, 2, 2, [*far, *end, left, right]))
-        found = [
-            [head[2]] + [rotate(head[2], "expert", -k) for k in range(1, group_size)]
-            for head in heads
-        ]
+        beside = crossed(normed, "expert", 1)
+        middle = lax.ppermute(normed, "expert", MIDDLE)
+        far = lax.ppermute(beside, "expert", MIDDLE)
+        outward = lax.ppermute(middle, "expert", OUTWARD)
+        heads = [logits_of(fill_all, 0, 2, [normed, beside])]
+        held, heads[0] = lax.optimization_barrier((far, heads[0]))
+        last = lax.ppermute(held, "expert", OUTWARD)
+        found = [stats_of(heads[0][2])]
+        middle, found[0] = lax.optimization_barrier((middle, found[0]))
+        heads.append(logits_of(fill_far, 2, 2, [middle, outward, held, last]))
+        found.append(stats_of(heads[1][2]))
     else:
         gathered = lax.all_gather(normed, "expert")
         pieces = [gathered[k] for k in range(group_size)]
@@ -1051,7 +1027,7 @@
         gathered = lax.all_gather(heads[0][2], "expert")
         found = [
             [
-                lax.dynamic_index_in_dim(gathered, (member + k) % group_size, 0, keepdims=False)
+                lax.dynamic_index_in_dim(gathered, member ^ k, 0, keepdims=False)
                 for k in range(group_size)
             ]
         ]

time: 215 us -> 216 us (level)
  waiting for transfers between devices: 78.9 us -> 95.6 us
  starting transfers between devices: 74.8 us -> 60.1 us
    ppermute x24 -> x23, waiting for transfers between devices: 46.2 us -> 63 us  [the longest x19 63 us: crossed(): return lax.ppermute(value, axis, [(i, i ^ by) for i in range(count)])]
    ppermute x24 -> x23, starting transfers between devices: 52.2 us -> 37.8 us  [the longest x19 33.6 us: crossed(): return lax.ppermute(value, axis, [(i, i ^ by) for i in range(count)])]
  transfers between devices with their start and end apart: 52 -> 51, of which waited for: 26 -> 26; matrix products, arithmetic and copies ran while one was open for 1% -> 1% of each run, Pallas kernels for 10% -> 8%
where the time goes in v2:
time: 216 us
  waiting for transfers between devices  95.6 us (44%)
  starting transfers between devices  60.1 us (28%)
  Pallas kernels  42.5 us (20%)
  local copies, waits for them, and re-layouts  16 us (7%)
    ppermute x19, waiting for transfers between devices, crossed(): return lax.ppermute(value, axis, [(i, i ^ by) for i in range(count)])  63 us
    ppermute x19, starting transfers between devices, crossed(): return lax.ppermute(value, axis, [(i, i ^ by) for i in range(count)])  33.6 us
    ppermute x28, waiting for transfers between devices, swap(): return lax.ppermute(value, axis, [(0, 1), (1, 0)])  32.5 us
    ppermute x28, starting transfers between devices, swap(): return lax.ppermute(value, axis, [(0, 1), (1, 0)])  22.3 us
    unnamed x64, local copies, waits for them, and re-layouts  14.6 us
    pallas_call x3, Pallas kernels, head_gradient(): call(kernel, tuple((bf16_rows(each * BLOCK_ROWS, width) for _ in range(ou...  10.6 us
    pallas_call x1, Pallas kernels, ctc_pass(): call(kernel, (jax.ShapeDtypeStruct((COLS, row_count), jnp.float32), bf16_...  6.83 us
    pallas_call x2, Pallas kernels, head_logits(): call(kernel, (jax.ShapeDtypeStruct((height, row_count), jnp.float32), bf1...  6.46 us
  transfers between devices with their start and end apart: 51, of which 26 were waited for; matrix products, arithmetic and copies ran while one was open for 1% of the time, Pallas kernels for 8%

profile of v2, /device:TPU:0, one launch (start us, length us, event | category | flops | bytes accessed | tf_op | source)
XLA Modules:
  0.0 215.9 jit_solution(614516992435044821)
XLA Ops:
  0.7 3.0 %collective-permute-start = (s32[8,48]{1,0:T(8,128)}, s32[8,48]{1,0:T(8,128)S(1)}, u32[]{:S(2)}, u32[]{:S(2)}) collective-permute-start(s32[8,48]{1,0:T(8,128)} %bitcast.56), channel_id=1, source_target_pairs={{0,16},{16,0},{1,17},{17,1},{2,18},{18,2},{3,19},{19,3},{4,20},{20... | collective-permute-start | bytes 4616 | tf_op jit(solution)/shard_map/ppermute | solution.py:715
  14.3 2.6 %collective-permute-start.4 = (bf16[56,1280]{1,0:T(8,128)(2,1)}, bf16[56,1280]{1,0:T(8,128)(2,1)}, u32[]{:S(2)}, u32[]{:S(2)}) collective-permute-start(bf16[56,1280]{1,0:T(8,128)(2,1)} %get-tuple-element.93), channel_id=1, source_target_pairs={{0,8},{4,12},{8,0},{12,4},{1,9},{5,13},{9,1},{13,5},{2,10},{6,14},... | collective-permute-start | bytes 430088 | tf_op jit(solution)/shard_map/ppermute | solution.py:720
  20.4 7.2 %collective-permute-done.4.refs_8_ = bf16[56,1280]{1,0:T(8,128)(2,1)} collective-permute-done((bf16[56,1280]{1,0:T(8,128)(2,1)}, bf16[56,1280]{1,0:T(8,128)(2,1)}, u32[]{:S(2)}, u32[]{:S(2)}) %collective-permute-start.4) | collective-permute-done | bytes 143392 | tf_op jit(solution)/shard_map/ppermute | solution.py:720
  34.0 3.1 %collective-permute-start.10 = (bf16[56,1280]{1,0:T(8,128)(2,1)S(1)}, bf16[56,1280]{1,0:T(8,128)(2,1)S(1)}, u32[]{:S(2)}, u32[]{:S(2)}) collective-permute-start(bf16[56,1280]{1,0:T(8,128)(2,1)S(1)} %get-tuple-element.110), channel_id=1, source_target_pairs={{0,8},{4,12},{8,0},{12,4},{1,9},{5,13},{9,1},{13,5},{2,10},{6,14},... | collective-permute-start | bytes 430088 | tf_op jit(solution)/shard_map/ppermute | solution.py:720
  38.4 9.4 %collective-permute-done.10.refs_4_.refs_2_ = bf16[56,1280]{1,0:T(8,128)(2,1)S(1)} collective-permute-done((bf16[56,1280]{1,0:T(8,128)(2,1)S(1)}, bf16[56,1280]{1,0:T(8,128)(2,1)S(1)}, u32[]{:S(2)}, u32[]{:S(2)}) %collective-permute-start.10) | collective-permute-done | bytes 143392 | tf_op jit(solution)/shard_map/ppermute | solution.py:720
  52.2 2.3 %collective-permute-start.12 = (bf16[56,1280]{1,0:T(8,128)(2,1)}, bf16[56,1280]{1,0:T(8,128)(2,1)}, u32[]{:S(2)}, u32[]{:S(2)}) collective-permute-start(bf16[56,1280]{1,0:T(8,128)(2,1)} %get-tuple-element.117), channel_id=1, source_target_pairs={{0,4},{4,0},{8,12},{12,8},{1,5},{5,1},{9,13},{13,9},{2,6},{6,2},{1... | collective-permute-start | bytes 430088 | tf_op jit(solution)/shard_map/ppermute | solution.py:720
  56.9 2.4 %copy-done.1 = bf16[1280,2000]{0,1:T(8,128)(2,1)S(1)} copy-done((bf16[1280,2000]{0,1:T(8,128)(2,1)S(1)}, bf16[1280,2000]{0,1:T(8,128)(2,1)}, u32[]{:S(2)}) %copy-start.1) | copy-done | bytes 5120024
  64.0 4.0 %collective-permute-done.13.refs_8_ = bf16[56,1280]{1,0:T(8,128)(2,1)} collective-permute-done((bf16[56,1280]{1,0:T(8,128)(2,1)}, bf16[56,1280]{1,0:T(8,128)(2,1)}, u32[]{:S(2)}, u32[]{:S(2)}) %collective-permute-start.13) | collective-permute-done | bytes 143392 | tf_op jit(solution)/shard_map/ppermute | solution.py:720
  68.0 2.3 %shard_map.136 = (bf16[56,1280]{1,0:T(8,128)(2,1)S(1)}, bf16[56,1280]{1,0:T(8,128)(2,1)S(1)}, bf16[56,1280]{1,0:T(8,128)(2,1)S(1)}, bf16[56,1280]{1,0:T(8,128)(2,1)S(1)}) custom-call(s32[1]{0:T(128)} %bitcast.38.pick_ref, bf16[1280,256]{1,0:T(8,128)(2,1)S(1)} %bitcast.51, bf16[256,1280]{1,0:T(8,128)(2,1)S(1)} %bitcast.54, ...), custom_call_target="tpu_custom_call" | custom-call | flops 293601280 | tf_op jit(solution)/shard_map/pallas_call | solution.py:188
  70.4 2.6 %collective-permute-start.15 = (bf16[56,1280]{1,0:T(8,128)(2,1)S(1)}, bf16[56,1280]{1,0:T(8,128)(2,1)S(1)}, u32[]{:S(2)}, u32[]{:S(2)}) collective-permute-start(bf16[56,1280]{1,0:T(8,128)(2,1)S(1)} %get-tuple-element.126), channel_id=1, source_target_pairs={{0,4},{4,0},{8,12},{12,8},{1,5},{5,1},{9,13},{13,9},{2,6},{6,2},{1... | collective-permute-start | bytes 430088 | tf_op jit(solution)/shard_map/ppermute | solution.py:720
  77.2 7.8 %collective-permute-done.16.refs_4_ = bf16[56,1280]{1,0:T(8,128)(2,1)S(1)} collective-permute-done((bf16[56,1280]{1,0:T(8,128)(2,1)S(1)}, bf16[56,1280]{1,0:T(8,128)(2,1)S(1)}, u32[]{:S(2)}, u32[]{:S(2)}) %collective-permute-start.16) | collective-permute-done | bytes 143392 | tf_op jit(solution)/shard_map/ppermute | solution.py:720
  85.9 3.1 %collective-permute-start.19 = (bf16[192,1280]{1,0:T(8,128)(2,1)S(1)}, bf16[192,1280]{1,0:T(8,128)(2,1)S(1)}, u32[]{:S(2)}, u32[]{:S(2)}) collective-permute-start(bf16[192,1280]{1,0:T(8,128)(2,1)S(1)} %shard_map.137.refs_0_), channel_id=1, source_target_pairs={{0,4},{4,0},{8,12},{12,8},{1,5},{5,1},{9,13},{13,9},{2,6},{6,2},{1... | collective-permute-start | bytes 1474568 | tf_op jit(solution)/shard_map/ppermute | solution.py:720
  89.7 10.2 %collective-permute-done.19.refs_1_ = bf16[192,1280]{1,0:T(8,128)(2,1)S(1)} collective-permute-done((bf16[192,1280]{1,0:T(8,128)(2,1)S(1)}, bf16[192,1280]{1,0:T(8,128)(2,1)S(1)}, u32[]{:S(2)}, u32[]{:S(2)}) %collective-permute-start.19) | collective-permute-done | bytes 491552 | tf_op jit(solution)/shard_map/ppermute | solution.py:720
  102.2 2.4 %copy-done.2 = bf16[1280,2000]{0,1:T(8,128)(2,1)S(1)} copy-done((bf16[1280,2000]{0,1:T(8,128)(2,1)S(1)}, bf16[1280,2000]{0,1:T(8,128)(2,1)}, u32[]{:S(2)}) %copy-start.2) | copy-done | bytes 5120024
  104.6 3.2 %shard_map.138 = (f32[2048,384]{1,0:T(8,128)S(1)}, bf16[384,1280]{1,0:T(8,128)(2,1)S(1)}, f32[2,16,192]{2,1,0:T(8,128)S(1)}) custom-call(s32[1]{0:T(128)} %bitcast.member_ref, bf16[2000,1280]{1,0:T(8,128)(2,1)S(1)} %bitcast.47, bf16[256,1280]{1,0:T(8,128)(2,1)S(1)} %get-tuple-element.129.label_ref, bf16[192,1280]{1,0:T(8,128)(2,1)S(1)} %shard_map.137.refs_0_, ...), custom_call_target="tpu_custom_call" | custom-call | flops 2013265920 | tf_op jit(solution)/shard_map/pallas_call | solution.py:420
  109.1 7.6 %collective-permute-start.21 = (f32[2,16,192]{2,1,0:T(8,128)S(1)}, f32[2,16,192]{2,1,0:T(8,128)S(1)}, u32[]{:S(2)}, u32[]{:S(2)}) collective-permute-start(f32[2,16,192]{2,1,0:T(8,128)S(1)} %get-tuple-element.134.refs_0_), channel_id=1, source_target_pairs={{0,4},{4,0},{8,12},{12,8},{1,5},{5,1},{9,13},{13,9},{2,6},{6,2},{1... | collective-permute-start | bytes 73736 | tf_op jit(solution)/shard_map/ppermute | solution.py:720
  116.7 10.4 %collective-permute-done.21.refs_1_ = f32[2,16,192]{2,1,0:T(8,128)S(1)} collective-permute-done((f32[2,16,192]{2,1,0:T(8,128)S(1)}, f32[2,16,192]{2,1,0:T(8,128)S(1)}, u32[]{:S(2)}, u32[]{:S(2)}) %collective-permute-start.21) | collective-permute-done | bytes 24608 | tf_op jit(solution)/shard_map/ppermute | solution.py:720
  127.6 4.3 %collective-permute-done.23.refs_3_ = f32[2,16,192]{2,1,0:T(8,128)S(1)} collective-permute-done((f32[2,16,192]{2,1,0:T(8,128)S(1)}, f32[2,16,192]{2,1,0:T(8,128)S(1)}, u32[]{:S(2)}, u32[]{:S(2)}) %collective-permute-start.23) | collective-permute-done | bytes 24608 | tf_op jit(solution)/shard_map/ppermute | solution.py:720
  131.9 3.3 %shard_map.139 = (f32[2048,384]{1,0:T(8,128)S(1)}, bf16[384,1280]{1,0:T(8,128)(2,1)S(1)}, f32[2,16,192]{2,1,0:T(8,128)S(1)}) custom-call(s32[1]{0:T(128)} %bitcast.member_ref, bf16[2000,1280]{1,0:T(8,128)(2,1)S(1)} %bitcast.48, bf16[256,1280]{1,0:T(8,128)(2,1)S(1)} %get-tuple-element.129.label_ref, bf16[192,1280]{1,0:T(8,128)(2,1)S(1)} %collective-permute-done.18.refs_0_, ...), custom_call_target="tpu_custom_call" | custom-call | flops 2013265920 | tf_op jit(solution)/shard_map/pallas_call | solution.py:420
  135.2 2.9 %collective-permute-start.27 = (f32[2,16,192]{2,1,0:T(8,128)S(1)}, f32[2,16,192]{2,1,0:T(8,128)S(1)}, u32[]{:S(2)}, u32[]{:S(2)}) collective-permute-start(f32[2,16,192]{2,1,0:T(8,128)S(1)} %get-tuple-element.140.refs_4_), channel_id=1, source_target_pairs={{0,8},{4,12},{8,0},{12,4},{1,9},{5,13},{9,1},{13,5},{2,10},{6,14},... | collective-permute-start | bytes 73736 | tf_op jit(solution)/shard_map/ppermute | solution.py:720
  140.0 4.0 %collective-permute-done.28.refs_7_ = f32[2,16,192]{2,1,0:T(8,128)S(1)} collective-permute-done((f32[2,16,192]{2,1,0:T(8,128)S(1)}, f32[2,16,192]{2,1,0:T(8,128)S(1)}, u32[]{:S(2)}, u32[]{:S(2)}) %collective-permute-start.28) | collective-permute-done | bytes 24608 | tf_op jit(solution)/shard_map/ppermute | solution.py:720
  144.1 6.8 %shard_map.140 = (f32[16,768]{1,0:T(8,128)S(1)}, bf16[256,768]{1,0:T(8,128)(2,1)S(1)}, bf16[256,768]{1,0:T(8,128)(2,1)S(1)}, f32[1,4]{1,0:T(1,128)}) custom-call(s32[16]{0:T(128)S(1)} %fusion.slots_ref, s32[16,128]{1,0:T(8,128)S(1)} %get-tuple-element.114.notes_ref, f32[2,16,192]{2,1,0:T(8,128)S(1)} %get-tuple-element.134.refs_0_, ...), custom_call_target="tpu_custom_call" | custom-call | flops 67108864 | tf_op jit(solution)/shard_map/pallas_call | solution.py:606
  150.9 4.9 %shard_map.141 = (bf16[512,1280]{1,0:T(8,128)(2,1)S(1)}, bf16[512,1280]{1,0:T(8,128)(2,1)S(1)}) custom-call(s32[4]{0:T(128)S(1)} %get-tuple-element.146.order_ref, f32[2048,384]{1,0:T(8,128)S(1)} %get-tuple-element.147.refs_0_, f32[2048,384]{1,0:T(8,128)S(1)} %get-tuple-element.148.refs_1_, bf16[384,1280]{1,0:T(8,128)(2,1)S(1)} %get-tuple-element.149.refs_2_, ...), custom_call_target="tpu_custom_call" | custom-call | flops 2818572288 | tf_op jit(solution)/shard_map/pallas_call | solution.py:657
  156.4 2.8 %shard_map.142.own_ref = bf16[512,1280]{1,0:T(8,128)(2,1)S(1)} custom-call(s32[2]{0:T(128)S(1)} %get-tuple-element.156.order_ref, f32[2048,384]{1,0:T(8,128)S(1)} %get-tuple-element.147.refs_0_, f32[2048,384]{1,0:T(8,128)S(1)} %get-tuple-element.148.refs_1_, bf16[384,1280]{1,0:T(8,128)(2,1)S(1)} %get-tuple-element.149.refs_2_, ...), custom_call_target="tpu_custom_call" | custom-call | flops 1409286144 | tf_op jit(solution)/shard_map/pallas_call | solution.py:657
  164.2 2.8 %shard_map.144.own_ref = bf16[512,1280]{1,0:T(8,128)(2,1)S(1)} custom-call(s32[2]{0:T(128)S(1)} %get-tuple-element.158.order_ref, f32[2048,384]{1,0:T(8,128)S(1)} %get-tuple-element.147.refs_0_, f32[2048,384]{1,0:T(8,128)S(1)} %get-tuple-element.148.refs_1_, bf16[384,1280]{1,0:T(8,128)(2,1)S(1)} %get-tuple-element.149.refs_2_, ...), custom_call_target="tpu_custom_call" | custom-call | flops 1409286144 | tf_op jit(solution)/shard_map/pallas_call | solution.py:657
  167.1 3.7 %collective-permute-done.32.refs_0_ = bf16[128,1280]{1,0:T(8,128)(2,1)S(1)} collective-permute-done((bf16[128,1280]{1,0:T(8,128)(2,1)S(1)}, bf16[128,1280]{1,0:T(8,128)(2,1)S(1)}, u32[]{:S(2)}, u32[]{:S(2)}) %collective-permute-start.32) | collective-permute-done | bytes 327712 | tf_op jit(solution)/shard_map/ppermute | solution.py:715
  175.2 2.6 %collective-permute-done.31.refs_0_ = bf16[128,1280]{1,0:T(8,128)(2,1)S(1)} collective-permute-done((bf16[128,1280]{1,0:T(8,128)(2,1)S(1)}, bf16[128,1280]{1,0:T(8,128)(2,1)S(1)}, u32[]{:S(2)}, u32[]{:S(2)}) %collective-permute-start.31) | collective-permute-done | bytes 327712 | tf_op jit(solution)/shard_map/ppermute | solution.py:715
  177.9 6.1 %collective-permute-done.34.refs_1_ = bf16[128,1280]{1,0:T(8,128)(2,1)S(1)} collective-permute-done((bf16[128,1280]{1,0:T(8,128)(2,1)S(1)}, bf16[128,1280]{1,0:T(8,128)(2,1)S(1)}, u32[]{:S(2)}, u32[]{:S(2)}) %collective-permute-start.34) | collective-permute-done | bytes 327712 | tf_op jit(solution)/shard_map/ppermute | solution.py:715
  189.0 6.6 %collective-permute-done.37.refs_2_ = bf16[128,1280]{1,0:T(8,128)(2,1)S(1)} collective-permute-done((bf16[128,1280]{1,0:T(8,128)(2,1)S(1)}, bf16[128,1280]{1,0:T(8,128)(2,1)S(1)}, u32[]{:S(2)}, u32[]{:S(2)}) %collective-permute-start.37) | collective-permute-done | bytes 327712 | tf_op jit(solution)/shard_map/ppermute | solution.py:715
  198.8 3.8 %collective-permute-done.43.refs_3_ = bf16[128,1280]{1,0:T(8,128)(2,1)S(1)} collective-permute-done((bf16[128,1280]{1,0:T(8,128)(2,1)S(1)}, bf16[128,1280]{1,0:T(8,128)(2,1)S(1)}, u32[]{:S(2)}, u32[]{:S(2)}) %collective-permute-start.43) | collective-permute-done | bytes 327712 | tf_op jit(solution)/shard_map/ppermute | solution.py:715
  204.3 4.7 %collective-permute-done.38.refs_0_ = bf16[128,1280]{1,0:T(8,128)(2,1)S(1)} collective-permute-done((bf16[128,1280]{1,0:T(8,128)(2,1)S(1)}, bf16[128,1280]{1,0:T(8,128)(2,1)S(1)}, u32[]{:S(2)}, u32[]{:S(2)}) %collective-permute-start.38) | collective-permute-done | bytes 327712 | tf_op jit(solution)/shard_map/ppermute | solution.py:715
  211.5 2.6 %shard_map.147.refs_4_ = bf16[2000,1280]{1,0:T(8,128)(2,1)} custom-call(s32[12]{0:T(128)S(1)} %stack.122.offsets_ref, bf16[128,1280]{1,0:T(8,128)(2,1)S(1)} %get-tuple-element.165.refs_0_, bf16[128,1280]{1,0:T(8,128)(2,1)S(1)} %get-tuple-element.166.refs_1_, bf16[128,1280]{1,0:T(8,128)(2,1)S(1)} %collective-permute-done.37.refs_2_, ...), custom_call_target="tpu_custom_call" | custom-call | tf_op jit(solution)/shard_map/pallas_call | solution.py:704
  (183 shorter events, 68.9 us)
Async XLA Ops:
  6.9 20.7 %collective-permute-start.1 = (bf16[1280,128]{1,0:T(8,128)(2,1)}, bf16[1280,128]{1,0:T(8,128)(2,1)S(1)}, u32[]{:S(2)}, u32[]{:S(2)}) collective-permute-start(bf16[1280,128]{1,0:T(8,128)(2,1)} %get-tuple-element.90), channel_id=1, source_target_pairs={{0,16},{16,0},{1,17},{17,1},{2,18},{18,2},{3,19},{19,3},{4,20},{20... | collective-permute-start | bytes 983048 | tf_op jit(solution)/shard_map/ppermute | solution.py:715
  7.1 20.5 %collective-permute-start.2 = (bf16[128,1280]{1,0:T(8,128)(2,1)}, bf16[128,1280]{1,0:T(8,128)(2,1)}, u32[]{:S(2)}, u32[]{:S(2)}) collective-permute-start(bf16[128,1280]{1,0:T(8,128)(2,1)} %get-tuple-element.91), channel_id=1, source_target_pairs={{0,16},{16,0},{1,17},{17,1},{2,18},{18,2},{3,19},{19,3},{4,20},{20... | collective-permute-start | bytes 983048 | tf_op jit(solution)/shard_map/ppermute | solution.py:715
  14.3 13.3 %collective-permute-start.4 = (bf16[56,1280]{1,0:T(8,128)(2,1)}, bf16[56,1280]{1,0:T(8,128)(2,1)}, u32[]{:S(2)}, u32[]{:S(2)}) collective-permute-start(bf16[56,1280]{1,0:T(8,128)(2,1)} %get-tuple-element.93), channel_id=1, source_target_pairs={{0,8},{4,12},{8,0},{12,4},{1,9},{5,13},{9,1},{13,5},{2,10},{6,14},... | collective-permute-start | bytes 430088 | tf_op jit(solution)/shard_map/ppermute | solution.py:720
  16.9 10.7 %collective-permute-start.5 = (bf16[56,1280]{1,0:T(8,128)(2,1)}, bf16[56,1280]{1,0:T(8,128)(2,1)}, u32[]{:S(2)}, u32[]{:S(2)}) collective-permute-start(bf16[56,1280]{1,0:T(8,128)(2,1)} %get-tuple-element.94), channel_id=1, source_target_pairs={{0,12},{4,8},{8,4},{12,0},{1,13},{5,9},{9,5},{13,1},{2,14},{6,10},... | collective-permute-start | bytes 430088 | tf_op jit(solution)/shard_map/ppermute | solution.py:720
  34.0 13.8 %collective-permute-start.10 = (bf16[56,1280]{1,0:T(8,128)(2,1)S(1)}, bf16[56,1280]{1,0:T(8,128)(2,1)S(1)}, u32[]{:S(2)}, u32[]{:S(2)}) collective-permute-start(bf16[56,1280]{1,0:T(8,128)(2,1)S(1)} %get-tuple-element.110), channel_id=1, source_target_pairs={{0,8},{4,12},{8,0},{12,4},{1,9},{5,13},{9,1},{13,5},{2,10},{6,14},... | collective-permute-start | bytes 430088 | tf_op jit(solution)/shard_map/ppermute | solution.py:720
  37.1 10.7 %collective-permute-start.11 = (bf16[56,1280]{1,0:T(8,128)(2,1)S(1)}, bf16[56,1280]{1,0:T(8,128)(2,1)S(1)}, u32[]{:S(2)}, u32[]{:S(2)}) collective-permute-start(bf16[56,1280]{1,0:T(8,128)(2,1)S(1)} %get-tuple-element.111), channel_id=1, source_target_pairs={{0,12},{4,8},{8,4},{12,0},{1,13},{5,9},{9,5},{13,1},{2,14},{6,10},... | collective-permute-start | bytes 430088 | tf_op jit(solution)/shard_map/ppermute | solution.py:720
  38.4 10.2 %collective-permute-start.9 = (bf16[56,1280]{1,0:T(8,128)(2,1)S(1)}, bf16[56,1280]{1,0:T(8,128)(2,1)S(1)}, u32[]{:S(2)}, u32[]{:S(2)}) collective-permute-start(bf16[56,1280]{1,0:T(8,128)(2,1)S(1)} %get-tuple-element.109), channel_id=1, source_target_pairs={{0,4},{4,0},{8,12},{12,8},{1,5},{5,1},{9,13},{13,9},{2,6},{6,2},{1... | collective-permute-start | bytes 430088 | tf_op jit(solution)/shard_map/ppermute | solution.py:720
  52.2 11.8 %collective-permute-start.12 = (bf16[56,1280]{1,0:T(8,128)(2,1)}, bf16[56,1280]{1,0:T(8,128)(2,1)}, u32[]{:S(2)}, u32[]{:S(2)}) collective-permute-start(bf16[56,1280]{1,0:T(8,128)(2,1)} %get-tuple-element.117), channel_id=1, source_target_pairs={{0,4},{4,0},{8,12},{12,8},{1,5},{5,1},{9,13},{13,9},{2,6},{6,2},{1... | collective-permute-start | bytes 430088 | tf_op jit(solution)/shard_map/ppermute | solution.py:720
  54.5 13.5 %collective-permute-start.13 = (bf16[56,1280]{1,0:T(8,128)(2,1)}, bf16[56,1280]{1,0:T(8,128)(2,1)}, u32[]{:S(2)}, u32[]{:S(2)}) collective-permute-start(bf16[56,1280]{1,0:T(8,128)(2,1)} %get-tuple-element.118), channel_id=1, source_target_pairs={{0,8},{4,12},{8,0},{12,4},{1,9},{5,13},{9,1},{13,5},{2,10},{6,14},... | collective-permute-start | bytes 430088 | tf_op jit(solution)/shard_map/ppermute | solution.py:720
  55.2 12.8 %collective-permute-start.14 = (bf16[56,1280]{1,0:T(8,128)(2,1)}, bf16[56,1280]{1,0:T(8,128)(2,1)}, u32[]{:S(2)}, u32[]{:S(2)}) collective-permute-start(bf16[56,1280]{1,0:T(8,128)(2,1)} %get-tuple-element.119), channel_id=1, source_target_pairs={{0,12},{4,8},{8,4},{12,0},{1,13},{5,9},{9,5},{13,1},{2,14},{6,10},... | collective-permute-start | bytes 430088 | tf_op jit(solution)/shard_map/ppermute | solution.py:720
  72.9 12.0 %collective-permute-start.16 = (bf16[56,1280]{1,0:T(8,128)(2,1)S(1)}, bf16[56,1280]{1,0:T(8,128)(2,1)S(1)}, u32[]{:S(2)}, u32[]{:S(2)}) collective-permute-start(bf16[56,1280]{1,0:T(8,128)(2,1)S(1)} %get-tuple-element.127), channel_id=1, source_target_pairs={{0,8},{4,12},{8,0},{12,4},{1,9},{5,13},{9,1},{13,5},{2,10},{6,14},... | collective-permute-start | bytes 430088 | tf_op jit(solution)/shard_map/ppermute | solution.py:720
  73.4 11.6 %collective-permute-start.17 = (bf16[56,1280]{1,0:T(8,128)(2,1)S(1)}, bf16[56,1280]{1,0:T(8,128)(2,1)S(1)}, u32[]{:S(2)}, u32[]{:S(2)}) collective-permute-start(bf16[56,1280]{1,0:T(8,128)(2,1)S(1)} %get-tuple-element.128), channel_id=1, source_target_pairs={{0,12},{4,8},{8,4},{12,0},{1,13},{5,9},{9,5},{13,1},{2,14},{6,10},... | collective-permute-start | bytes 430088 | tf_op jit(solution)/shard_map/ppermute | solution.py:720
  85.9 14.0 %collective-permute-start.19 = (bf16[192,1280]{1,0:T(8,128)(2,1)S(1)}, bf16[192,1280]{1,0:T(8,128)(2,1)S(1)}, u32[]{:S(2)}, u32[]{:S(2)}) collective-permute-start(bf16[192,1280]{1,0:T(8,128)(2,1)S(1)} %shard_map.137.refs_0_), channel_id=1, source_target_pairs={{0,4},{4,0},{8,12},{12,8},{1,5},{5,1},{9,13},{13,9},{2,6},{6,2},{1... | collective-permute-start | bytes 1474568 | tf_op jit(solution)/shard_map/ppermute | solution.py:720
  89.1 11.6 %collective-permute-start.18 = (bf16[192,1280]{1,0:T(8,128)(2,1)S(1)}, bf16[192,1280]{1,0:T(8,128)(2,1)S(1)}, u32[]{:S(2)}, u32[]{:S(2)}) collective-permute-start(bf16[192,1280]{1,0:T(8,128)(2,1)S(1)} %shard_map.137.refs_0_), channel_id=1, source_target_pairs={{4,8},{8,4},{5,9},{9,5},{6,10},{10,6},{7,11},{11,7},{20,24},{24,20... | collective-permute-start | bytes 1474568 | tf_op jit(solution)/shard_map/ppermute | solution.py:1013
  100.7 31.2 %collective-permute-start.24 = (bf16[192,1280]{1,0:T(8,128)(2,1)S(1)}, bf16[192,1280]{1,0:T(8,128)(2,1)S(1)}, u32[]{:S(2)}, u32[]{:S(2)}) collective-permute-start(bf16[192,1280]{1,0:T(8,128)(2,1)S(1)} %collective-permute-done.18.refs_0_), channel_id=1, source_target_pairs={{4,0},{8,12},{5,1},{9,13},{6,2},{10,14},{7,3},{11,15},{20,16},{24,... | collective-permute-start | bytes 1474568 | tf_op jit(solution)/shard_map/ppermute | solution.py:1015
  107.8 24.1 %collective-permute-start.25 = (bf16[192,1280]{1,0:T(8,128)(2,1)S(1)}, bf16[192,1280]{1,0:T(8,128)(2,1)S(1)}, u32[]{:S(2)}, u32[]{:S(2)}) collective-permute-start(bf16[192,1280]{1,0:T(8,128)(2,1)S(1)} %collective-permute-done.20.refs_2_), channel_id=1, source_target_pairs={{4,0},{8,12},{5,1},{9,13},{6,2},{10,14},{7,3},{11,15},{20,16},{24,... | collective-permute-start | bytes 1474568 | tf_op jit(solution)/shard_map/ppermute | solution.py:1018
  109.1 18.0 %collective-permute-start.21 = (f32[2,16,192]{2,1,0:T(8,128)S(1)}, f32[2,16,192]{2,1,0:T(8,128)S(1)}, u32[]{:S(2)}, u32[]{:S(2)}) collective-permute-start(f32[2,16,192]{2,1,0:T(8,128)S(1)} %get-tuple-element.134.refs_0_), channel_id=1, source_target_pairs={{0,4},{4,0},{8,12},{12,8},{1,5},{5,1},{9,13},{13,9},{2,6},{6,2},{1... | collective-permute-start | bytes 73736 | tf_op jit(solution)/shard_map/ppermute | solution.py:720
  116.7 10.9 %collective-permute-start.22 = (f32[2,16,192]{2,1,0:T(8,128)S(1)}, f32[2,16,192]{2,1,0:T(8,128)S(1)}, u32[]{:S(2)}, u32[]{:S(2)}) collective-permute-start(f32[2,16,192]{2,1,0:T(8,128)S(1)} %get-tuple-element.134.refs_0_), channel_id=1, source_target_pairs={{0,8},{4,12},{8,0},{12,4},{1,9},{5,13},{9,1},{13,5},{2,10},{6,14},... | collective-permute-start | bytes 73736 | tf_op jit(solution)/shard_map/ppermute | solution.py:720
  155.9 11.2 %collective-permute-start.30 = (bf16[512,1280]{1,0:T(8,128)(2,1)S(1)}, bf16[512,1280]{1,0:T(8,128)(2,1)S(1)}, u32[]{:S(2)}, u32[]{:S(2)}) collective-permute-start(bf16[512,1280]{1,0:T(8,128)(2,1)S(1)} %get-tuple-element.159), channel_id=1, source_target_pairs={{0,1},{1,0},{2,3},{3,2},{4,5},{5,4},{6,7},{7,6},{8,9},{9,8},{10,11... | collective-permute-start | bytes 3932168 | tf_op jit(solution)/shard_map/ppermute | solution.py:715
  160.1 10.6 %collective-permute-start.32 = (bf16[128,1280]{1,0:T(8,128)(2,1)S(1)}, bf16[128,1280]{1,0:T(8,128)(2,1)S(1)}, u32[]{:S(2)}, u32[]{:S(2)}) collective-permute-start(bf16[128,1280]{1,0:T(8,128)(2,1)S(1)} %get-tuple-element.157), channel_id=1, source_target_pairs={{0,16},{16,0},{1,17},{17,1},{2,18},{18,2},{3,19},{19,3},{4,20},{20... | collective-permute-start | bytes 983048 | tf_op jit(solution)/shard_map/ppermute | solution.py:715
  160.2 10.6 %collective-permute-start.33 = (bf16[128,1280]{1,0:T(8,128)(2,1)S(1)}, bf16[128,1280]{1,0:T(8,128)(2,1)S(1)}, u32[]{:S(2)}, u32[]{:S(2)}) collective-permute-start(bf16[128,1280]{1,0:T(8,128)(2,1)S(1)} %get-tuple-element.161), channel_id=1, source_target_pairs={{0,2},{2,0},{1,3},{3,1},{4,6},{6,4},{5,7},{7,5},{8,10},{10,8},{9,1... | collective-permute-start | bytes 983048 | tf_op jit(solution)/shard_map/ppermute | solution.py:715
  162.2 15.6 %collective-permute-start.31 = (bf16[128,1280]{1,0:T(8,128)(2,1)S(1)}, bf16[128,1280]{1,0:T(8,128)(2,1)S(1)}, u32[]{:S(2)}, u32[]{:S(2)}) collective-permute-start(bf16[128,1280]{1,0:T(8,128)(2,1)S(1)} %get-tuple-element.160), channel_id=1, source_target_pairs={{0,16},{16,0},{1,17},{17,1},{2,18},{18,2},{3,19},{19,3},{4,20},{20... | collective-permute-start | bytes 983048 | tf_op jit(solution)/shard_map/ppermute | solution.py:715
  163.8 14.1 %collective-permute-start.35 = (bf16[128,1280]{1,0:T(8,128)(2,1)S(1)}, bf16[128,1280]{1,0:T(8,128)(2,1)S(1)}, u32[]{:S(2)}, u32[]{:S(2)}) collective-permute-start(bf16[128,1280]{1,0:T(8,128)(2,1)S(1)} %get-tuple-element.163), channel_id=1, source_target_pairs={{0,2},{2,0},{1,3},{3,1},{4,6},{6,4},{5,7},{7,5},{8,10},{10,8},{9,1... | collective-permute-start | bytes 983048 | tf_op jit(solution)/shard_map/ppermute | solution.py:715
  171.6 12.4 %collective-permute-start.34 = (bf16[128,1280]{1,0:T(8,128)(2,1)S(1)}, bf16[128,1280]{1,0:T(8,128)(2,1)S(1)}, u32[]{:S(2)}, u32[]{:S(2)}) collective-permute-start(bf16[128,1280]{1,0:T(8,128)(2,1)S(1)} %get-tuple-element.162), channel_id=1, source_target_pairs={{0,2},{2,0},{1,3},{3,1},{4,6},{6,4},{5,7},{7,5},{8,10},{10,8},{9,1... | collective-permute-start | bytes 983048 | tf_op jit(solution)/shard_map/ppermute | solution.py:715
  173.7 10.4 %collective-permute-start.36 = (bf16[128,1280]{1,0:T(8,128)(2,1)S(1)}, bf16[128,1280]{1,0:T(8,128)(2,1)S(1)}, u32[]{:S(2)}, u32[]{:S(2)}) collective-permute-start(bf16[128,1280]{1,0:T(8,128)(2,1)S(1)} %get-tuple-element.164), channel_id=1, source_target_pairs={{0,16},{16,0},{1,17},{17,1},{2,18},{18,2},{3,19},{19,3},{4,20},{20... | collective-permute-start | bytes 983048 | tf_op jit(solution)/shard_map/ppermute | solution.py:715
  184.9 10.7 %collective-permute-start.37 = (bf16[128,1280]{1,0:T(8,128)(2,1)S(1)}, bf16[128,1280]{1,0:T(8,128)(2,1)S(1)}, u32[]{:S(2)}, u32[]{:S(2)}) collective-permute-start(bf16[128,1280]{1,0:T(8,128)(2,1)S(1)} %get-tuple-element.165.refs_0_), channel_id=1, source_target_pairs={{0,2},{2,0},{1,3},{3,1},{4,6},{6,4},{5,7},{7,5},{8,10},{10,8},{9,1... | collective-permute-start | bytes 983048 | tf_op jit(solution)/shard_map/ppermute | solution.py:715
  186.6 10.7 %collective-permute-start.39 = (bf16[128,1280]{1,0:T(8,128)(2,1)S(1)}, bf16[128,1280]{1,0:T(8,128)(2,1)S(1)}, u32[]{:S(2)}, u32[]{:S(2)}) collective-permute-start(bf16[128,1280]{1,0:T(8,128)(2,1)S(1)} %get-tuple-element.166.refs_1_), channel_id=1, source_target_pairs={{0,16},{16,0},{1,17},{17,1},{2,18},{18,2},{3,19},{19,3},{4,20},{20... | collective-permute-start | bytes 983048 | tf_op jit(solution)/shard_map/ppermute | solution.py:715
  188.1 14.5 %collective-permute-start.43 = (bf16[128,1280]{1,0:T(8,128)(2,1)S(1)}, bf16[128,1280]{1,0:T(8,128)(2,1)S(1)}, u32[]{:S(2)}, u32[]{:S(2)}) collective-permute-start(bf16[128,1280]{1,0:T(8,128)(2,1)S(1)} %get-tuple-element.166.refs_1_), channel_id=1, source_target_pairs={{0,2},{2,0},{1,3},{3,1},{4,6},{6,4},{5,7},{7,5},{8,10},{10,8},{9,1... | collective-permute-start | bytes 983048 | tf_op jit(solution)/shard_map/ppermute | solution.py:715
  188.6 15.6 %collective-permute-start.44 = (bf16[128,1280]{1,0:T(8,128)(2,1)S(1)}, bf16[128,1280]{1,0:T(8,128)(2,1)S(1)}, u32[]{:S(2)}, u32[]{:S(2)}) collective-permute-start(bf16[128,1280]{1,0:T(8,128)(2,1)S(1)} %get-tuple-element.165.refs_0_), channel_id=1, source_target_pairs={{0,16},{16,0},{1,17},{17,1},{2,18},{18,2},{3,19},{19,3},{4,20},{20... | collective-permute-start | bytes 983048 | tf_op jit(solution)/shard_map/ppermute | solution.py:715
  195.6 13.4 %collective-permute-start.38 = (bf16[128,1280]{1,0:T(8,128)(2,1)S(1)}, bf16[128,1280]{1,0:T(8,128)(2,1)S(1)}, u32[]{:S(2)}, u32[]{:S(2)}) collective-permute-start(bf16[128,1280]{1,0:T(8,128)(2,1)S(1)} %collective-permute-done.37.refs_2_), channel_id=1, source_target_pairs={{0,16},{16,0},{1,17},{17,1},{2,18},{18,2},{3,19},{19,3},{4,20},{20... | collective-permute-start | bytes 983048 | tf_op jit(solution)/shard_map/ppermute | solution.py:715
  197.3 11.7 %collective-permute-start.40 = (bf16[128,1280]{1,0:T(8,128)(2,1)S(1)}, bf16[128,1280]{1,0:T(8,128)(2,1)S(1)}, u32[]{:S(2)}, u32[]{:S(2)}) collective-permute-start(bf16[128,1280]{1,0:T(8,128)(2,1)S(1)} %collective-permute-done.39.refs_5_), channel_id=1, source_target_pairs={{0,2},{2,0},{1,3},{3,1},{4,6},{6,4},{5,7},{7,5},{8,10},{10,8},{9,1... | collective-permute-start | bytes 983048 | tf_op jit(solution)/shard_map/ppermute | solution.py:715
  198.8 10.7 %collective-permute-start.45 = (bf16[128,1280]{1,0:T(8,128)(2,1)S(1)}, bf16[128,1280]{1,0:T(8,128)(2,1)S(1)}, u32[]{:S(2)}, u32[]{:S(2)}) collective-permute-start(bf16[128,1280]{1,0:T(8,128)(2,1)S(1)} %get-tuple-element.165.refs_0_), channel_id=1, source_target_pairs={{0,1},{1,0},{2,3},{3,2},{4,5},{5,4},{6,7},{7,6},{8,9},{9,8},{10,11... | collective-permute-start | bytes 983048 | tf_op jit(solution)/shard_map/ppermute | solution.py:715
  (51 other events, 273.7 us)

commit v3 on v2

--- a/solution.py
+++ b/solution.py
@@ -360,7 +360,7 @@
 
 
 def head_logits(
-    fill, first_slot, count, pieces, member, weight, label_weight, frame_count
+    fill, first_slot, count, pieces, member, weight, label_weight, frame_count, earlier=None
 ):
     given = len(pieces)
     span, width = pieces[0].shape
@@ -369,10 +369,12 @@
     height = round_up(shard, BLOCK_ROWS)
     entries = row_count // frame_count * COLS
     first_entry = first_slot * entries // count
+    others = [] if earlier is None else [earlier]
+    ahead = 0 if earlier is None else earlier.shape[0]
 
     def kernel(member_ref, weight_ref, label_ref, *refs):
         piece_refs = refs[:given]
-        logits_ref, rows_ref, stats_ref = refs[given:]
+        logits_ref, rows_ref, stats_ref = refs[given + len(others) :]
 
         def put(slot, piece_ref):
             rows_ref[slot * span : (slot + 1) * span] = piece_ref[...]
@@ -414,21 +416,23 @@
         place = lax.broadcasted_iota(jnp.int32, (COLS, row_count), 0)
         stats = jnp.where(place == PEAK, peak, picked)
         stats = jnp.where(place == TOTAL, total, stats)
+        for slot in range(ahead):
+            stats_ref[slot] = refs[given][slot]
         for slot in range(count):
-            stats_ref[slot] = stats[:, slot * span : (slot + 1) * span]
+            stats_ref[ahead + slot] = stats[:, slot * span : (slot + 1) * span]
 
     return call(
         kernel,
         (
             jax.ShapeDtypeStruct((height, row_count), jnp.float32),
             bf16_rows(row_count, width),
-            jax.ShapeDtypeStruct((count, COLS, span), jnp.float32),
+            jax.ShapeDtypeStruct((ahead + count, COLS, span), jnp.float32),
         ),
         2 * height * row_count * width,
         LARGE_LIMIT,
-        in_specs=[smem_spec()] + [vmem_spec()] * (2 + given),
+        in_specs=[smem_spec()] + [vmem_spec()] * (2 + given + len(others)),
         out_specs=tuple(vmem_spec() for _ in range(3)),
-    )(member, weight, label_weight, *pieces)
+    )(member, weight, label_weight, *pieces, *others)
 
 
 def fill_far(place, piece_refs, put, put_if):
@@ -867,9 +871,6 @@
     layers = []
     if paired:
         other_table = swap(own_table, "section")
-        sent_in, sent_out = half_weights(core.astype(jnp.int32).reshape(1), *own)
-        came_in = swap(sent_in, "section")
-        came_out = swap(sent_out, "section")
     else:
         all_tables = lax.all_gather(own_table, "section")
         all_in = lax.all_gather(own[0], "section")
@@ -881,7 +882,12 @@
     outgoing = dispatch(current, layer_ids[0], member_ref, experts, capacity, frame_count)
     received = exchange(outgoing)
     if paired:
-        (came_in, came_out), received = lax.optimization_barrier(((came_in, came_out), received))
+        sent_in, sent_out = half_weights(
+            after(core.astype(jnp.int32).reshape(1), outgoing[0]), *own
+        )
+        came_in = swap(sent_in, "section")
+        came_out = swap(sent_out, "section")
+        came_in, came_out = lax.optimization_barrier((came_in, came_out, received))[:2]
         other = [(came_in, came_out), (swap(came_in, "dpi"), swap(came_out, "dpi"))]
         for layer in range(sections):
             mine = (section_id == layer).astype(jnp.int32).reshape(1)
@@ -999,9 +1005,9 @@
                 frame_count,
             )
 
-    def logits_of(fill, first, count, pieces):
+    def logits_of(fill, first, count, pieces, earlier=None):
         return head_logits(
-            fill, first, count, pieces, member_ref, weight_rows, label_weight, frame_count
+            fill, first, count, pieces, member_ref, weight_rows, label_weight, frame_count, earlier
         )
 
     def stats_of(stats):
@@ -1016,10 +1022,8 @@
         heads = [logits_of(fill_all, 0, 2, [normed, beside])]
         held, heads[0] = lax.optimization_barrier((far, heads[0]))
         last = lax.ppermute(held, "expert", OUTWARD)
-        found = [stats_of(heads[0][2])]
-        middle, found[0] = lax.optimization_barrier((middle, found[0]))
-        heads.append(logits_of(fill_far, 2, 2, [middle, outward, held, last]))
-        found.append(stats_of(heads[1][2]))
+        heads.append(logits_of(fill_far, 2, 2, [middle, outward, held, last], heads[0][2]))
+        found = [stats_of(heads[1][2])]
     else:
         gathered = lax.all_gather(normed, "expert")
         pieces = [gathered[k] for k in range(group_size)]

time: 216 us -> 212 us (0.981)
  starting transfers between devices: 60.1 us -> 51 us
  waiting for transfers between devices: 95.6 us -> 102 us
  local copies, waits for them, and re-layouts: 16 us -> 13.2 us
    ppermute x19 -> x16, waiting for transfers between devices: 63 us -> 49 us  [crossed(): return lax.ppermute(value, axis, [(i, i ^ by) for i in range(count)])]
    ppermute x1, waiting for transfers between devices: 0.01 us -> 9.29 us  [per_device(): last = lax.ppermute(held, 'expert', OUTWARD)]
    ppermute x1, waiting for transfers between devices: 0.01 us -> 8.74 us  [per_device(): outward = lax.ppermute(middle, 'expert', OUTWARD)]
    ppermute x19 -> x16, starting transfers between devices: 33.6 us -> 25 us  [crossed(): return lax.ppermute(value, axis, [(i, i ^ by) for i in range(count)])]
    unnamed x64 -> x56, local copies, waits for them, and re-layouts: 14.6 us -> 11.7 us
  transfers between devices with their start and end apart: 51 -> 48, of which waited for: 26 -> 30; matrix products, arithmetic and copies ran while one was open for 1% -> 2% of each run, Pallas kernels for 8% -> 7%
where the time goes in v3:
time: 212 us; the launch traced here: 211 us
  waiting for transfers between devices  102 us (48%)
  starting transfers between devices  51 us (24%)
  Pallas kernels  42.5 us (20%)
  local copies, waits for them, and re-layouts  13.2 us (6%)
    ppermute x16, waiting for transfers between devices, crossed(): return lax.ppermute(value, axis, [(i, i ^ by) for i in range(count)])  49 us
    ppermute x28, waiting for transfers between devices, swap(): return lax.ppermute(value, axis, [(0, 1), (1, 0)])  34.5 us
    ppermute x16, starting transfers between devices, crossed(): return lax.ppermute(value, axis, [(i, i ^ by) for i in range(count)])  25 us
    ppermute x28, starting transfers between devices, swap(): return lax.ppermute(value, axis, [(0, 1), (1, 0)])  21.9 us
    unnamed x56, local copies, waits for them, and re-layouts  11.7 us
    pallas_call x3, Pallas kernels, head_gradient(): call(kernel, tuple((bf16_rows(each * BLOCK_ROWS, width) for _ in range(ou...  10.6 us
    ppermute x1, waiting for transfers between devices, per_device(): last = lax.ppermute(held, 'expert', OUTWARD)  9.29 us
    ppermute x1, waiting for transfers between devices, per_device(): outward = lax.ppermute(middle, 'expert', OUTWARD)  8.74 us
  transfers between devices with their start and end apart: 48, of which 30 were waited for; matrix products, arithmetic and copies ran while one was open for 2% of the time, Pallas kernels for 7%

profile of v3, /device:TPU:0, one launch (start us, length us, event | category | flops | bytes accessed | tf_op | source)
XLA Modules:
  0.0 211.2 jit_solution(15873963194822203434)
XLA Ops:
  0.7 3.0 %collective-permute-start = (s32[8,48]{1,0:T(8,128)}, s32[8,48]{1,0:T(8,128)S(1)}, u32[]{:S(2)}, u32[]{:S(2)}) collective-permute-start(s32[8,48]{1,0:T(8,128)} %bitcast.56), channel_id=1, source_target_pairs={{0,16},{16,0},{1,17},{17,1},{2,18},{18,2},{3,19},{19,3},{4,20},{20... | collective-permute-start | bytes 4616 | tf_op jit(solution)/shard_map/ppermute | solution.py:719
  12.8 2.6 %collective-permute-start.2 = (bf16[56,1280]{1,0:T(8,128)(2,1)}, bf16[56,1280]{1,0:T(8,128)(2,1)}, u32[]{:S(2)}, u32[]{:S(2)}) collective-permute-start(bf16[56,1280]{1,0:T(8,128)(2,1)} %get-tuple-element.83), channel_id=1, source_target_pairs={{0,8},{4,12},{8,0},{12,4},{1,9},{5,13},{9,1},{13,5},{2,10},{6,14},... | collective-permute-start | bytes 430088 | tf_op jit(solution)/shard_map/ppermute | solution.py:724
  19.8 6.3 %collective-permute-done.2.refs_8_ = bf16[56,1280]{1,0:T(8,128)(2,1)} collective-permute-done((bf16[56,1280]{1,0:T(8,128)(2,1)}, bf16[56,1280]{1,0:T(8,128)(2,1)}, u32[]{:S(2)}, u32[]{:S(2)}) %collective-permute-start.2) | collective-permute-done | bytes 143392 | tf_op jit(solution)/shard_map/ppermute | solution.py:724
  32.9 2.7 %collective-permute-start.10 = (bf16[56,1280]{1,0:T(8,128)(2,1)S(1)}, bf16[56,1280]{1,0:T(8,128)(2,1)S(1)}, u32[]{:S(2)}, u32[]{:S(2)}) collective-permute-start(bf16[56,1280]{1,0:T(8,128)(2,1)S(1)} %get-tuple-element.99), channel_id=1, source_target_pairs={{0,8},{4,12},{8,0},{12,4},{1,9},{5,13},{9,1},{13,5},{2,10},{6,14},... | collective-permute-start | bytes 430088 | tf_op jit(solution)/shard_map/ppermute | solution.py:724
  37.1 9.5 %collective-permute-done.10.refs_4_.refs_2_ = bf16[56,1280]{1,0:T(8,128)(2,1)S(1)} collective-permute-done((bf16[56,1280]{1,0:T(8,128)(2,1)S(1)}, bf16[56,1280]{1,0:T(8,128)(2,1)S(1)}, u32[]{:S(2)}, u32[]{:S(2)}) %collective-permute-start.10) | collective-permute-done | bytes 143392 | tf_op jit(solution)/shard_map/ppermute | solution.py:724
  50.7 2.5 %collective-permute-start.12 = (bf16[56,1280]{1,0:T(8,128)(2,1)}, bf16[56,1280]{1,0:T(8,128)(2,1)}, u32[]{:S(2)}, u32[]{:S(2)}) collective-permute-start(bf16[56,1280]{1,0:T(8,128)(2,1)} %get-tuple-element.105), channel_id=1, source_target_pairs={{0,4},{4,0},{8,12},{12,8},{1,5},{5,1},{9,13},{13,9},{2,6},{6,2},{1... | collective-permute-start | bytes 430088 | tf_op jit(solution)/shard_map/ppermute | solution.py:724
  56.6 2.4 %copy-done.1 = bf16[1280,2000]{0,1:T(8,128)(2,1)S(1)} copy-done((bf16[1280,2000]{0,1:T(8,128)(2,1)S(1)}, bf16[1280,2000]{0,1:T(8,128)(2,1)}, u32[]{:S(2)}) %copy-start.1) | copy-done | bytes 5120024
  63.6 3.3 %collective-permute-done.13.refs_8_ = bf16[56,1280]{1,0:T(8,128)(2,1)} collective-permute-done((bf16[56,1280]{1,0:T(8,128)(2,1)}, bf16[56,1280]{1,0:T(8,128)(2,1)}, u32[]{:S(2)}, u32[]{:S(2)}) %collective-permute-start.13) | collective-permute-done | bytes 143392 | tf_op jit(solution)/shard_map/ppermute | solution.py:724
  67.0 2.3 %shard_map.136 = (bf16[56,1280]{1,0:T(8,128)(2,1)S(1)}, bf16[56,1280]{1,0:T(8,128)(2,1)S(1)}, bf16[56,1280]{1,0:T(8,128)(2,1)S(1)}, bf16[56,1280]{1,0:T(8,128)(2,1)S(1)}) custom-call(s32[1]{0:T(128)} %bitcast.38.pick_ref, bf16[1280,256]{1,0:T(8,128)(2,1)S(1)} %bitcast.51, bf16[256,1280]{1,0:T(8,128)(2,1)S(1)} %bitcast.54, ...), custom_call_target="tpu_custom_call" | custom-call | flops 293601280 | tf_op jit(solution)/shard_map/pallas_call | solution.py:188
  69.3 2.8 %collective-permute-start.15 = (bf16[56,1280]{1,0:T(8,128)(2,1)S(1)}, bf16[56,1280]{1,0:T(8,128)(2,1)S(1)}, u32[]{:S(2)}, u32[]{:S(2)}) collective-permute-start(bf16[56,1280]{1,0:T(8,128)(2,1)S(1)} %get-tuple-element.116), channel_id=1, source_target_pairs={{0,4},{4,0},{8,12},{12,8},{1,5},{5,1},{9,13},{13,9},{2,6},{6,2},{1... | collective-permute-start | bytes 430088 | tf_op jit(solution)/shard_map/ppermute | solution.py:724
  77.3 8.1 %collective-permute-done.16.refs_4_ = bf16[56,1280]{1,0:T(8,128)(2,1)S(1)} collective-permute-done((bf16[56,1280]{1,0:T(8,128)(2,1)S(1)}, bf16[56,1280]{1,0:T(8,128)(2,1)S(1)}, u32[]{:S(2)}, u32[]{:S(2)}) %collective-permute-start.16) | collective-permute-done | bytes 143392 | tf_op jit(solution)/shard_map/ppermute | solution.py:724
  86.5 2.4 %collective-permute-start.20 = (bf16[192,1280]{1,0:T(8,128)(2,1)S(1)}, bf16[192,1280]{1,0:T(8,128)(2,1)S(1)}, u32[]{:S(2)}, u32[]{:S(2)}) collective-permute-start(bf16[192,1280]{1,0:T(8,128)(2,1)S(1)} %shard_map.137.refs_0_), channel_id=1, source_target_pairs={{0,4},{4,0},{8,12},{12,8},{1,5},{5,1},{9,13},{13,9},{2,6},{6,2},{1... | collective-permute-start | bytes 1474568 | tf_op jit(solution)/shard_map/ppermute | solution.py:724
  89.6 9.5 %collective-permute-done.20.refs_1_ = bf16[192,1280]{1,0:T(8,128)(2,1)S(1)} collective-permute-done((bf16[192,1280]{1,0:T(8,128)(2,1)S(1)}, bf16[192,1280]{1,0:T(8,128)(2,1)S(1)}, u32[]{:S(2)}, u32[]{:S(2)}) %collective-permute-start.20) | collective-permute-done | bytes 491552 | tf_op jit(solution)/shard_map/ppermute | solution.py:724
  101.3 2.4 %copy-done.2 = bf16[1280,2000]{0,1:T(8,128)(2,1)S(1)} copy-done((bf16[1280,2000]{0,1:T(8,128)(2,1)S(1)}, bf16[1280,2000]{0,1:T(8,128)(2,1)}, u32[]{:S(2)}) %copy-start.2) | copy-done | bytes 5120024
  103.8 3.2 %shard_map.138 = (f32[2048,384]{1,0:T(8,128)S(1)}, bf16[384,1280]{1,0:T(8,128)(2,1)S(1)}, f32[2,16,192]{2,1,0:T(8,128)S(1)}) custom-call(s32[1]{0:T(128)} %bitcast.member_ref, bf16[2000,1280]{1,0:T(8,128)(2,1)S(1)} %bitcast.47, bf16[256,1280]{1,0:T(8,128)(2,1)S(1)} %get-tuple-element.109.label_ref, bf16[192,1280]{1,0:T(8,128)(2,1)S(1)} %shard_map.137.refs_0_, ...), custom_call_target="tpu_custom_call" | custom-call | flops 2013265920 | tf_op jit(solution)/shard_map/pallas_call | solution.py:424
  108.3 8.7 %collective-permute-done.19.refs_1_ = bf16[192,1280]{1,0:T(8,128)(2,1)S(1)} collective-permute-done((bf16[192,1280]{1,0:T(8,128)(2,1)S(1)}, bf16[192,1280]{1,0:T(8,128)(2,1)S(1)}, u32[]{:S(2)}, u32[]{:S(2)}) %collective-permute-start.19) | collective-permute-done | bytes 491552 | tf_op jit(solution)/shard_map/ppermute | solution.py:1021
  117.0 9.3 %collective-permute-done.22.refs_3_ = bf16[192,1280]{1,0:T(8,128)(2,1)S(1)} collective-permute-done((bf16[192,1280]{1,0:T(8,128)(2,1)S(1)}, bf16[192,1280]{1,0:T(8,128)(2,1)S(1)}, u32[]{:S(2)}, u32[]{:S(2)}) %collective-permute-start.22) | collective-permute-done | bytes 491552 | tf_op jit(solution)/shard_map/ppermute | solution.py:1024
  126.3 3.3 %shard_map.139 = (f32[2048,384]{1,0:T(8,128)S(1)}, bf16[384,1280]{1,0:T(8,128)(2,1)S(1)}, f32[4,16,192]{2,1,0:T(8,128)S(1)}) custom-call(s32[1]{0:T(128)} %bitcast.member_ref, bf16[2000,1280]{1,0:T(8,128)(2,1)S(1)} %bitcast.48, bf16[256,1280]{1,0:T(8,128)(2,1)S(1)} %get-tuple-element.109.label_ref, bf16[192,1280]{1,0:T(8,128)(2,1)S(1)} %collective-permute-done.18.refs_0_, ...), custom_call_target="tpu_custom_call" | custom-call | flops 2013265920 | tf_op jit(solution)/shard_map/pallas_call | solution.py:424
  131.3 2.5 %collective-permute-done.23.refs_1_ = f32[4,16,192]{2,1,0:T(8,128)S(1)} collective-permute-done((f32[4,16,192]{2,1,0:T(8,128)S(1)}, f32[4,16,192]{2,1,0:T(8,128)S(1)}, u32[]{:S(2)}, u32[]{:S(2)}) %collective-permute-start.23) | collective-permute-done | bytes 49184 | tf_op jit(solution)/shard_map/ppermute | solution.py:724
  134.1 2.7 %collective-permute-done.24.refs_2_ = f32[4,16,192]{2,1,0:T(8,128)S(1)} collective-permute-done((f32[4,16,192]{2,1,0:T(8,128)S(1)}, f32[4,16,192]{2,1,0:T(8,128)S(1)}, u32[]{:S(2)}, u32[]{:S(2)}) %collective-permute-start.24) | collective-permute-done | bytes 49184 | tf_op jit(solution)/shard_map/ppermute | solution.py:724
  136.8 2.4 %collective-permute-done.25.refs_3_ = f32[4,16,192]{2,1,0:T(8,128)S(1)} collective-permute-done((f32[4,16,192]{2,1,0:T(8,128)S(1)}, f32[4,16,192]{2,1,0:T(8,128)S(1)}, u32[]{:S(2)}, u32[]{:S(2)}) %collective-permute-start.25) | collective-permute-done | bytes 49184 | tf_op jit(solution)/shard_map/ppermute | solution.py:724
  139.2 6.9 %shard_map.140 = (f32[16,768]{1,0:T(8,128)S(1)}, bf16[256,768]{1,0:T(8,128)(2,1)S(1)}, bf16[256,768]{1,0:T(8,128)(2,1)S(1)}, f32[1,4]{1,0:T(1,128)}) custom-call(s32[16]{0:T(128)S(1)} %fusion.slots_ref, s32[16,128]{1,0:T(8,128)S(1)} %get-tuple-element.103.notes_ref, f32[4,16,192]{2,1,0:T(8,128)S(1)} %get-tuple-element.124.refs_0_, ...), custom_call_target="tpu_custom_call" | custom-call | flops 67108864 | tf_op jit(solution)/shard_map/pallas_call | solution.py:610
  146.1 4.9 %shard_map.141 = (bf16[512,1280]{1,0:T(8,128)(2,1)S(1)}, bf16[512,1280]{1,0:T(8,128)(2,1)S(1)}) custom-call(s32[4]{0:T(128)S(1)} %get-tuple-element.130.order_ref, f32[2048,384]{1,0:T(8,128)S(1)} %get-tuple-element.131.refs_0_, f32[2048,384]{1,0:T(8,128)S(1)} %get-tuple-element.132.refs_1_, bf16[384,1280]{1,0:T(8,128)(2,1)S(1)} %get-tuple-element.133.refs_2_, ...), custom_call_target="tpu_custom_call" | custom-call | flops 2818572288 | tf_op jit(solution)/shard_map/pallas_call | solution.py:661
  151.6 2.8 %shard_map.142.own_ref = bf16[512,1280]{1,0:T(8,128)(2,1)S(1)} custom-call(s32[2]{0:T(128)S(1)} %get-tuple-element.140.order_ref, f32[2048,384]{1,0:T(8,128)S(1)} %get-tuple-element.131.refs_0_, f32[2048,384]{1,0:T(8,128)S(1)} %get-tuple-element.132.refs_1_, bf16[384,1280]{1,0:T(8,128)(2,1)S(1)} %get-tuple-element.133.refs_2_, ...), custom_call_target="tpu_custom_call" | custom-call | flops 1409286144 | tf_op jit(solution)/shard_map/pallas_call | solution.py:661
  159.4 2.8 %shard_map.144.own_ref = bf16[512,1280]{1,0:T(8,128)(2,1)S(1)} custom-call(s32[2]{0:T(128)S(1)} %get-tuple-element.142.order_ref, f32[2048,384]{1,0:T(8,128)S(1)} %get-tuple-element.131.refs_0_, f32[2048,384]{1,0:T(8,128)S(1)} %get-tuple-element.132.refs_1_, bf16[384,1280]{1,0:T(8,128)(2,1)S(1)} %get-tuple-element.133.refs_2_, ...), custom_call_target="tpu_custom_call" | custom-call | flops 1409286144 | tf_op jit(solution)/shard_map/pallas_call | solution.py:661
  162.2 3.7 %collective-permute-done.29.refs_0_ = bf16[128,1280]{1,0:T(8,128)(2,1)S(1)} collective-permute-done((bf16[128,1280]{1,0:T(8,128)(2,1)S(1)}, bf16[128,1280]{1,0:T(8,128)(2,1)S(1)}, u32[]{:S(2)}, u32[]{:S(2)}) %collective-permute-start.29) | collective-permute-done | bytes 327712 | tf_op jit(solution)/shard_map/ppermute | solution.py:719
  170.3 2.6 %collective-permute-done.28.refs_0_ = bf16[128,1280]{1,0:T(8,128)(2,1)S(1)} collective-permute-done((bf16[128,1280]{1,0:T(8,128)(2,1)S(1)}, bf16[128,1280]{1,0:T(8,128)(2,1)S(1)}, u32[]{:S(2)}, u32[]{:S(2)}) %collective-permute-start.28) | collective-permute-done | bytes 327712 | tf_op jit(solution)/shard_map/ppermute | solution.py:719
  173.7 5.8 %collective-permute-done.31.refs_1_ = bf16[128,1280]{1,0:T(8,128)(2,1)S(1)} collective-permute-done((bf16[128,1280]{1,0:T(8,128)(2,1)S(1)}, bf16[128,1280]{1,0:T(8,128)(2,1)S(1)}, u32[]{:S(2)}, u32[]{:S(2)}) %collective-permute-start.31) | collective-permute-done | bytes 327712 | tf_op jit(solution)/shard_map/ppermute | solution.py:719
  184.5 6.6 %collective-permute-done.34.refs_2_ = bf16[128,1280]{1,0:T(8,128)(2,1)S(1)} collective-permute-done((bf16[128,1280]{1,0:T(8,128)(2,1)S(1)}, bf16[128,1280]{1,0:T(8,128)(2,1)S(1)}, u32[]{:S(2)}, u32[]{:S(2)}) %collective-permute-start.34) | collective-permute-done | bytes 327712 | tf_op jit(solution)/shard_map/ppermute | solution.py:719
  193.9 4.2 %collective-permute-done.40.refs_3_ = bf16[128,1280]{1,0:T(8,128)(2,1)S(1)} collective-permute-done((bf16[128,1280]{1,0:T(8,128)(2,1)S(1)}, bf16[128,1280]{1,0:T(8,128)(2,1)S(1)}, u32[]{:S(2)}, u32[]{:S(2)}) %collective-permute-start.40) | collective-permute-done | bytes 327712 | tf_op jit(solution)/shard_map/ppermute | solution.py:719
  199.7 4.6 %collective-permute-done.35.refs_0_ = bf16[128,1280]{1,0:T(8,128)(2,1)S(1)} collective-permute-done((bf16[128,1280]{1,0:T(8,128)(2,1)S(1)}, bf16[128,1280]{1,0:T(8,128)(2,1)S(1)}, u32[]{:S(2)}, u32[]{:S(2)}) %collective-permute-start.35) | collective-permute-done | bytes 327712 | tf_op jit(solution)/shard_map/ppermute | solution.py:719
  206.9 2.6 %shard_map.147.refs_4_ = bf16[2000,1280]{1,0:T(8,128)(2,1)} custom-call(s32[12]{0:T(128)S(1)} %stack.122.offsets_ref, bf16[128,1280]{1,0:T(8,128)(2,1)S(1)} %get-tuple-element.149.refs_0_, bf16[128,1280]{1,0:T(8,128)(2,1)S(1)} %get-tuple-element.150.refs_1_, bf16[128,1280]{1,0:T(8,128)(2,1)S(1)} %collective-permute-done.34.refs_2_, ...), custom_call_target="tpu_custom_call" | custom-call | tf_op jit(solution)/shard_map/pallas_call | solution.py:708
  (169 shorter events, 70.4 us)
Async XLA Ops:
  9.2 17.0 %collective-permute-start.5 = (bf16[1280,128]{1,0:T(8,128)(2,1)}, bf16[1280,128]{1,0:T(8,128)(2,1)S(1)}, u32[]{:S(2)}, u32[]{:S(2)}) collective-permute-start(bf16[1280,128]{1,0:T(8,128)(2,1)} %get-tuple-element.87), channel_id=1, source_target_pairs={{0,16},{16,0},{1,17},{17,1},{2,18},{18,2},{3,19},{19,3},{4,20},{20... | collective-permute-start | bytes 983048 | tf_op jit(solution)/shard_map/ppermute | solution.py:719
  10.3 16.3 %collective-permute-start.6 = (bf16[128,1280]{1,0:T(8,128)(2,1)}, bf16[128,1280]{1,0:T(8,128)(2,1)}, u32[]{:S(2)}, u32[]{:S(2)}) collective-permute-start(bf16[128,1280]{1,0:T(8,128)(2,1)} %get-tuple-element.88), channel_id=1, source_target_pairs={{0,16},{16,0},{1,17},{17,1},{2,18},{18,2},{3,19},{19,3},{4,20},{20... | collective-permute-start | bytes 983048 | tf_op jit(solution)/shard_map/ppermute | solution.py:719
  12.8 13.3 %collective-permute-start.2 = (bf16[56,1280]{1,0:T(8,128)(2,1)}, bf16[56,1280]{1,0:T(8,128)(2,1)}, u32[]{:S(2)}, u32[]{:S(2)}) collective-permute-start(bf16[56,1280]{1,0:T(8,128)(2,1)} %get-tuple-element.83), channel_id=1, source_target_pairs={{0,8},{4,12},{8,0},{12,4},{1,9},{5,13},{9,1},{13,5},{2,10},{6,14},... | collective-permute-start | bytes 430088 | tf_op jit(solution)/shard_map/ppermute | solution.py:724
  15.4 10.7 %collective-permute-start.3 = (bf16[56,1280]{1,0:T(8,128)(2,1)}, bf16[56,1280]{1,0:T(8,128)(2,1)}, u32[]{:S(2)}, u32[]{:S(2)}) collective-permute-start(bf16[56,1280]{1,0:T(8,128)(2,1)} %get-tuple-element.84), channel_id=1, source_target_pairs={{0,12},{4,8},{8,4},{12,0},{1,13},{5,9},{9,5},{13,1},{2,14},{6,10},... | collective-permute-start | bytes 430088 | tf_op jit(solution)/shard_map/ppermute | solution.py:724
  18.9 8.5 %collective-permute-start.4 = (f32[16,1280]{1,0:T(8,128)S(1)}, f32[16,1280]{1,0:T(8,128)S(1)}, u32[]{:S(2)}, u32[]{:S(2)}) collective-permute-start(f32[16,1280]{1,0:T(8,128)S(1)} %maximum_maximum_fusion.refs_0_), channel_id=1, source_target_pairs={{0,16},{16,0},{1,17},{17,1},{2,18},{18,2},{3,19},{19,3},{4,20},{20... | collective-permute-start | bytes 245768 | tf_op jit(solution)/shard_map/ppermute | solution.py:719
  32.9 13.8 %collective-permute-start.10 = (bf16[56,1280]{1,0:T(8,128)(2,1)S(1)}, bf16[56,1280]{1,0:T(8,128)(2,1)S(1)}, u32[]{:S(2)}, u32[]{:S(2)}) collective-permute-start(bf16[56,1280]{1,0:T(8,128)(2,1)S(1)} %get-tuple-element.99), channel_id=1, source_target_pairs={{0,8},{4,12},{8,0},{12,4},{1,9},{5,13},{9,1},{13,5},{2,10},{6,14},... | collective-permute-start | bytes 430088 | tf_op jit(solution)/shard_map/ppermute | solution.py:724
  35.6 11.0 %collective-permute-start.11 = (bf16[56,1280]{1,0:T(8,128)(2,1)S(1)}, bf16[56,1280]{1,0:T(8,128)(2,1)S(1)}, u32[]{:S(2)}, u32[]{:S(2)}) collective-permute-start(bf16[56,1280]{1,0:T(8,128)(2,1)S(1)} %get-tuple-element.100), channel_id=1, source_target_pairs={{0,12},{4,8},{8,4},{12,0},{1,13},{5,9},{9,5},{13,1},{2,14},{6,10},... | collective-permute-start | bytes 430088 | tf_op jit(solution)/shard_map/ppermute | solution.py:724
  37.0 10.2 %collective-permute-start.9 = (bf16[56,1280]{1,0:T(8,128)(2,1)S(1)}, bf16[56,1280]{1,0:T(8,128)(2,1)S(1)}, u32[]{:S(2)}, u32[]{:S(2)}) collective-permute-start(bf16[56,1280]{1,0:T(8,128)(2,1)S(1)} %get-tuple-element.98), channel_id=1, source_target_pairs={{0,4},{4,0},{8,12},{12,8},{1,5},{5,1},{9,13},{13,9},{2,6},{6,2},{1... | collective-permute-start | bytes 430088 | tf_op jit(solution)/shard_map/ppermute | solution.py:724
  50.7 12.9 %collective-permute-start.12 = (bf16[56,1280]{1,0:T(8,128)(2,1)}, bf16[56,1280]{1,0:T(8,128)(2,1)}, u32[]{:S(2)}, u32[]{:S(2)}) collective-permute-start(bf16[56,1280]{1,0:T(8,128)(2,1)} %get-tuple-element.105), channel_id=1, source_target_pairs={{0,4},{4,0},{8,12},{12,8},{1,5},{5,1},{9,13},{13,9},{2,6},{6,2},{1... | collective-permute-start | bytes 430088 | tf_op jit(solution)/shard_map/ppermute | solution.py:724
  53.2 13.7 %collective-permute-start.13 = (bf16[56,1280]{1,0:T(8,128)(2,1)}, bf16[56,1280]{1,0:T(8,128)(2,1)}, u32[]{:S(2)}, u32[]{:S(2)}) collective-permute-start(bf16[56,1280]{1,0:T(8,128)(2,1)} %get-tuple-element.106), channel_id=1, source_target_pairs={{0,8},{4,12},{8,0},{12,4},{1,9},{5,13},{9,1},{13,5},{2,10},{6,14},... | collective-permute-start | bytes 430088 | tf_op jit(solution)/shard_map/ppermute | solution.py:724
  55.2 11.7 %collective-permute-start.14 = (bf16[56,1280]{1,0:T(8,128)(2,1)}, bf16[56,1280]{1,0:T(8,128)(2,1)}, u32[]{:S(2)}, u32[]{:S(2)}) collective-permute-start(bf16[56,1280]{1,0:T(8,128)(2,1)} %get-tuple-element.107), channel_id=1, source_target_pairs={{0,12},{4,8},{8,4},{12,0},{1,13},{5,9},{9,5},{13,1},{2,14},{6,10},... | collective-permute-start | bytes 430088 | tf_op jit(solution)/shard_map/ppermute | solution.py:724
  69.3 8.1 %collective-permute-start.15 = (bf16[56,1280]{1,0:T(8,128)(2,1)S(1)}, bf16[56,1280]{1,0:T(8,128)(2,1)S(1)}, u32[]{:S(2)}, u32[]{:S(2)}) collective-permute-start(bf16[56,1280]{1,0:T(8,128)(2,1)S(1)} %get-tuple-element.116), channel_id=1, source_target_pairs={{0,4},{4,0},{8,12},{12,8},{1,5},{5,1},{9,13},{13,9},{2,6},{6,2},{1... | collective-permute-start | bytes 430088 | tf_op jit(solution)/shard_map/ppermute | solution.py:724
  72.1 13.4 %collective-permute-start.16 = (bf16[56,1280]{1,0:T(8,128)(2,1)S(1)}, bf16[56,1280]{1,0:T(8,128)(2,1)S(1)}, u32[]{:S(2)}, u32[]{:S(2)}) collective-permute-start(bf16[56,1280]{1,0:T(8,128)(2,1)S(1)} %get-tuple-element.117), channel_id=1, source_target_pairs={{0,8},{4,12},{8,0},{12,4},{1,9},{5,13},{9,1},{13,5},{2,10},{6,14},... | collective-permute-start | bytes 430088 | tf_op jit(solution)/shard_map/ppermute | solution.py:724
  74.0 11.5 %collective-permute-start.17 = (bf16[56,1280]{1,0:T(8,128)(2,1)S(1)}, bf16[56,1280]{1,0:T(8,128)(2,1)S(1)}, u32[]{:S(2)}, u32[]{:S(2)}) collective-permute-start(bf16[56,1280]{1,0:T(8,128)(2,1)S(1)} %get-tuple-element.118), channel_id=1, source_target_pairs={{0,12},{4,8},{8,4},{12,0},{1,13},{5,9},{9,5},{13,1},{2,14},{6,10},... | collective-permute-start | bytes 430088 | tf_op jit(solution)/shard_map/ppermute | solution.py:724
  86.5 12.6 %collective-permute-start.20 = (bf16[192,1280]{1,0:T(8,128)(2,1)S(1)}, bf16[192,1280]{1,0:T(8,128)(2,1)S(1)}, u32[]{:S(2)}, u32[]{:S(2)}) collective-permute-start(bf16[192,1280]{1,0:T(8,128)(2,1)S(1)} %shard_map.137.refs_0_), channel_id=1, source_target_pairs={{0,4},{4,0},{8,12},{12,8},{1,5},{5,1},{9,13},{13,9},{2,6},{6,2},{1... | collective-permute-start | bytes 1474568 | tf_op jit(solution)/shard_map/ppermute | solution.py:724
  88.9 10.9 %collective-permute-start.18 = (bf16[192,1280]{1,0:T(8,128)(2,1)S(1)}, bf16[192,1280]{1,0:T(8,128)(2,1)S(1)}, u32[]{:S(2)}, u32[]{:S(2)}) collective-permute-start(bf16[192,1280]{1,0:T(8,128)(2,1)S(1)} %shard_map.137.refs_0_), channel_id=1, source_target_pairs={{4,8},{8,4},{5,9},{9,5},{6,10},{10,6},{7,11},{11,7},{20,24},{24,20... | collective-permute-start | bytes 1474568 | tf_op jit(solution)/shard_map/ppermute | solution.py:1019
  99.8 17.2 %collective-permute-start.19 = (bf16[192,1280]{1,0:T(8,128)(2,1)S(1)}, bf16[192,1280]{1,0:T(8,128)(2,1)S(1)}, u32[]{:S(2)}, u32[]{:S(2)}) collective-permute-start(bf16[192,1280]{1,0:T(8,128)(2,1)S(1)} %collective-permute-done.18.refs_0_), channel_id=1, source_target_pairs={{4,0},{8,12},{5,1},{9,13},{6,2},{10,14},{7,3},{11,15},{20,16},{24,... | collective-permute-start | bytes 1474568 | tf_op jit(solution)/shard_map/ppermute | solution.py:1021
  107.0 19.3 %collective-permute-start.22 = (bf16[192,1280]{1,0:T(8,128)(2,1)S(1)}, bf16[192,1280]{1,0:T(8,128)(2,1)S(1)}, u32[]{:S(2)}, u32[]{:S(2)}) collective-permute-start(bf16[192,1280]{1,0:T(8,128)(2,1)S(1)} %collective-permute-done.21.refs_2_), channel_id=1, source_target_pairs={{4,0},{8,12},{5,1},{9,13},{6,2},{10,14},{7,3},{11,15},{20,16},{24,... | collective-permute-start | bytes 1474568 | tf_op jit(solution)/shard_map/ppermute | solution.py:1024
  151.1 11.2 %collective-permute-start.27 = (bf16[512,1280]{1,0:T(8,128)(2,1)S(1)}, bf16[512,1280]{1,0:T(8,128)(2,1)S(1)}, u32[]{:S(2)}, u32[]{:S(2)}) collective-permute-start(bf16[512,1280]{1,0:T(8,128)(2,1)S(1)} %get-tuple-element.143), channel_id=1, source_target_pairs={{0,1},{1,0},{2,3},{3,2},{4,5},{5,4},{6,7},{7,6},{8,9},{9,8},{10,11... | collective-permute-start | bytes 3932168 | tf_op jit(solution)/shard_map/ppermute | solution.py:719
  155.3 10.6 %collective-permute-start.29 = (bf16[128,1280]{1,0:T(8,128)(2,1)S(1)}, bf16[128,1280]{1,0:T(8,128)(2,1)S(1)}, u32[]{:S(2)}, u32[]{:S(2)}) collective-permute-start(bf16[128,1280]{1,0:T(8,128)(2,1)S(1)} %get-tuple-element.141), channel_id=1, source_target_pairs={{0,16},{16,0},{1,17},{17,1},{2,18},{18,2},{3,19},{19,3},{4,20},{20... | collective-permute-start | bytes 983048 | tf_op jit(solution)/shard_map/ppermute | solution.py:719
  156.1 10.6 %collective-permute-start.30 = (bf16[128,1280]{1,0:T(8,128)(2,1)S(1)}, bf16[128,1280]{1,0:T(8,128)(2,1)S(1)}, u32[]{:S(2)}, u32[]{:S(2)}) collective-permute-start(bf16[128,1280]{1,0:T(8,128)(2,1)S(1)} %get-tuple-element.145), channel_id=1, source_target_pairs={{0,2},{2,0},{1,3},{3,1},{4,6},{6,4},{5,7},{7,5},{8,10},{10,8},{9,1... | collective-permute-start | bytes 983048 | tf_op jit(solution)/shard_map/ppermute | solution.py:719
  157.6 15.3 %collective-permute-start.28 = (bf16[128,1280]{1,0:T(8,128)(2,1)S(1)}, bf16[128,1280]{1,0:T(8,128)(2,1)S(1)}, u32[]{:S(2)}, u32[]{:S(2)}) collective-permute-start(bf16[128,1280]{1,0:T(8,128)(2,1)S(1)} %get-tuple-element.144), channel_id=1, source_target_pairs={{0,16},{16,0},{1,17},{17,1},{2,18},{18,2},{3,19},{19,3},{4,20},{20... | collective-permute-start | bytes 983048 | tf_op jit(solution)/shard_map/ppermute | solution.py:719
  158.9 14.8 %collective-permute-start.32 = (bf16[128,1280]{1,0:T(8,128)(2,1)S(1)}, bf16[128,1280]{1,0:T(8,128)(2,1)S(1)}, u32[]{:S(2)}, u32[]{:S(2)}) collective-permute-start(bf16[128,1280]{1,0:T(8,128)(2,1)S(1)} %get-tuple-element.147), channel_id=1, source_target_pairs={{0,2},{2,0},{1,3},{3,1},{4,6},{6,4},{5,7},{7,5},{8,10},{10,8},{9,1... | collective-permute-start | bytes 983048 | tf_op jit(solution)/shard_map/ppermute | solution.py:719
  167.5 12.1 %collective-permute-start.31 = (bf16[128,1280]{1,0:T(8,128)(2,1)S(1)}, bf16[128,1280]{1,0:T(8,128)(2,1)S(1)}, u32[]{:S(2)}, u32[]{:S(2)}) collective-permute-start(bf16[128,1280]{1,0:T(8,128)(2,1)S(1)} %get-tuple-element.146), channel_id=1, source_target_pairs={{0,2},{2,0},{1,3},{3,1},{4,6},{6,4},{5,7},{7,5},{8,10},{10,8},{9,1... | collective-permute-start | bytes 983048 | tf_op jit(solution)/shard_map/ppermute | solution.py:719
  169.1 10.5 %collective-permute-start.33 = (bf16[128,1280]{1,0:T(8,128)(2,1)S(1)}, bf16[128,1280]{1,0:T(8,128)(2,1)S(1)}, u32[]{:S(2)}, u32[]{:S(2)}) collective-permute-start(bf16[128,1280]{1,0:T(8,128)(2,1)S(1)} %get-tuple-element.148), channel_id=1, source_target_pairs={{0,16},{16,0},{1,17},{17,1},{2,18},{18,2},{3,19},{19,3},{4,20},{20... | collective-permute-start | bytes 983048 | tf_op jit(solution)/shard_map/ppermute | solution.py:719
  180.4 10.7 %collective-permute-start.34 = (bf16[128,1280]{1,0:T(8,128)(2,1)S(1)}, bf16[128,1280]{1,0:T(8,128)(2,1)S(1)}, u32[]{:S(2)}, u32[]{:S(2)}) collective-permute-start(bf16[128,1280]{1,0:T(8,128)(2,1)S(1)} %get-tuple-element.149.refs_0_), channel_id=1, source_target_pairs={{0,2},{2,0},{1,3},{3,1},{4,6},{6,4},{5,7},{7,5},{8,10},{10,8},{9,1... | collective-permute-start | bytes 983048 | tf_op jit(solution)/shard_map/ppermute | solution.py:719
  182.0 10.6 %collective-permute-start.36 = (bf16[128,1280]{1,0:T(8,128)(2,1)S(1)}, bf16[128,1280]{1,0:T(8,128)(2,1)S(1)}, u32[]{:S(2)}, u32[]{:S(2)}) collective-permute-start(bf16[128,1280]{1,0:T(8,128)(2,1)S(1)} %get-tuple-element.150.refs_1_), channel_id=1, source_target_pairs={{0,16},{16,0},{1,17},{17,1},{2,18},{18,2},{3,19},{19,3},{4,20},{20... | collective-permute-start | bytes 983048 | tf_op jit(solution)/shard_map/ppermute | solution.py:719
  183.3 14.9 %collective-permute-start.40 = (bf16[128,1280]{1,0:T(8,128)(2,1)S(1)}, bf16[128,1280]{1,0:T(8,128)(2,1)S(1)}, u32[]{:S(2)}, u32[]{:S(2)}) collective-permute-start(bf16[128,1280]{1,0:T(8,128)(2,1)S(1)} %get-tuple-element.150.refs_1_), channel_id=1, source_target_pairs={{0,2},{2,0},{1,3},{3,1},{4,6},{6,4},{5,7},{7,5},{8,10},{10,8},{9,1... | collective-permute-start | bytes 983048 | tf_op jit(solution)/shard_map/ppermute | solution.py:719
  183.8 15.9 %collective-permute-start.41 = (bf16[128,1280]{1,0:T(8,128)(2,1)S(1)}, bf16[128,1280]{1,0:T(8,128)(2,1)S(1)}, u32[]{:S(2)}, u32[]{:S(2)}) collective-permute-start(bf16[128,1280]{1,0:T(8,128)(2,1)S(1)} %get-tuple-element.149.refs_0_), channel_id=1, source_target_pairs={{0,16},{16,0},{1,17},{17,1},{2,18},{18,2},{3,19},{19,3},{4,20},{20... | collective-permute-start | bytes 983048 | tf_op jit(solution)/shard_map/ppermute | solution.py:719
  191.1 13.2 %collective-permute-start.35 = (bf16[128,1280]{1,0:T(8,128)(2,1)S(1)}, bf16[128,1280]{1,0:T(8,128)(2,1)S(1)}, u32[]{:S(2)}, u32[]{:S(2)}) collective-permute-start(bf16[128,1280]{1,0:T(8,128)(2,1)S(1)} %collective-permute-done.34.refs_2_), channel_id=1, source_target_pairs={{0,16},{16,0},{1,17},{17,1},{2,18},{18,2},{3,19},{19,3},{4,20},{20... | collective-permute-start | bytes 983048 | tf_op jit(solution)/shard_map/ppermute | solution.py:719
  192.7 11.7 %collective-permute-start.37 = (bf16[128,1280]{1,0:T(8,128)(2,1)S(1)}, bf16[128,1280]{1,0:T(8,128)(2,1)S(1)}, u32[]{:S(2)}, u32[]{:S(2)}) collective-permute-start(bf16[128,1280]{1,0:T(8,128)(2,1)S(1)} %collective-permute-done.36.refs_5_), channel_id=1, source_target_pairs={{0,2},{2,0},{1,3},{3,1},{4,6},{6,4},{5,7},{7,5},{8,10},{10,8},{9,1... | collective-permute-start | bytes 983048 | tf_op jit(solution)/shard_map/ppermute | solution.py:719
  193.9 10.9 %collective-permute-start.42 = (bf16[128,1280]{1,0:T(8,128)(2,1)S(1)}, bf16[128,1280]{1,0:T(8,128)(2,1)S(1)}, u32[]{:S(2)}, u32[]{:S(2)}) collective-permute-start(bf16[128,1280]{1,0:T(8,128)(2,1)S(1)} %get-tuple-element.149.refs_0_), channel_id=1, source_target_pairs={{0,1},{1,0},{2,3},{3,2},{4,5},{5,4},{6,7},{7,6},{8,9},{9,8},{10,11... | collective-permute-start | bytes 983048 | tf_op jit(solution)/shard_map/ppermute | solution.py:719
  (44 other events, 203.6 us)

commit v4 on v3

--- a/solution.py
+++ b/solution.py
@@ -288,10 +288,10 @@
     return [(i, min(BLOCK_ROWS, shard - i)) for i in range(0, shard, BLOCK_ROWS)]
 
 
-def label_rows(weight, notes, member, pairs, spare, label_max, line):
+def label_rows(weight, notes, member, groups, pairs, spare, label_max, line):
     shard, width = weight.shape
     sources = len(notes)
-    utterances = sources * pairs
+    utterances = sources * groups * pairs
     entries = utterances * COLS
 
     def kernel(member_ref, weight_ref, *refs):
@@ -312,8 +312,8 @@
             ]
         names_ref[...] = jnp.zeros(names_ref.shape, jnp.int32)
         for slot in range(sources):
-            for pair in range(pairs):
-                row = slot * pairs + pair
+            for pair in range(groups * pairs):
+                row = (pair // pairs * sources + slot) * pairs + pair % pairs
                 names_ref[row : row + 1, :COLS] = found[slot][:, pair * COLS : (pair + 1) * COLS]
         lane = lax.broadcasted_iota(jnp.int32, (utterances, LANES), 1)
         named = jnp.where(lane < label_max, names_ref[...], jnp.where(lane == label_max, 0, -1))
@@ -435,13 +435,16 @@
     )(member, weight, label_weight, *pieces, *others)
 
 
-def fill_far(place, piece_refs, put, put_if):
-    middle, outward, far, last = piece_refs
+def fill_line(place, piece_refs, put, put_if):
+    own, beside, middle, outward, far, last = piece_refs
     ends = (place == 0) | (place == 3)
-    put_if(ends, 0, outward)
-    put_if(ends, 1, last)
-    put_if((place == 1) | (place == 2), 0, middle)
-    put_if((place == 1) | (place == 2), 1, far)
+    inner = (place == 1) | (place == 2)
+    put(0, own)
+    put(1, beside)
+    put_if(ends, 2, outward)
+    put_if(ends, 3, last)
+    put_if(inner, 2, middle)
+    put_if(inner, 3, far)
 
 
 def fill_all(place, piece_refs, put, put_if):
@@ -461,7 +464,7 @@
     )
 
 
-def ctc_pass(stats, slots, notes, frame_count, label_max, kept):
+def ctc_pass(stats, slots, notes, frame_count, label_max, parts, kept):
     calls, sources = len(stats), len(stats[0])
     each, _, span = stats[0][0].shape
     count = calls * each
@@ -574,7 +577,9 @@
         near_state = jnp.sum(jnp.where(lane == counts - 1, fwd_label, 0.0), axis=1, keepdims=True)
         log_like = log_add(end_state, near_state)
         turned_losses = jnp.transpose(jnp.broadcast_to(-log_like, (utterances, LANES)), (1, 0))
-        loss_ref[...] = turned_losses[:1, :kept]
+        for part in range(parts):
+            first = part * utterances // parts
+            loss_ref[:, part * kept : (part + 1) * kept] = turned_losses[:1, first : first + kept]
 
         def occupy(step, carry):
             blank = jnp.exp(blank_fwd[step] + blank_bwd[step] - log_like)
@@ -613,7 +618,7 @@
             jax.ShapeDtypeStruct((COLS, row_count), jnp.float32),
             bf16_rows(entries, row_count),
             bf16_rows(entries, row_count),
-            jax.ShapeDtypeStruct((1, kept), jnp.float32),
+            jax.ShapeDtypeStruct((1, parts * kept), jnp.float32),
         ),
         1 << 26,
         in_specs=[smem_spec()] + [vmem_spec()] * (1 + calls * sources),
@@ -737,7 +742,7 @@
     return LINE_ORDER if count == 4 else np.tile(np.arange(count), (count, 1))
 
 
-def slot_tables(count):
+def slot_tables(count, groups):
     orders = slot_orders(count)
     tables = np.zeros((count, count, count), np.int32)
     for member in range(count):
@@ -745,7 +750,8 @@
             source = member ^ k
             for slot in range(count):
                 tables[member, k, slot] = list(orders[source]).index(orders[member][slot])
-    return tables.reshape(count, count * count)
+    tables = np.concatenate([tables + g * count for g in range(groups)], axis=2)
+    return tables.reshape(count, groups * count * count)
 
 
 def wide(ref, start, size):
@@ -831,9 +837,11 @@
     per_section = pair_count // sections
     first_pair = section_id * per_section
     share = (utt_dev * frame_count * 9 + 8 * experts - 1) // (8 * experts)
-    filled = share * -(-per_section // utt_dev)
+    group_count = 2 if per_section % (2 * utt_dev) == 0 else 1
+    group_pairs = per_section // group_count
+    filled = share * -(-group_pairs // utt_dev)
     capacity = round_up(filled + 1, 8)
-    span = per_section * frame_count
+    span = group_pairs * frame_count
     member_ref = member.astype(jnp.int32).reshape(1)
 
     def mine_of(value):
@@ -843,11 +851,14 @@
         return [blocks[0]] + [crossed(blocks[k], "expert", k) for k in range(1, group_size)]
 
     def lanes_of(ids):
-        return jnp.pad(mine_of(ids), ((0, 0), (0, LANES - frame_count)), constant_values=-1)
-
-    current = lax.dynamic_slice_in_dim(
-        frames.reshape(pair_count * frame_count, width), first_pair * frame_count, span, 0
-    )
+        ids = jnp.pad(mine_of(ids), ((0, 0), (0, LANES - frame_count)), constant_values=-1)
+        return [ids[g * group_pairs : (g + 1) * group_pairs] for g in range(group_count)]
+
+    flat_frames = frames.reshape(pair_count * frame_count, width)
+    current = [
+        lax.dynamic_slice_in_dim(flat_frames, first_pair * frame_count + g * span, span, 0)
+        for g in range(group_count)
+    ]
     own_ids = routing.reshape(pair_count, frame_count)
     paired = sections == 2 and inner_size == 2
     if paired:
@@ -879,11 +890,14 @@
             chosen = (all_in[layer], all_out[layer])
             layers.append(((all_tables[layer],), chosen, [], jnp.ones((1,), jnp.int32)))
 
-    outgoing = dispatch(current, layer_ids[0], member_ref, experts, capacity, frame_count)
-    received = exchange(outgoing)
+    outgoing = [
+        dispatch(current[g], layer_ids[0][g], member_ref, experts, capacity, frame_count)
+        for g in range(group_count)
+    ]
+    received = [exchange(blocks) for blocks in outgoing]
     if paired:
         sent_in, sent_out = half_weights(
-            after(core.astype(jnp.int32).reshape(1), outgoing[0]), *own
+            after(core.astype(jnp.int32).reshape(1), outgoing[0][0]), *own
         )
         came_in = swap(sent_in, "section")
         came_out = swap(sent_out, "section")
@@ -894,7 +908,7 @@
             layers.append(((own_table, other_table), own, other, mine))
 
     labels, frame_lengths, label_lengths = lax.optimization_barrier(
-        (labels, frame_lengths, label_lengths, outgoing[0])
+        (labels, frame_lengths, label_lengths, outgoing[-1][0])
     )[:3]
     notes = jnp.concatenate(
         [
@@ -911,7 +925,7 @@
     shard = head_weight.shape[1]
     weight_rows = jnp.transpose(head_weight)
     line = group_size == 4
-    tables = jnp.asarray(slot_tables(group_size))
+    tables = jnp.asarray(slot_tables(group_size, group_count))
     slots = lax.dynamic_index_in_dim(tables, member, 0, keepdims=False)
     outer = lax.axis_index("dpo")
     blocks = -(-shard // BLOCK_ROWS)
@@ -958,51 +972,70 @@
     kept_order, chip_place, first_offsets, last_offsets = early[6:]
     layer_ids = [layer_ids[0]] + list(later_ids)
 
+    def tied(value, others, g):
+        marks = [other for i, other in enumerate(others) if i != g]
+        return after(value, *marks) if marks else value
+
+    normed, marks = [], []
     for layer in range(sections):
         choices, weights, others, pick_own = layers[layer]
-        note = notes if layer == 0 else None
-        done = run_expert(received, choices, weights, others, pick_own, filled, note)
-        returned = exchange(done)
+        done = [
+            run_expert(
+                received[g],
+                choices,
+                weights,
+                others,
+                tied(pick_own, marks, g),
+                filled,
+                notes if layer == 0 and g == 0 else None,
+            )
+            for g in range(group_count)
+        ]
+        returned = [exchange(parts) for parts in done]
+        marks = [parts[0] for parts in done]
+        tokens = [tied(member_ref, marks, g) for g in range(group_count)]
+        sizes = (experts, capacity, frame_count)
+        if layer < sections - 1:
+            made = [
+                combine_and_dispatch(
+                    current[g],
+                    returned[g],
+                    layer_ids[layer][g],
+                    choices,
+                    pick_own,
+                    layer_ids[layer + 1][g],
+                    tokens[g],
+                    *sizes,
+                )
+                for g in range(group_count)
+            ]
+            current = [pair[0] for pair in made]
+            received = [exchange(pair[1]) for pair in made]
+            marks = current
+        else:
+            normed = [
+                combine_and_norm(
+                    current[g],
+                    returned[g],
+                    layer_ids[layer][g],
+                    choices,
+                    pick_own,
+                    head_row,
+                    tokens[g],
+                    *sizes,
+                )
+                for g in range(group_count)
+            ]
         if layer == 0:
-            found = returned
+            found = list(returned[0])
             if not line:
-                stacked = jnp.stack(returned)
+                stacked = jnp.stack(found)
                 found = [
                     lax.dynamic_index_in_dim(stacked, member ^ k, 0, keepdims=False)
                     for k in range(group_size)
                 ]
-        if layer < sections - 1:
-            current, outgoing = combine_and_dispatch(
-                current,
-                returned,
-                layer_ids[layer],
-                choices,
-                pick_own,
-                layer_ids[layer + 1],
-                member_ref,
-                experts,
-                capacity,
-                frame_count,
-            )
-            received = exchange(outgoing)
-            if layer == 0:
-                found = [after(found[0], current)] + list(found[1:])
-                label_weight, places, names = label_rows(
-                    weight_rows, found, member_ref, per_section, filled, label_max, line
-                )
-                received, label_weight = lax.optimization_barrier((received, label_weight))
-        else:
-            normed = combine_and_norm(
-                current,
-                returned,
-                layer_ids[layer],
-                choices,
-                pick_own,
-                head_row,
-                member_ref,
-                experts,
-                capacity,
-                frame_count,
+            label_weight, places, names = label_rows(
+                weight_rows, found, member_ref, group_count, group_pairs, filled, label_max, line
             )
 
     def logits_of(fill, first, count, pieces, earlier=None):
@@ -1014,33 +1047,35 @@
         first = crossed(stats, "expert", 1)
         return [stats, first, crossed(stats, "expert", 2), crossed(first, "expert", 2)]
 
-    if line:
-        beside = crossed(normed, "expert", 1)
-        middle = lax.ppermute(normed, "expert", MIDDLE)
-        far = lax.ppermute(beside, "expert", MIDDLE)
-        outward = lax.ppermute(middle, "expert", OUTWARD)
-        heads = [logits_of(fill_all, 0, 2, [normed, beside])]
-        held, heads[0] = lax.optimization_barrier((far, heads[0]))
-        last = lax.ppermute(held, "expert", OUTWARD)
-        heads.append(logits_of(fill_far, 2, 2, [middle, outward, held, last], heads[0][2]))
-        found = [stats_of(heads[1][2])]
-    else:
-        gathered = lax.all_gather(normed, "expert")
-        pieces = [gathered[k] for k in range(group_size)]
-        heads = [logits_of(fill_all, 0, group_size, pieces)]
-        gathered = lax.all_gather(heads[0][2], "expert")
-        found = [
-            [
-                lax.dynamic_index_in_dim(gathered, member ^ k, 0, keepdims=False)
-                for k in range(group_size)
-            ]
-        ]
-    kept_losses = per_section if line else group_size * per_section
+    heads, found = [], []
+    for g in range(group_count):
+        if line:
+            beside = crossed(normed[g], "expert", 1)
+            middle = lax.ppermute(normed[g], "expert", MIDDLE)
+            far = lax.ppermute(beside, "expert", MIDDLE)
+            outward = lax.ppermute(middle, "expert", OUTWARD)
+            last = lax.ppermute(far, "expert", OUTWARD)
+            pieces = [normed[g], beside, middle, outward, far, last]
+            heads.append(logits_of(fill_line, g * group_size, group_size, pieces))
+            found.append(stats_of(heads[g][2]))
+        else:
+            gathered = lax.all_gather(normed[g], "expert")
+            pieces = [gathered[k] for k in range(group_size)]
+            heads.append(logits_of(fill_all, g * group_size, group_size, pieces))
+            gathered = lax.all_gather(heads[g][2], "expert")
+            found.append(
+                [
+                    lax.dynamic_index_in_dim(gathered, member ^ k, 0, keepdims=False)
+                    for k in range(group_size)
+                ]
+            )
+    kept_losses = group_pairs if line else group_size * group_pairs
     occupancy, high, low, losses = ctc_pass(
-        found, slots, names, frame_count, label_max, kept_losses
+        found, slots, names, frame_count, label_max, group_count, kept_losses
     )
     if not line:
-        losses = lax.dynamic_slice(losses, (0, member * per_section), (1, per_section))
+        pairs = losses.reshape(group_count, group_size, group_pairs)
+        losses = lax.dynamic_index_in_dim(pairs, member, 1).reshape(1, per_section)
     losses = jnp.transpose(losses)
 
     def gradient(order, outputs, each):

time: 212 us -> 223 us (1.052)
  waiting for transfers between devices: 102 us -> 67 us
  starting transfers between devices: 51 us -> 81.9 us
  local copies, waits for them, and re-layouts: 13.2 us -> 24.7 us
    ppermute x16 -> x32, starting transfers between devices: 25 us -> 52 us  [crossed(): return lax.ppermute(value, axis, [(i, i ^ by) for i in range(count)])]
    ppermute x16 -> x32, waiting for transfers between devices: 49 us -> 25.7 us  [crossed(): return lax.ppermute(value, axis, [(i, i ^ by) for i in range(count)])]
    ppermute x1 -> x2, waiting for transfers between devices: 8.74 us -> 3.46 us  [per_device(): outward = lax.ppermute(middle, 'expert', OUTWARD)]
    ppermute x2 -> x4, waiting for transfers between devices: 9.3 us -> 5.27 us  [the longest x2 5.27 us: per_device(): last = lax.ppermute(far, 'expert', OUTWARD)]
    dynamic_slice x4, local copies, waits for them, and re-layouts: 0.03 us -> 3.13 us  [mine_of(): return lax.dynamic_slice_in_dim(value, first_pair, per_section, 0)]
    optimization_barrier x2, local copies, waits for them, and re-layouts: 0.18 us -> 2.68 us  [per_device(): lax.optimization_barrier((labels, frame_lengths, label_lengths, outgoing[...]
    unnamed x56 -> x76, local copies, waits for them, and re-layouts: 11.7 us -> 11 us
  transfers between devices with their start and end apart: 48 -> 68, of which waited for: 30 -> 29; matrix products, arithmetic and copies ran while one was open for 2% -> 8% of each run, Pallas kernels for 7% -> 12%
where the time goes in v4:
time: 223 us; the launch traced here: 222 us
  starting transfers between devices  81.9 us (37%)
  waiting for transfers between devices  67 us (30%)
  Pallas kernels  43.6 us (20%)
  local copies, waits for them, and re-layouts  24.7 us (11%)
  other arithmetic  3.75 us (2%)
    ppermute x32, starting transfers between devices, crossed(): return lax.ppermute(value, axis, [(i, i ^ by) for i in range(count)])  52 us
    ppermute x28, waiting for transfers between devices, swap(): return lax.ppermute(value, axis, [(0, 1), (1, 0)])  32.6 us
    ppermute x32, waiting for transfers between devices, crossed(): return lax.ppermute(value, axis, [(i, i ^ by) for i in range(count)])  25.7 us
    ppermute x28, starting transfers between devices, swap(): return lax.ppermute(value, axis, [(0, 1), (1, 0)])  21.8 us
    unnamed x76, local copies, waits for them, and re-layouts  11 us
    pallas_call x3, Pallas kernels, head_gradient(): call(kernel, tuple((bf16_rows(each * BLOCK_ROWS, width) for _ in range(ou...  10.6 us
    pallas_call x1, Pallas kernels, ctc_pass(): call(kernel, (jax.ShapeDtypeStruct((COLS, row_count), jnp.float32), bf16_...  7.14 us
    pallas_call x2, Pallas kernels, head_logits(): call(kernel, (jax.ShapeDtypeStruct((height, row_count), jnp.float32), bf1...  6.48 us
  transfers between devices with their start and end apart: 68, of which 29 were waited for; matrix products, arithmetic and copies ran while one was open for 8% of the time, Pallas kernels for 12%

profile of v4, /device:TPU:0, one launch (start us, length us, event | category | flops | bytes accessed | tf_op | source)
XLA Modules:
  0.0 222.4 jit_solution(1218074863270931279)
XLA Ops:
  0.7 3.0 %collective-permute-start = (s32[8,48]{1,0:T(8,128)}, s32[8,48]{1,0:T(8,128)S(1)}, u32[]{:S(2)}, u32[]{:S(2)}) collective-permute-start(s32[8,48]{1,0:T(8,128)} %bitcast.61), channel_id=1, source_target_pairs={{0,16},{16,0},{1,17},{17,1},{2,18},{18,2},{3,19},{19,3},{4,20},{20... | collective-permute-start | bytes 4616 | tf_op jit(solution)/shard_map/ppermute | solution.py:724
  14.4 2.6 %collective-permute-start.2 = (bf16[32,1280]{1,0:T(8,128)(2,1)}, bf16[32,1280]{1,0:T(8,128)(2,1)S(1)}, u32[]{:S(2)}, u32[]{:S(2)}) collective-permute-start(bf16[32,1280]{1,0:T(8,128)(2,1)} %get-tuple-element.102), channel_id=1, source_target_pairs={{0,8},{4,12},{8,0},{12,4},{1,9},{5,13},{9,1},{13,5},{2,10},{6,14},... | collective-permute-start | bytes 245768 | tf_op jit(solution)/shard_map/ppermute | solution.py:729
  31.7 3.5 %collective-permute-start.5 = (bf16[32,1280]{1,0:T(8,128)(2,1)}, bf16[32,1280]{1,0:T(8,128)(2,1)S(1)}, u32[]{:S(2)}, u32[]{:S(2)}) collective-permute-start(bf16[32,1280]{1,0:T(8,128)(2,1)} %copy-done.29), channel_id=1, source_target_pairs={{0,8},{4,12},{8,0},{12,4},{1,9},{5,13},{9,1},{13,5},{2,10},{6,14},... | collective-permute-start | bytes 245768 | tf_op jit(solution)/shard_map/ppermute | solution.py:729
  37.1 2.5 %collective-permute-done.5.refs_8_ = bf16[32,1280]{1,0:T(8,128)(2,1)S(1)} collective-permute-done((bf16[32,1280]{1,0:T(8,128)(2,1)}, bf16[32,1280]{1,0:T(8,128)(2,1)S(1)}, u32[]{:S(2)}, u32[]{:S(2)}) %collective-permute-start.5) | collective-permute-done | bytes 81952 | tf_op jit(solution)/shard_map/ppermute | solution.py:729
  39.6 2.7 %collective-permute-done.6.refs_9_ = bf16[32,1280]{1,0:T(8,128)(2,1)S(1)} collective-permute-done((bf16[32,1280]{1,0:T(8,128)(2,1)}, bf16[32,1280]{1,0:T(8,128)(2,1)S(1)}, u32[]{:S(2)}, u32[]{:S(2)}) %collective-permute-start.6) | collective-permute-done | bytes 81952 | tf_op jit(solution)/shard_map/ppermute | solution.py:729
  47.6 2.8 %collective-permute-start.17 = (bf16[32,1280]{1,0:T(8,128)(2,1)S(1)}, bf16[32,1280]{1,0:T(8,128)(2,1)S(1)}, u32[]{:S(2)}, u32[]{:S(2)}) collective-permute-start(bf16[32,1280]{1,0:T(8,128)(2,1)S(1)} %get-tuple-element.137), channel_id=1, source_target_pairs={{0,12},{4,8},{8,4},{12,0},{1,13},{5,9},{9,5},{13,1},{2,14},{6,10},... | collective-permute-start | bytes 245768 | tf_op jit(solution)/shard_map/ppermute | solution.py:729
  52.8 2.8 %collective-permute-start.14 = (bf16[32,1280]{1,0:T(8,128)(2,1)S(1)}, bf16[32,1280]{1,0:T(8,128)(2,1)S(1)}, u32[]{:S(2)}, u32[]{:S(2)}) collective-permute-start(bf16[32,1280]{1,0:T(8,128)(2,1)S(1)} %get-tuple-element.121), channel_id=1, source_target_pairs={{0,12},{4,8},{8,4},{12,0},{1,13},{5,9},{9,5},{13,1},{2,14},{6,10},... | collective-permute-start | bytes 245768 | tf_op jit(solution)/shard_map/ppermute | solution.py:729
  58.1 5.2 %collective-permute-start.18 = (bf16[32,1280]{1,0:T(8,128)(2,1)}, bf16[32,1280]{1,0:T(8,128)(2,1)S(1)}, u32[]{:S(2)}, u32[]{:S(2)}) collective-permute-start(bf16[32,1280]{1,0:T(8,128)(2,1)} %get-tuple-element.139), channel_id=1, source_target_pairs={{0,4},{4,0},{8,12},{12,8},{1,5},{5,1},{9,13},{13,9},{2,6},{6,2},{1... | collective-permute-start | bytes 245768 | tf_op jit(solution)/shard_map/ppermute | solution.py:729
  81.8 3.6 %collective-permute-done.36.refs_4_ = bf16[32,1280]{1,0:T(8,128)(2,1)S(1)} collective-permute-done((bf16[32,1280]{1,0:T(8,128)(2,1)S(1)}, bf16[32,1280]{1,0:T(8,128)(2,1)S(1)}, u32[]{:S(2)}, u32[]{:S(2)}) %collective-permute-start.36) | collective-permute-done | bytes 81952 | tf_op jit(solution)/shard_map/ppermute | solution.py:729
  89.7 2.5 %collective-permute-start.26 = (bf16[32,1280]{1,0:T(8,128)(2,1)S(1)}, bf16[32,1280]{1,0:T(8,128)(2,1)S(1)}, u32[]{:S(2)}, u32[]{:S(2)}) collective-permute-start(bf16[32,1280]{1,0:T(8,128)(2,1)S(1)} %get-tuple-element.154), channel_id=1, source_target_pairs={{0,12},{4,8},{8,4},{12,0},{1,13},{5,9},{9,5},{13,1},{2,14},{6,10},... | collective-permute-start | bytes 245768 | tf_op jit(solution)/shard_map/ppermute | solution.py:729
  92.2 4.7 %collective-permute-done.24.refs_3_ = bf16[32,1280]{1,0:T(8,128)(2,1)S(1)} collective-permute-done((bf16[32,1280]{1,0:T(8,128)(2,1)S(1)}, bf16[32,1280]{1,0:T(8,128)(2,1)S(1)}, u32[]{:S(2)}, u32[]{:S(2)}) %collective-permute-start.24) | collective-permute-done | bytes 81952 | tf_op jit(solution)/shard_map/ppermute | solution.py:729
  101.6 4.1 %collective-permute-done.27.refs_1_ = bf16[96,1280]{1,0:T(8,128)(2,1)S(1)} collective-permute-done((bf16[96,1280]{1,0:T(8,128)(2,1)S(1)}, bf16[96,1280]{1,0:T(8,128)(2,1)S(1)}, u32[]{:S(2)}, u32[]{:S(2)}) %collective-permute-start.27) | collective-permute-done | bytes 245792 | tf_op jit(solution)/shard_map/ppermute | solution.py:729
  111.9 2.4 %copy-done.3 = bf16[1280,2000]{0,1:T(8,128)(2,1)S(1)} copy-done((bf16[1280,2000]{0,1:T(8,128)(2,1)S(1)}, bf16[1280,2000]{0,1:T(8,128)(2,1)}, u32[]{:S(2)}) %copy-start.3) | copy-done | bytes 5120024
  116.3 3.5 %collective-permute-done.40.refs_3_ = bf16[96,1280]{1,0:T(8,128)(2,1)S(1)} collective-permute-done((bf16[96,1280]{1,0:T(8,128)(2,1)S(1)}, bf16[96,1280]{1,0:T(8,128)(2,1)S(1)}, u32[]{:S(2)}, u32[]{:S(2)}) %collective-permute-start.40) | collective-permute-done | bytes 245792 | tf_op jit(solution)/shard_map/ppermute | solution.py:1056
  119.7 5.3 %collective-permute-done.42.refs_5_ = bf16[96,1280]{1,0:T(8,128)(2,1)S(1)} collective-permute-done((bf16[96,1280]{1,0:T(8,128)(2,1)S(1)}, bf16[96,1280]{1,0:T(8,128)(2,1)S(1)}, u32[]{:S(2)}, u32[]{:S(2)}) %collective-permute-start.42) | collective-permute-done | bytes 245792 | tf_op jit(solution)/shard_map/ppermute | solution.py:1057
  125.0 2.4 %copy-done.4 = bf16[1280,2000]{0,1:T(8,128)(2,1)S(1)} copy-done((bf16[1280,2000]{0,1:T(8,128)(2,1)S(1)}, bf16[1280,2000]{0,1:T(8,128)(2,1)}, u32[]{:S(2)}) %copy-start.4) | copy-done | bytes 5120024
  127.4 3.2 %shard_map.144 = (f32[2048,384]{1,0:T(8,128)S(1)}, bf16[384,1280]{1,0:T(8,128)(2,1)S(1)}, f32[4,16,96]{2,1,0:T(8,128)S(1)}) custom-call(s32[1]{0:T(128)} %bitcast.member_ref, bf16[2000,1280]{1,0:T(8,128)(2,1)S(1)} %bitcast.57, bf16[256,1280]{1,0:T(8,128)(2,1)S(1)} %get-tuple-element.123.label_ref, bf16[96,1280]{1,0:T(8,128)(2,1)S(1)} %shard_map.143.refs_0_, ...), custom_call_target="tpu_custom_call" | custom-call | flops 2013265920 | tf_op jit(solution)/shard_map/pallas_call | solution.py:424
  130.7 6.0 %collective-permute-start.43 = (f32[4,16,96]{2,1,0:T(8,128)S(1)}, f32[4,16,96]{2,1,0:T(8,128)S(1)}, u32[]{:S(2)}, u32[]{:S(2)}) collective-permute-start(f32[4,16,96]{2,1,0:T(8,128)S(1)} %get-tuple-element.160.refs_4_), channel_id=1, source_target_pairs={{0,4},{4,0},{8,12},{12,8},{1,5},{5,1},{9,13},{13,9},{2,6},{6,2},{1... | collective-permute-start | bytes 73736 | tf_op jit(solution)/shard_map/ppermute | solution.py:729
  136.7 3.3 %shard_map.142 = (f32[2048,384]{1,0:T(8,128)S(1)}, bf16[384,1280]{1,0:T(8,128)(2,1)S(1)}, f32[4,16,96]{2,1,0:T(8,128)S(1)}) custom-call(s32[1]{0:T(128)} %bitcast.member_ref, bf16[2000,1280]{1,0:T(8,128)(2,1)S(1)} %bitcast.58, bf16[256,1280]{1,0:T(8,128)(2,1)S(1)} %get-tuple-element.123.label_ref, bf16[96,1280]{1,0:T(8,128)(2,1)S(1)} %shard_map.141.refs_0_, ...), custom_call_target="tpu_custom_call" | custom-call | flops 2013265920 | tf_op jit(solution)/shard_map/pallas_call | solution.py:424
  140.0 2.4 %collective-permute-start.44 = (f32[4,16,96]{2,1,0:T(8,128)S(1)}, f32[4,16,96]{2,1,0:T(8,128)S(1)}, u32[]{:S(2)}, u32[]{:S(2)}) collective-permute-start(f32[4,16,96]{2,1,0:T(8,128)S(1)} %get-tuple-element.160.refs_4_), channel_id=1, source_target_pairs={{0,8},{4,12},{8,0},{12,4},{1,9},{5,13},{9,1},{13,5},{2,10},{6,14},... | collective-permute-start | bytes 73736 | tf_op jit(solution)/shard_map/ppermute | solution.py:729
  147.8 2.4 %collective-permute-done.34.refs_3_ = f32[4,16,96]{2,1,0:T(8,128)S(1)} collective-permute-done((f32[4,16,96]{2,1,0:T(8,128)S(1)}, f32[4,16,96]{2,1,0:T(8,128)S(1)}, u32[]{:S(2)}, u32[]{:S(2)}) %collective-permute-start.34) | collective-permute-done | bytes 24608 | tf_op jit(solution)/shard_map/ppermute | solution.py:729
  150.2 7.1 %shard_map.145 = (f32[16,768]{1,0:T(8,128)S(1)}, bf16[256,768]{1,0:T(8,128)(2,1)S(1)}, bf16[256,768]{1,0:T(8,128)(2,1)S(1)}, f32[1,4]{1,0:T(1,128)}) custom-call(s32[32]{0:T(128)S(1)} %copy-done.25, s32[16,128]{1,0:T(8,128)S(1)} %get-tuple-element.122.notes_ref, f32[4,16,96]{2,1,0:T(8,128)S(1)} %get-tuple-element.155.refs_0_, ...), custom_call_target="tpu_custom_call" | custom-call | flops 67108864 | tf_op jit(solution)/shard_map/pallas_call | solution.py:615
  157.3 4.9 %shard_map.146 = (bf16[512,1280]{1,0:T(8,128)(2,1)S(1)}, bf16[512,1280]{1,0:T(8,128)(2,1)S(1)}) custom-call(s32[4]{0:T(128)S(1)} %copy-done.26, f32[2048,384]{1,0:T(8,128)S(1)} %get-tuple-element.167.refs_0_, f32[2048,384]{1,0:T(8,128)S(1)} %get-tuple-element.168.refs_1_, bf16[384,1280]{1,0:T(8,128)(2,1)S(1)} %get-tuple-element.169.refs_2_, ...), custom_call_target="tpu_custom_call" | custom-call | flops 2818572288 | tf_op jit(solution)/shard_map/pallas_call | solution.py:666
  162.8 2.8 %shard_map.147.own_ref = bf16[512,1280]{1,0:T(8,128)(2,1)S(1)} custom-call(s32[2]{0:T(128)S(1)} %get-tuple-element.176.order_ref, f32[2048,384]{1,0:T(8,128)S(1)} %get-tuple-element.167.refs_0_, f32[2048,384]{1,0:T(8,128)S(1)} %get-tuple-element.168.refs_1_, bf16[384,1280]{1,0:T(8,128)(2,1)S(1)} %get-tuple-element.169.refs_2_, ...), custom_call_target="tpu_custom_call" | custom-call | flops 1409286144 | tf_op jit(solution)/shard_map/pallas_call | solution.py:666
  170.6 2.8 %shard_map.149.own_ref = bf16[512,1280]{1,0:T(8,128)(2,1)S(1)} custom-call(s32[2]{0:T(128)S(1)} %get-tuple-element.178.order_ref, f32[2048,384]{1,0:T(8,128)S(1)} %get-tuple-element.167.refs_0_, f32[2048,384]{1,0:T(8,128)S(1)} %get-tuple-element.168.refs_1_, bf16[384,1280]{1,0:T(8,128)(2,1)S(1)} %get-tuple-element.169.refs_2_, ...), custom_call_target="tpu_custom_call" | custom-call | flops 1409286144 | tf_op jit(solution)/shard_map/pallas_call | solution.py:666
  173.5 3.7 %collective-permute-done.49.refs_0_ = bf16[128,1280]{1,0:T(8,128)(2,1)S(1)} collective-permute-done((bf16[128,1280]{1,0:T(8,128)(2,1)S(1)}, bf16[128,1280]{1,0:T(8,128)(2,1)S(1)}, u32[]{:S(2)}, u32[]{:S(2)}) %collective-permute-start.49) | collective-permute-done | bytes 327712 | tf_op jit(solution)/shard_map/ppermute | solution.py:724
  181.6 2.6 %collective-permute-done.48.refs_0_ = bf16[128,1280]{1,0:T(8,128)(2,1)S(1)} collective-permute-done((bf16[128,1280]{1,0:T(8,128)(2,1)S(1)}, bf16[128,1280]{1,0:T(8,128)(2,1)S(1)}, u32[]{:S(2)}, u32[]{:S(2)}) %collective-permute-start.48) | collective-permute-done | bytes 327712 | tf_op jit(solution)/shard_map/ppermute | solution.py:724
  184.7 5.8 %collective-permute-done.51.refs_1_ = bf16[128,1280]{1,0:T(8,128)(2,1)S(1)} collective-permute-done((bf16[128,1280]{1,0:T(8,128)(2,1)S(1)}, bf16[128,1280]{1,0:T(8,128)(2,1)S(1)}, u32[]{:S(2)}, u32[]{:S(2)}) %collective-permute-start.51) | collective-permute-done | bytes 327712 | tf_op jit(solution)/shard_map/ppermute | solution.py:724
  195.6 6.6 %collective-permute-done.54.refs_2_ = bf16[128,1280]{1,0:T(8,128)(2,1)S(1)} collective-permute-done((bf16[128,1280]{1,0:T(8,128)(2,1)S(1)}, bf16[128,1280]{1,0:T(8,128)(2,1)S(1)}, u32[]{:S(2)}, u32[]{:S(2)}) %collective-permute-start.54) | collective-permute-done | bytes 327712 | tf_op jit(solution)/shard_map/ppermute | solution.py:724
  205.2 4.0 %collective-permute-done.60.refs_3_ = bf16[128,1280]{1,0:T(8,128)(2,1)S(1)} collective-permute-done((bf16[128,1280]{1,0:T(8,128)(2,1)S(1)}, bf16[128,1280]{1,0:T(8,128)(2,1)S(1)}, u32[]{:S(2)}, u32[]{:S(2)}) %collective-permute-start.60) | collective-permute-done | bytes 327712 | tf_op jit(solution)/shard_map/ppermute | solution.py:724
  210.8 4.6 %collective-permute-done.55.refs_0_ = bf16[128,1280]{1,0:T(8,128)(2,1)S(1)} collective-permute-done((bf16[128,1280]{1,0:T(8,128)(2,1)S(1)}, bf16[128,1280]{1,0:T(8,128)(2,1)S(1)}, u32[]{:S(2)}, u32[]{:S(2)}) %collective-permute-start.55) | collective-permute-done | bytes 327712 | tf_op jit(solution)/shard_map/ppermute | solution.py:724
  218.0 2.6 %shard_map.152.refs_4_ = bf16[2000,1280]{1,0:T(8,128)(2,1)} custom-call(s32[12]{0:T(128)S(1)} %stack.122.offsets_ref, bf16[128,1280]{1,0:T(8,128)(2,1)S(1)} %get-tuple-element.185.refs_0_, bf16[128,1280]{1,0:T(8,128)(2,1)S(1)} %get-tuple-element.186.refs_1_, bf16[128,1280]{1,0:T(8,128)(2,1)S(1)} %collective-permute-done.54.refs_2_, ...), custom_call_target="tpu_custom_call" | custom-call | tf_op jit(solution)/shard_map/pallas_call | solution.py:713
  (234 shorter events, 102.4 us)
Async XLA Ops:
  10.7 31.6 %collective-permute-start.8 = (bf16[1280,128]{1,0:T(8,128)(2,1)S(1)}, bf16[1280,128]{1,0:T(8,128)(2,1)S(1)}, u32[]{:S(2)}, u32[]{:S(2)}) collective-permute-start(bf16[1280,128]{1,0:T(8,128)(2,1)S(1)} %get-tuple-element.109), channel_id=1, source_target_pairs={{0,16},{16,0},{1,17},{17,1},{2,18},{18,2},{3,19},{19,3},{4,20},{20... | collective-permute-start | bytes 983048 | tf_op jit(solution)/shard_map/ppermute | solution.py:724
  11.0 31.3 %collective-permute-start.9 = (bf16[128,1280]{1,0:T(8,128)(2,1)S(1)}, bf16[128,1280]{1,0:T(8,128)(2,1)S(1)}, u32[]{:S(2)}, u32[]{:S(2)}) collective-permute-start(bf16[128,1280]{1,0:T(8,128)(2,1)S(1)} %get-tuple-element.110), channel_id=1, source_target_pairs={{0,16},{16,0},{1,17},{17,1},{2,18},{18,2},{3,19},{19,3},{4,20},{20... | collective-permute-start | bytes 983048 | tf_op jit(solution)/shard_map/ppermute | solution.py:724
  12.8 18.2 %collective-permute-start.1 = (bf16[32,1280]{1,0:T(8,128)(2,1)}, bf16[32,1280]{1,0:T(8,128)(2,1)S(1)}, u32[]{:S(2)}, u32[]{:S(2)}) collective-permute-start(bf16[32,1280]{1,0:T(8,128)(2,1)} %get-tuple-element.101), channel_id=1, source_target_pairs={{0,4},{4,0},{8,12},{12,8},{1,5},{5,1},{9,13},{13,9},{2,6},{6,2},{1... | collective-permute-start | bytes 245768 | tf_op jit(solution)/shard_map/ppermute | solution.py:729
  14.4 17.3 %collective-permute-start.2 = (bf16[32,1280]{1,0:T(8,128)(2,1)}, bf16[32,1280]{1,0:T(8,128)(2,1)S(1)}, u32[]{:S(2)}, u32[]{:S(2)}) collective-permute-start(bf16[32,1280]{1,0:T(8,128)(2,1)} %get-tuple-element.102), channel_id=1, source_target_pairs={{0,8},{4,12},{8,0},{12,4},{1,9},{5,13},{9,1},{13,5},{2,10},{6,14},... | collective-permute-start | bytes 245768 | tf_op jit(solution)/shard_map/ppermute | solution.py:729
  17.0 18.2 %collective-permute-start.3 = (bf16[32,1280]{1,0:T(8,128)(2,1)}, bf16[32,1280]{1,0:T(8,128)(2,1)S(1)}, u32[]{:S(2)}, u32[]{:S(2)}) collective-permute-start(bf16[32,1280]{1,0:T(8,128)(2,1)} %get-tuple-element.103), channel_id=1, source_target_pairs={{0,12},{4,8},{8,4},{12,0},{1,13},{5,9},{9,5},{13,1},{2,14},{6,10},... | collective-permute-start | bytes 245768 | tf_op jit(solution)/shard_map/ppermute | solution.py:729
  46.1 10.4 %collective-permute-start.16 = (bf16[32,1280]{1,0:T(8,128)(2,1)S(1)}, bf16[32,1280]{1,0:T(8,128)(2,1)S(1)}, u32[]{:S(2)}, u32[]{:S(2)}) collective-permute-start(bf16[32,1280]{1,0:T(8,128)(2,1)S(1)} %get-tuple-element.136), channel_id=1, source_target_pairs={{0,8},{4,12},{8,0},{12,4},{1,9},{5,13},{9,1},{13,5},{2,10},{6,14},... | collective-permute-start | bytes 245768 | tf_op jit(solution)/shard_map/ppermute | solution.py:729
  51.2 12.3 %collective-permute-start.12 = (bf16[32,1280]{1,0:T(8,128)(2,1)S(1)}, bf16[32,1280]{1,0:T(8,128)(2,1)S(1)}, u32[]{:S(2)}, u32[]{:S(2)}) collective-permute-start(bf16[32,1280]{1,0:T(8,128)(2,1)S(1)} %get-tuple-element.119), channel_id=1, source_target_pairs={{0,4},{4,0},{8,12},{12,8},{1,5},{5,1},{9,13},{13,9},{2,6},{6,2},{1... | collective-permute-start | bytes 245768 | tf_op jit(solution)/shard_map/ppermute | solution.py:729
  51.2 14.4 %collective-permute-start.13 = (bf16[32,1280]{1,0:T(8,128)(2,1)S(1)}, bf16[32,1280]{1,0:T(8,128)(2,1)S(1)}, u32[]{:S(2)}, u32[]{:S(2)}) collective-permute-start(bf16[32,1280]{1,0:T(8,128)(2,1)S(1)} %get-tuple-element.120), channel_id=1, source_target_pairs={{0,8},{4,12},{8,0},{12,4},{1,9},{5,13},{9,1},{13,5},{2,10},{6,14},... | collective-permute-start | bytes 245768 | tf_op jit(solution)/shard_map/ppermute | solution.py:729
  52.8 12.9 %collective-permute-start.14 = (bf16[32,1280]{1,0:T(8,128)(2,1)S(1)}, bf16[32,1280]{1,0:T(8,128)(2,1)S(1)}, u32[]{:S(2)}, u32[]{:S(2)}) collective-permute-start(bf16[32,1280]{1,0:T(8,128)(2,1)S(1)} %get-tuple-element.121), channel_id=1, source_target_pairs={{0,12},{4,8},{8,4},{12,0},{1,13},{5,9},{9,5},{13,1},{2,14},{6,10},... | collective-permute-start | bytes 245768 | tf_op jit(solution)/shard_map/ppermute | solution.py:729
  58.1 13.4 %collective-permute-start.18 = (bf16[32,1280]{1,0:T(8,128)(2,1)}, bf16[32,1280]{1,0:T(8,128)(2,1)S(1)}, u32[]{:S(2)}, u32[]{:S(2)}) collective-permute-start(bf16[32,1280]{1,0:T(8,128)(2,1)} %get-tuple-element.139), channel_id=1, source_target_pairs={{0,4},{4,0},{8,12},{12,8},{1,5},{5,1},{9,13},{13,9},{2,6},{6,2},{1... | collective-permute-start | bytes 245768 | tf_op jit(solution)/shard_map/ppermute | solution.py:729
  63.3 10.4 %collective-permute-start.19 = (bf16[32,1280]{1,0:T(8,128)(2,1)}, bf16[32,1280]{1,0:T(8,128)(2,1)S(1)}, u32[]{:S(2)}, u32[]{:S(2)}) collective-permute-start(bf16[32,1280]{1,0:T(8,128)(2,1)} %get-tuple-element.140), channel_id=1, source_target_pairs={{0,8},{4,12},{8,0},{12,4},{1,9},{5,13},{9,1},{13,5},{2,10},{6,14},... | collective-permute-start | bytes 245768 | tf_op jit(solution)/shard_map/ppermute | solution.py:729
  63.5 10.2 %collective-permute-start.20 = (bf16[32,1280]{1,0:T(8,128)(2,1)}, bf16[32,1280]{1,0:T(8,128)(2,1)}, u32[]{:S(2)}, u32[]{:S(2)}) collective-permute-start(bf16[32,1280]{1,0:T(8,128)(2,1)} %get-tuple-element.141), channel_id=1, source_target_pairs={{0,12},{4,8},{8,4},{12,0},{1,13},{5,9},{9,5},{13,1},{2,14},{6,10},... | collective-permute-start | bytes 245768 | tf_op jit(solution)/shard_map/ppermute | solution.py:729
  86.3 14.0 %collective-permute-start.38 = (bf16[96,1280]{1,0:T(8,128)(2,1)S(1)}, bf16[96,1280]{1,0:T(8,128)(2,1)S(1)}, u32[]{:S(2)}, u32[]{:S(2)}) collective-permute-start(bf16[96,1280]{1,0:T(8,128)(2,1)S(1)} %shard_map.143.refs_0_), channel_id=1, source_target_pairs={{0,4},{4,0},{8,12},{12,8},{1,5},{5,1},{9,13},{13,9},{2,6},{6,2},{1... | collective-permute-start | bytes 737288 | tf_op jit(solution)/shard_map/ppermute | solution.py:729
  106.5 13.3 %collective-permute-start.40 = (bf16[96,1280]{1,0:T(8,128)(2,1)S(1)}, bf16[96,1280]{1,0:T(8,128)(2,1)S(1)}, u32[]{:S(2)}, u32[]{:S(2)}) collective-permute-start(bf16[96,1280]{1,0:T(8,128)(2,1)S(1)} %collective-permute-done.39.refs_2_), channel_id=1, source_target_pairs={{4,0},{8,12},{5,1},{9,13},{6,2},{10,14},{7,3},{11,15},{20,16},{24,... | collective-permute-start | bytes 737288 | tf_op jit(solution)/shard_map/ppermute | solution.py:1056
  107.8 17.2 %collective-permute-start.42 = (bf16[96,1280]{1,0:T(8,128)(2,1)S(1)}, bf16[96,1280]{1,0:T(8,128)(2,1)S(1)}, u32[]{:S(2)}, u32[]{:S(2)}) collective-permute-start(bf16[96,1280]{1,0:T(8,128)(2,1)S(1)} %collective-permute-done.41.refs_4_), channel_id=1, source_target_pairs={{4,0},{8,12},{5,1},{9,13},{6,2},{10,14},{7,3},{11,15},{20,16},{24,... | collective-permute-start | bytes 737288 | tf_op jit(solution)/shard_map/ppermute | solution.py:1057
  109.1 27.6 %collective-permute-start.29 = (bf16[96,1280]{1,0:T(8,128)(2,1)S(1)}, bf16[96,1280]{1,0:T(8,128)(2,1)S(1)}, u32[]{:S(2)}, u32[]{:S(2)}) collective-permute-start(bf16[96,1280]{1,0:T(8,128)(2,1)S(1)} %collective-permute-done.28.refs_2_), channel_id=1, source_target_pairs={{4,0},{8,12},{5,1},{9,13},{6,2},{10,14},{7,3},{11,15},{20,16},{24,... | collective-permute-start | bytes 737288 | tf_op jit(solution)/shard_map/ppermute | solution.py:1056
  110.4 26.3 %collective-permute-start.31 = (bf16[96,1280]{1,0:T(8,128)(2,1)S(1)}, bf16[96,1280]{1,0:T(8,128)(2,1)S(1)}, u32[]{:S(2)}, u32[]{:S(2)}) collective-permute-start(bf16[96,1280]{1,0:T(8,128)(2,1)S(1)} %collective-permute-done.30.refs_4_), channel_id=1, source_target_pairs={{4,0},{8,12},{5,1},{9,13},{6,2},{10,14},{7,3},{11,15},{20,16},{24,... | collective-permute-start | bytes 737288 | tf_op jit(solution)/shard_map/ppermute | solution.py:1057
  130.7 12.3 %collective-permute-start.43 = (f32[4,16,96]{2,1,0:T(8,128)S(1)}, f32[4,16,96]{2,1,0:T(8,128)S(1)}, u32[]{:S(2)}, u32[]{:S(2)}) collective-permute-start(f32[4,16,96]{2,1,0:T(8,128)S(1)} %get-tuple-element.160.refs_4_), channel_id=1, source_target_pairs={{0,4},{4,0},{8,12},{12,8},{1,5},{5,1},{9,13},{13,9},{2,6},{6,2},{1... | collective-permute-start | bytes 73736 | tf_op jit(solution)/shard_map/ppermute | solution.py:729
  162.3 11.2 %collective-permute-start.47 = (bf16[512,1280]{1,0:T(8,128)(2,1)S(1)}, bf16[512,1280]{1,0:T(8,128)(2,1)S(1)}, u32[]{:S(2)}, u32[]{:S(2)}) collective-permute-start(bf16[512,1280]{1,0:T(8,128)(2,1)S(1)} %get-tuple-element.179), channel_id=1, source_target_pairs={{0,1},{1,0},{2,3},{3,2},{4,5},{5,4},{6,7},{7,6},{8,9},{9,8},{10,11... | collective-permute-start | bytes 3932168 | tf_op jit(solution)/shard_map/ppermute | solution.py:724
  166.5 10.6 %collective-permute-start.49 = (bf16[128,1280]{1,0:T(8,128)(2,1)S(1)}, bf16[128,1280]{1,0:T(8,128)(2,1)S(1)}, u32[]{:S(2)}, u32[]{:S(2)}) collective-permute-start(bf16[128,1280]{1,0:T(8,128)(2,1)S(1)} %get-tuple-element.177), channel_id=1, source_target_pairs={{0,16},{16,0},{1,17},{17,1},{2,18},{18,2},{3,19},{19,3},{4,20},{20... | collective-permute-start | bytes 983048 | tf_op jit(solution)/shard_map/ppermute | solution.py:724
  167.1 10.6 %collective-permute-start.50 = (bf16[128,1280]{1,0:T(8,128)(2,1)S(1)}, bf16[128,1280]{1,0:T(8,128)(2,1)S(1)}, u32[]{:S(2)}, u32[]{:S(2)}) collective-permute-start(bf16[128,1280]{1,0:T(8,128)(2,1)S(1)} %get-tuple-element.181), channel_id=1, source_target_pairs={{0,2},{2,0},{1,3},{3,1},{4,6},{6,4},{5,7},{7,5},{8,10},{10,8},{9,1... | collective-permute-start | bytes 983048 | tf_op jit(solution)/shard_map/ppermute | solution.py:724
  168.8 15.4 %collective-permute-start.48 = (bf16[128,1280]{1,0:T(8,128)(2,1)S(1)}, bf16[128,1280]{1,0:T(8,128)(2,1)S(1)}, u32[]{:S(2)}, u32[]{:S(2)}) collective-permute-start(bf16[128,1280]{1,0:T(8,128)(2,1)S(1)} %get-tuple-element.180), channel_id=1, source_target_pairs={{0,16},{16,0},{1,17},{17,1},{2,18},{18,2},{3,19},{19,3},{4,20},{20... | collective-permute-start | bytes 983048 | tf_op jit(solution)/shard_map/ppermute | solution.py:724
  170.1 14.6 %collective-permute-start.52 = (bf16[128,1280]{1,0:T(8,128)(2,1)S(1)}, bf16[128,1280]{1,0:T(8,128)(2,1)S(1)}, u32[]{:S(2)}, u32[]{:S(2)}) collective-permute-start(bf16[128,1280]{1,0:T(8,128)(2,1)S(1)} %get-tuple-element.183), channel_id=1, source_target_pairs={{0,2},{2,0},{1,3},{3,1},{4,6},{6,4},{5,7},{7,5},{8,10},{10,8},{9,1... | collective-permute-start | bytes 983048 | tf_op jit(solution)/shard_map/ppermute | solution.py:724
  178.5 12.1 %collective-permute-start.51 = (bf16[128,1280]{1,0:T(8,128)(2,1)S(1)}, bf16[128,1280]{1,0:T(8,128)(2,1)S(1)}, u32[]{:S(2)}, u32[]{:S(2)}) collective-permute-start(bf16[128,1280]{1,0:T(8,128)(2,1)S(1)} %get-tuple-element.182), channel_id=1, source_target_pairs={{0,2},{2,0},{1,3},{3,1},{4,6},{6,4},{5,7},{7,5},{8,10},{10,8},{9,1... | collective-permute-start | bytes 983048 | tf_op jit(solution)/shard_map/ppermute | solution.py:724
  180.2 10.4 %collective-permute-start.53 = (bf16[128,1280]{1,0:T(8,128)(2,1)S(1)}, bf16[128,1280]{1,0:T(8,128)(2,1)S(1)}, u32[]{:S(2)}, u32[]{:S(2)}) collective-permute-start(bf16[128,1280]{1,0:T(8,128)(2,1)S(1)} %get-tuple-element.184), channel_id=1, source_target_pairs={{0,16},{16,0},{1,17},{17,1},{2,18},{18,2},{3,19},{19,3},{4,20},{20... | collective-permute-start | bytes 983048 | tf_op jit(solution)/shard_map/ppermute | solution.py:724
  191.5 10.7 %collective-permute-start.54 = (bf16[128,1280]{1,0:T(8,128)(2,1)S(1)}, bf16[128,1280]{1,0:T(8,128)(2,1)S(1)}, u32[]{:S(2)}, u32[]{:S(2)}) collective-permute-start(bf16[128,1280]{1,0:T(8,128)(2,1)S(1)} %get-tuple-element.185.refs_0_), channel_id=1, source_target_pairs={{0,2},{2,0},{1,3},{3,1},{4,6},{6,4},{5,7},{7,5},{8,10},{10,8},{9,1... | collective-permute-start | bytes 983048 | tf_op jit(solution)/shard_map/ppermute | solution.py:724
  193.2 10.6 %collective-permute-start.56 = (bf16[128,1280]{1,0:T(8,128)(2,1)S(1)}, bf16[128,1280]{1,0:T(8,128)(2,1)S(1)}, u32[]{:S(2)}, u32[]{:S(2)}) collective-permute-start(bf16[128,1280]{1,0:T(8,128)(2,1)S(1)} %get-tuple-element.186.refs_1_), channel_id=1, source_target_pairs={{0,16},{16,0},{1,17},{17,1},{2,18},{18,2},{3,19},{19,3},{4,20},{20... | collective-permute-start | bytes 983048 | tf_op jit(solution)/shard_map/ppermute | solution.py:724
  194.5 14.7 %collective-permute-start.60 = (bf16[128,1280]{1,0:T(8,128)(2,1)S(1)}, bf16[128,1280]{1,0:T(8,128)(2,1)S(1)}, u32[]{:S(2)}, u32[]{:S(2)}) collective-permute-start(bf16[128,1280]{1,0:T(8,128)(2,1)S(1)} %get-tuple-element.186.refs_1_), channel_id=1, source_target_pairs={{0,2},{2,0},{1,3},{3,1},{4,6},{6,4},{5,7},{7,5},{8,10},{10,8},{9,1... | collective-permute-start | bytes 983048 | tf_op jit(solution)/shard_map/ppermute | solution.py:724
  195.0 15.8 %collective-permute-start.61 = (bf16[128,1280]{1,0:T(8,128)(2,1)S(1)}, bf16[128,1280]{1,0:T(8,128)(2,1)S(1)}, u32[]{:S(2)}, u32[]{:S(2)}) collective-permute-start(bf16[128,1280]{1,0:T(8,128)(2,1)S(1)} %get-tuple-element.185.refs_0_), channel_id=1, source_target_pairs={{0,16},{16,0},{1,17},{17,1},{2,18},{18,2},{3,19},{19,3},{4,20},{20... | collective-permute-start | bytes 983048 | tf_op jit(solution)/shard_map/ppermute | solution.py:724
  202.2 13.3 %collective-permute-start.55 = (bf16[128,1280]{1,0:T(8,128)(2,1)S(1)}, bf16[128,1280]{1,0:T(8,128)(2,1)S(1)}, u32[]{:S(2)}, u32[]{:S(2)}) collective-permute-start(bf16[128,1280]{1,0:T(8,128)(2,1)S(1)} %collective-permute-done.54.refs_2_), channel_id=1, source_target_pairs={{0,16},{16,0},{1,17},{17,1},{2,18},{18,2},{3,19},{19,3},{4,20},{20... | collective-permute-start | bytes 983048 | tf_op jit(solution)/shard_map/ppermute | solution.py:724
  203.8 11.7 %collective-permute-start.57 = (bf16[128,1280]{1,0:T(8,128)(2,1)S(1)}, bf16[128,1280]{1,0:T(8,128)(2,1)S(1)}, u32[]{:S(2)}, u32[]{:S(2)}) collective-permute-start(bf16[128,1280]{1,0:T(8,128)(2,1)S(1)} %collective-permute-done.56.refs_5_), channel_id=1, source_target_pairs={{0,2},{2,0},{1,3},{3,1},{4,6},{6,4},{5,7},{7,5},{8,10},{10,8},{9,1... | collective-permute-start | bytes 983048 | tf_op jit(solution)/shard_map/ppermute | solution.py:724
  205.2 10.8 %collective-permute-start.62 = (bf16[128,1280]{1,0:T(8,128)(2,1)S(1)}, bf16[128,1280]{1,0:T(8,128)(2,1)S(1)}, u32[]{:S(2)}, u32[]{:S(2)}) collective-permute-start(bf16[128,1280]{1,0:T(8,128)(2,1)S(1)} %get-tuple-element.185.refs_0_), channel_id=1, source_target_pairs={{0,1},{1,0},{2,3},{3,2},{4,5},{5,4},{6,7},{7,6},{8,9},{9,8},{10,11... | collective-permute-start | bytes 983048 | tf_op jit(solution)/shard_map/ppermute | solution.py:724
  (74 other events, 629.2 us)
